TPU v7x, 32 devices: a whole 2x2x4 slice. The times are simulated.
32 devices in a mesh: lon: 16 (over z, x, core), lat: 2 (over y).
Axes of the slice: x: 2, y: 2, z: 4, core: 2. Of those that a mesh axis runs over, the one named last changes fastest.
Arguments:
- thermal_anomaly: float32 [75, 32, 256], P(None, 'lon', 'lat'), may hold values from -6 to 6
- saltiness_anomaly: float32 [75, 32, 256], P(None, 'lon', 'lat'), may hold values from -6 to 6
- zonal_flow: float32 [75, 32, 256], P(None, 'lon', 'lat'), may hold values from -3 to 3
- meridional_flow: float32 [75, 32, 256], P(None, 'lon', 'lat'), may hold values from -3 to 3
- flooded_layer_number: int32 [32, 256], P('lon', 'lat'), may hold values from 0 to 75
- sideways_diffusion: float32 [32, 256], P('lon', 'lat'), may hold values from 0.2 to 4
- ambient_diffusion: float32 [32, 256], P('lon', 'lat'), may hold values from 0.1 to 10
Outputs:
- temp_next: float32 [75, 32, 256], P(None, 'lon', 'lat')
- salt_next: float32 [75, 32, 256], P(None, 'lon', 'lat')
- u_next: float32 [75, 32, 256], P(None, 'lon', 'lat')
- v_next: float32 [75, 32, 256], P(None, 'lon', 'lat')
Inputs may be any that keep to these rules, and one draw needn't show every extreme that they name: flooded_layer_number counts wet levels from the top; 0 marks land.
All inputs are finite; a program needn't handle non-finite values.
Results may differ from a plain program's by a relative error of at most 0.0003.
Values sent between devices are 32-bit elements; how exact they have to be, the bound alone decides.
No kernel may reach another device: no remote copies, remote signals or barrier semaphores. Data moves between devices by JAX's collectives and lax.ppermute only.
A program may use at most 64 MiB of HBM per device.

v0:
```python
import jax
import jax.numpy as jnp
from jax import lax
from jax.sharding import PartitionSpec as P

SUBSTEPS = 2


dt_step = 0.05


def extended(x, sides, width):
    for axis, dim in sides:
        devices, length = (lax.axis_size(axis), x.shape[dim])
        up = [(i, (i + 1) % devices) for i in range(devices)]
        down = [(j, i) for i, j in up]
        last = lax.slice_in_dim(x, length - width, length, axis=dim)
        first = lax.slice_in_dim(x, 0, width, axis=dim)
        before = lax.ppermute(last, axis, up)
        after = lax.ppermute(first, axis, down)
        x = jnp.concatenate([before, x, after], axis=dim)
    return x


def density(temp_field, salt_field):
    return (
        0.8 * salt_field
        - 0.2 * temp_field
        - 0.05 * temp_field * temp_field
        + 0.03 * temp_field * salt_field
    )


def coriolis_rows(first_row, row_total, total_rows):
    row_index = first_row + jnp.arange(row_total, dtype=jnp.int32)
    mirrored = jnp.where(row_index >= total_rows, 2 * total_rows - 1 - row_index, row_index)
    return 0.2 + mirrored.astype(jnp.float32) / total_rows


def centre(array):
    return array[..., 1:-1, 1:-1]


def to_east(array):
    return array[..., 2:, 1:-1]


def to_west(array):
    return array[..., :-2, 1:-1]


def to_north(array):
    return array[..., 1:-1, 2:]


def to_south(array):
    return array[..., 1:-1, :-2]


def advance(padded, planet):
    layer_total = (padded.shape[0] - 2) // 4
    marine_state = padded[: 4 * layer_total].reshape(
        4, layer_total, padded.shape[1], padded.shape[2]
    )
    bottom = padded[4 * layer_total]
    lateral = padded[4 * layer_total + 1]
    level_index = jnp.arange(layer_total, dtype=jnp.float32)[:, None, None]
    wet_mask = (level_index < bottom[None]).astype(jnp.float32)
    pressure = 0.5 * jnp.cumsum(density(marine_state[0], marine_state[1]), axis=0)
    wet_centre = centre(wet_mask)
    lateral_centre = centre(lateral)
    field_centre = centre(marine_state)
    lateral_mix = jnp.zeros_like(field_centre)
    for neighbour in (to_east, to_west, to_north, to_south):
        face_coef = 0.5 * (lateral_centre + neighbour(lateral)) * wet_centre * neighbour(wet_mask)
        lateral_mix = lateral_mix + face_coef * (neighbour(marine_state) - field_centre)
    u_centre = field_centre[2]
    v_centre = field_centre[3]
    advection = (
        u_centre * (to_east(marine_state) - to_west(marine_state)) * 0.5
        + v_centre * (to_north(marine_state) - to_south(marine_state)) * 0.5
    )
    tendency = lateral_mix - advection
    planet_rows = planet[1:-1]
    tend_u = tendency[2] + planet_rows * v_centre - (to_east(pressure) - to_west(pressure)) * 0.5
    tend_v = tendency[3] - planet_rows * u_centre - (to_north(pressure) - to_south(pressure)) * 0.5
    tendency = jnp.stack([tendency[0], tendency[1], tend_u, tend_v])
    updated = wet_centre * (field_centre + dt_step * tendency)
    return updated.reshape(4 * layer_total, updated.shape[2], updated.shape[3])


def vertical_mix(marine_state, wet_mask, ambient_diffusion):
    layer_total = marine_state.shape[1]
    density_now = density(marine_state[0], marine_state[1])
    stratification = density_now[1:] - density_now[:-1]
    coupling = (
        ambient_diffusion[None]
        * (0.2 + 1.0 / (1.0 + 10.0 * jnp.maximum(stratification, 0.0)))
        * wet_mask[1:]
    )
    zero_plane = jnp.zeros_like(ambient_diffusion)
    ratio_prev = zero_plane
    value_prev = jnp.zeros_like(marine_state[:, 0])
    ratio_list = []
    value_list = []
    for level in range(layer_total):
        lower_coef = coupling[level - 1] if level > 0 else zero_plane
        upper_coef = coupling[level] if level < layer_total - 1 else zero_plane
        pivot_value = 1.0 + lower_coef + upper_coef + lower_coef * ratio_prev
        ratio_prev = -upper_coef / pivot_value
        value_prev = (marine_state[:, level] + lower_coef * value_prev) / pivot_value
        ratio_list.append(ratio_prev)
        value_list.append(value_prev)
    current = value_list[layer_total - 1]
    solved = [current]
    for level in range(layer_total - 2, -1, -1):
        current = value_list[level] - ratio_list[level] * current
        solved.append(current)
    return jnp.stack(solved[::-1], axis=1)


def extend(state_stack, fold_signs, margin):
    lon_index = lax.axis_index("lon")
    lat_index = lax.axis_index("lat")
    lon_count = lax.axis_size("lon")
    lat_count = lax.axis_size("lat")
    column_count = state_stack.shape[1]
    meridian_total = state_stack.shape[2]
    pivot_offset = column_count // 2
    padded = extended(state_stack, (("lon", 1), ("lat", 2)), margin)
    top_rows = state_stack[:, :, meridian_total - margin :][:, :, ::-1]
    total_cols = column_count * lon_count
    positions = (
        lon_index * column_count - margin + jnp.arange(column_count + 2 * margin, dtype=jnp.int32)
    )
    source = jnp.mod(total_cols - 1 - pivot_offset - positions, total_cols)
    shard_rows = lax.all_gather(top_rows, "lon", axis=1, tiled=True)
    offsets = jnp.arange(shard_rows.shape[1], dtype=jnp.int32)
    select = (source[:, None] == offsets[None, :]).astype(jnp.float32)
    folded = jnp.einsum("pq,aqr->apr", select, shard_rows, precision=lax.Precision.HIGHEST)
    folded = folded * fold_signs[:, None, None]
    padded_rows = padded.shape[2]
    edge_low = jnp.where(lat_index > 0, padded[:, :, :margin], 0.0)
    edge_high = jnp.where(lat_index == lat_count - 1, folded, padded[:, :, padded_rows - margin :])
    return jnp.concatenate(
        [edge_low, padded[:, :, margin : padded_rows - margin], edge_high], axis=2
    )


def shards(
    thermal_anomaly,
    saltiness_anomaly,
    zonal_flow,
    meridional_flow,
    flooded_layer_number,
    sideways_diffusion,
    ambient_diffusion,
):
    layer_total = thermal_anomaly.shape[0]
    meridian_total = thermal_anomaly.shape[2]
    lat_index = lax.axis_index("lat")
    total_rows = meridian_total * lax.axis_size("lat")
    statics = jnp.stack([flooded_layer_number.astype(jnp.float32), sideways_diffusion])
    marine_state = jnp.concatenate(
        [thermal_anomaly, saltiness_anomaly, zonal_flow, meridional_flow], axis=0
    )
    fold_signs = jnp.concatenate(
        [
            jnp.ones((2 * layer_total,), jnp.float32),
            -jnp.ones((2 * layer_total,), jnp.float32),
            jnp.ones((2,), jnp.float32),
        ]
    )
    padded = extend(jnp.concatenate([marine_state, statics], axis=0), fold_signs, SUBSTEPS)
    for substep in range(SUBSTEPS):
        margin = SUBSTEPS - substep
        planet = coriolis_rows(
            lat_index * meridian_total - margin, meridian_total + 2 * margin, total_rows
        )
        marine_state = advance(padded, planet)
        padded = jnp.concatenate([marine_state, padded[4 * layer_total :, 1:-1, 1:-1]], axis=0)
    level_index = jnp.arange(layer_total, dtype=jnp.float32)[:, None, None]
    wet_mask = (level_index < flooded_layer_number.astype(jnp.float32)[None]).astype(jnp.float32)
    final = vertical_mix(
        marine_state.reshape(4, layer_total, marine_state.shape[1], marine_state.shape[2]),
        wet_mask,
        ambient_diffusion,
    )
    return (final[0], final[1], final[2], final[3])


def solution(mesh):
    in_specs = (
        P(None, "lon", "lat"),
        P(None, "lon", "lat"),
        P(None, "lon", "lat"),
        P(None, "lon", "lat"),
        P("lon", "lat"),
        P("lon", "lat"),
        P("lon", "lat"),
    )
    out_specs = (
        P(None, "lon", "lat"),
        P(None, "lon", "lat"),
        P(None, "lon", "lat"),
        P(None, "lon", "lat"),
    )
    return jax.shard_map(shards, mesh=mesh, in_specs=in_specs, out_specs=out_specs, check_vma=False)
```

profile of v0, /device:TPU:0, one launch (start us, length us, event | category | flops | bytes accessed | tf_op | source)
XLA Modules:
  0.0 60.7 jit_solution(4643633810955425876)
XLA Ops:
  0.6 0.7 %fusion.183 = (f32[2,128]{1,0:T(2,128)S(1)}, f32[1,2,128]{2,1,0:T(2,128)S(1)}) fusion(s32[2,128]{1,0:T(2,128)} %param.11), kind=kLoop, calls=%fused_computation.681 | loop fusion | flops 256 | bytes 3072 | tf_op jit(solution)/shard_map/convert_element_type | solution.py:163
  1.3 0.1 copy.623
  1.5 1.0 %copy.619 = f32[75,2,128]{0,2,1:T(8,128)S(1)} copy(f32[75,2,128]{2,1,0:T(2,128)} %param.7) | data formatting | bytes 153600 | tf_op args[0]
  2.4 1.0 %copy.620 = f32[75,2,128]{0,2,1:T(8,128)S(1)} copy(f32[75,2,128]{2,1,0:T(2,128)} %param.8) | data formatting | bytes 153600 | tf_op args[1]
  3.4 1.0 %copy.621 = f32[75,2,128]{0,2,1:T(8,128)S(1)} copy(f32[75,2,128]{2,1,0:T(2,128)} %param.9) | data formatting | bytes 153600 | tf_op args[2]
  4.4 1.0 %copy.622 = f32[75,2,128]{0,2,1:T(8,128)S(1)} copy(f32[75,2,128]{2,1,0:T(2,128)} %param.10) | data formatting | bytes 153600 | tf_op args[3]
  5.4 0.8 %copy.624 = f32[1,2,128]{0,2,1:T(8,128)S(1)} copy(f32[1,2,128]{2,1,0:T(2,128)} %bitcast.1578) | data formatting | bytes 2048 | tf_op jit(solution)/shard_map/stack | solution.py:163
  6.2 0.0 copy-start.2
  6.2 0.3 concatenate.9
  6.5 5.5 %collective-permute-start.1 = (f32[302,2,128]{0,2,1:T(8,128)S(1)}, f32[302,2,128]{0,2,1:T(8,128)S(1)}, u32[]{:S(2)}, u32[]{:S(2)}) collective-permute-start(f32[302,2,128]{0,2,1:T(8,128)S(1)} %concatenate.9), channel_id=1, source_target_pairs={{2,0},{4,2},{6,4},{8,6},{10,8},{12,10},{14,12},{16,14},{18,16},{20... | collective-permute-start | bytes 927752 | tf_op jit(solution)/shard_map/ppermute | solution.py:20
  12.0 0.0 collective-permute-start
  12.0 0.1 rev.3
  12.2 20.9 %all_gather.3 = f32[302,32,2]{0,2,1:T(2,128)S(1)} all-gather(f32[302,2,2]{0,2,1:T(2,128)S(1)} %rev.3), channel_id=1, replica_groups=mesh['lon'=16,'lat'=2] {'lon'}, dimensions={1}, use_global_device_ids=true | all-gather | bytes 82144 | tf_op jit(solution)/shard_map/all_gather | solution.py:137
  33.0 0.2 fusion.30
  33.2 0.0 collective-permute-done.1
  33.2 0.0 collective-permute-done
  33.3 1.6 %collective-permute-start.2 = (f32[302,6,2]{0,2,1:T(2,128)S(1)}, f32[302,6,2]{0,2,1:T(2,128)S(1)}, u32[]{:S(2)}, u32[]{:S(2)}) collective-permute-start(f32[302,6,2]{0,2,1:T(2,128)S(1)} %get-tuple-element.257), channel_id=1, source_target_pairs={{0,1},{1,0},{2,3},{3,2},{4,5},{5,4},{6,7},{7,6},{8,9},{9,8},{10,11... | collective-permute-start | bytes 43496 | tf_op jit(solution)/shard_map/ppermute | solution.py:19
  34.9 0.1 slice.785
  34.9 0.1 slice.812
  35.0 0.5 collective-permute-start.3
  35.5 1.6 %collective-permute-done.2 = f32[302,6,2]{0,2,1:T(2,128)S(1)} collective-permute-done((f32[302,6,2]{0,2,1:T(2,128)S(1)}, f32[302,6,2]{0,2,1:T(2,128)S(1)}, u32[]{:S(2)}, u32[]{:S(2)}) %collective-permute-start.2) | collective-permute-done | bytes 14528 | tf_op jit(solution)/shard_map/ppermute | solution.py:19
  37.1 1.7 %collective-permute-done.3 = f32[302,6,2]{0,2,1:T(2,128)S(1)} collective-permute-done((f32[302,6,2]{0,2,1:T(2,128)S(1)}, f32[302,6,2]{0,2,1:T(2,128)S(1)}, u32[]{:S(2)}, u32[]{:S(2)}) %collective-permute-start.3) | collective-permute-done | bytes 14528 | tf_op jit(solution)/shard_map/ppermute | solution.py:20
  38.8 0.0 copy-done.2
  38.8 0.1 pad_maximum_fusion
  38.9 0.0 copy-start
  38.9 0.6 slice_reduce_fusion.2
  39.5 0.8 %slice_reduce_fusion = (f32[6,132]{1,0:T(8,128)S(1)}, f32[6,132]{1,0:T(8,128)S(1)}) fusion(f32[302,6,132]{0,2,1:T(8,128)S(1)} %pad_maximum_fusion), kind=kLoop, calls=%fused_computation.11 | loop fusion | bytes 12672 | tf_op jit(solution)/shard_map/slice | solution.py:66
  40.2 0.2 fusion.4
  40.5 0.0 copy-done
  40.5 0.1 fusion.44
  40.5 0.4 copy.634
  41.0 0.9 %broadcast_multiply_fusion = f32[75,6,132]{2,1,0:T(8,128)} fusion(f32[75,6,132]{2,1,0:T(8,128)S(1)} %copy.634), kind=kOutput, calls=%fused_computation.50 | output fusion | flops 4455000 | bytes 475200 | tf_op jit(solution)/shard_map/jit(cumsum)/reduce_window_sum | solution.py:69
  41.9 3.1 %copy.646 = f32[300,6,132]{2,1,0:T(8,128)S(1)} copy(f32[300,6,132]{0,2,1:T(8,128)} %bitcast.1372) | data formatting | bytes 1900800 | tf_op jit(solution)/shard_map/reshape | solution.py:62
  45.0 0.4 slice_bitcast_fusion.5
  45.4 0.7 %fusion.178 = (f32[75,4,130]{2,1,0:T(4,128)S(1)}, f32[75,4,130]{2,1,0:T(4,128)S(1)}, f32[75,4,130]{2,1,0:T(4,128)S(1)}, f32[75,4,130]{2,1,0:T(4,128)S(1)}, f32[75,4,130]{2,1,0:T(4,128)S(1)}) fusion(f32[75,6,132]{2,1,0:T(8,128)S(1)} %fusion.2, f32[4,130]{1,0:T(4,128)S(1)} %get-tuple-element.356, f32[4,130]{1,0:T(4,128)S(1)} %get-tuple-element.354, ...), kind=kLoop, calls=%fused_computation.676 | loop fusion | flops 312000 | bytes 1568320 | tf_op jit(solution)/shard_map/slice | solution.py:41
  46.1 2.8 %multiply_subtract_fusion = f32[4,75,4,130]{3,2,1,0:T(4,128)S(1)} fusion(f32[4,75,6,132]{3,2,1,0:T(8,128)S(1)} %bitcast.1369, f32[75,4,130]{2,1,0:T(4,128)S(1)} %get-tuple-element.248, f32[75,4,130]{2,1,0:T(4,128)S(1)} %get-tuple-element.247, f32[75,4,130]{2,1,0:T(4,128)S(1)} %get-tuple-element.260, f32[75,4,130]{2,1,0:T(4,128)S(1)} %get-tuple-element.261, ...), kind=kLoop, calls=%fused_computation.4 | loop fusion | flops 2808000 | bytes 4680000 | tf_op jit(solution)/shard_map/sub | solution.py:83
  49.0 0.0 copy-start.1
  49.0 0.1 slice.1001
  49.1 0.9 %copy-done.1 = f32[75,6,132]{2,1,0:T(8,128)S(1)} copy-done((f32[75,6,132]{2,1,0:T(8,128)S(1)}, f32[75,6,132]{2,1,0:T(8,128)}, u32[]{:S(2)}) %copy-start.1) | copy-done | bytes 237624
  50.1 0.9 %fusion.15 = (f32[1,75,4,130]{3,2,1,0:T(4,128)S(1)}, f32[1,75,4,130]{3,2,1,0:T(4,128)S(1)}) fusion(f32[75,6,132]{2,1,0:T(8,128)S(1)} %copy-done.1, f32[4,75,4,130]{3,2,1,0:T(4,128)S(1)} %multiply_subtract_fusion, f32[130]{0:T(256)S(1)} %slice.785, f32[4,75,6,132]{3,2,1,0:T(8,128)S(1)} %bitcast.1370), kind=kLoop, calls=%fused_computation.27 | loop fusion | flops 390000 | bytes 1560520 | tf_op jit(solution)/shard_map/stack | solution.py:87
  50.9 0.8 %fusion.1 = f32[4,75,4,130]{3,2,1,0:T(4,128)S(1)} fusion(f32[1,75,4,130]{3,2,1,0:T(4,128)S(1)} %get-tuple-element.246, f32[1,75,4,130]{3,2,1,0:T(4,128)S(1)} %get-tuple-element.245, f32[2,75,4,130]{3,2,1,0:T(4,128)S(1)} %slice.1001, f32[4,75,6,132]{3,2,1,0:T(8,128)S(1)} %bitcast.1371, f32[75,4,130]{2,1,0:T(4,128)S(1)} %get-tuple-element.259), kind=kLoop, calls=%fused_computation.3 | loop fusion | flops 780000 | bytes 2028000 | tf_op jit(solution)/shard_map/mul | solution.py:88
  51.8 0.2 slice_bitcast_fusion.9
  52.0 0.2 broadcast_multiply_fusion.1
  52.3 0.1 fusion.128
  52.3 0.1 fusion.25
  52.4 0.4 fusion.181
  52.8 1.3 %fusion.177 = (f32[4,75,2,128]{3,2,1,0:T(2,128)S(1)}, f32[4,75,2,128]{3,2,1,0:T(2,128)S(1)}, f32[4,75,2,128]{3,2,1,0:T(2,128)S(1)}, f32[4,75,2,128]{3,2,1,0:T(2,128)S(1)}) fusion(f32[4,75,4,130]{3,2,1,0:T(4,128)S(1)} %fusion.1, f32[75,2,128]{2,1,0:T(2,128)S(1)} %get-tuple-element.272, f32[75,2,128]{2,1,0:T(2,128)S(1)} %get-tuple-element.273, ...), kind=kLoop, calls=%fused_computation.675 | loop fusion | flops 1075200 | bytes 3148800 | tf_op jit(solution)/shard_map/slice | solution.py:41
  54.2 0.3 copy_subtract_fusion
  54.5 0.1 slice.1027
  54.6 0.1 fusion.182
  54.7 0.0 copy-start.3
  54.7 0.5 fusion.37
  55.2 0.3 fusion.18
  55.5 0.1 fusion.180
  55.6 0.1 fusion.33
  55.7 0.0 copy-done.3
  55.8 0.1 compare_select_fusion
  55.9 0.7 %multiply_add_fusion.1 = (f32[2,128]{1,0:T(2,128)S(1)}, f32[2,128]{1,0:T(2,128)S(1)}, f32[2,128]{1,0:T(2,128)S(1)}, f32[2,128]{1,0:T(2,128)S(1)}, f32[2,128]{1,0...) fusion(f32[74,2,128]{2,1,0:T(2,128)S(1)} %compare_select_fusion), kind=kLoop, calls=%fused_computation.475 | loop fusion | flops 113408 | bytes 140288 | tf_op jit(solution)/shard_map/add | solution.py:109
  56.6 0.4 fusion.132
  57.0 0.2 fusion.78
  57.2 0.4 constant_dynamic-update-slice_fusion.74
  57.8 1.2 %constant_dynamic-update-slice_fusion.62 = (f32[4,75,2,128]{3,0,2,1:T(4,128)S(1)}, f32[4,1,2,128]{3,0,2,1:T(4,128)S(1)}, f32[4,1,2,128]{3,0,2,1:T(4,128)S(1)}, f...) fusion(f32[4,75,2,128]{3,0,2,1:T(4,128)S(1)} %constant_dynamic-, ...), kind=kLoop, calls=%fused_computation.117 | loop fusion | flops 355328 | bytes 650240
  59.8 0.9 %fusion.179 = (f32[1,75,2,128]{3,0,2,1:T(1,128)}, f32[1,75,2,128]{3,0,2,1:T(1,128)}, f32[1,75,2,128]{3,0,2,1:T(1,128)}, f32[1,75,2,128]{3,0,2,1:T(1,128)}) fusion(f32[4,75,2,128]{3,0,2,1:T(4,128)S(1)} %constant_dynamic-update-slice_fusion), kind=kLoop, calls=%fused_computation.677 | loop fusion | bytes 614400 | tf_op jit(solution)/shard_map/slice | solution.py:189
  (85 shorter events, 0.9 us)
Async XLA Ops:
  6.2 32.5 %copy-start.2 = (f32[302]{0:T(512)S(1)}, f32[302]{0:T(512)}, u32[]{:S(2)}) copy-start(f32[302]{0:T(512)} %constant.33.clone.1) | copy-start | bytes 3628
  6.5 26.7 %collective-permute-start.1 = (f32[302,2,128]{0,2,1:T(8,128)S(1)}, f32[302,2,128]{0,2,1:T(8,128)S(1)}, u32[]{:S(2)}, u32[]{:S(2)}) collective-permute-start(f32[302,2,128]{0,2,1:T(8,128)S(1)} %concatenate.9), channel_id=1, source_target_pairs={{2,0},{4,2},{6,4},{8,6},{10,8},{12,10},{14,12},{16,14},{18,16},{20... | collective-permute-start | bytes 927752 | tf_op jit(solution)/shard_map/ppermute | solution.py:20
  12.0 21.3 %collective-permute-start = (f32[302,2,128]{0,2,1:T(8,128)S(1)}, f32[302,2,128]{0,2,1:T(8,128)S(1)}, u32[]{:S(2)}, u32[]{:S(2)}) collective-permute-start(f32[302,2,128]{0,2,1:T(8,128)S(1)} %concatenate.9), channel_id=1, source_target_pairs={{0,2},{2,4},{4,6},{6,8},{8,10},{10,12},{12,14},{14,16},{16,18},{18... | collective-permute-start | bytes 927752 | tf_op jit(solution)/shard_map/ppermute | solution.py:19
  33.3 3.8 %collective-permute-start.2 = (f32[302,6,2]{0,2,1:T(2,128)S(1)}, f32[302,6,2]{0,2,1:T(2,128)S(1)}, u32[]{:S(2)}, u32[]{:S(2)}) collective-permute-start(f32[302,6,2]{0,2,1:T(2,128)S(1)} %get-tuple-element.257), channel_id=1, source_target_pairs={{0,1},{1,0},{2,3},{3,2},{4,5},{5,4},{6,7},{7,6},{8,9},{9,8},{10,11... | collective-permute-start | bytes 43496 | tf_op jit(solution)/shard_map/ppermute | solution.py:19
  35.0 3.8 %collective-permute-start.3 = (f32[302,6,2]{0,2,1:T(2,128)S(1)}, f32[302,6,2]{0,2,1:T(2,128)S(1)}, u32[]{:S(2)}, u32[]{:S(2)}) collective-permute-start(f32[302,6,2]{0,2,1:T(2,128)S(1)} %get-tuple-element.258), channel_id=1, source_target_pairs={{1,0},{0,1},{3,2},{2,3},{5,4},{4,5},{7,6},{6,7},{9,8},{8,9},{11,10... | collective-permute-start | bytes 43496 | tf_op jit(solution)/shard_map/ppermute | solution.py:20
  38.9 1.5 %copy-start = (f32[302,6,132]{0,2,1:T(8,128)}, f32[302,6,132]{0,2,1:T(8,128)S(1)}, u32[]{:S(2)}) copy-start(f32[302,6,132]{0,2,1:T(8,128)S(1)} %pad_maximum_fusion) | copy-start | bytes 2870212
  49.0 1.1 %copy-start.1 = (f32[75,6,132]{2,1,0:T(8,128)S(1)}, f32[75,6,132]{2,1,0:T(8,128)}, u32[]{:S(2)}) copy-start(f32[75,6,132]{2,1,0:T(8,128)} %broadcast_multiply_fusion) | copy-start | bytes 712804
  54.7 1.0 %copy-start.3 = (f32[2,128]{1,0:T(2,128)S(1)}, f32[2,128]{1,0:T(2,128)}, u32[]{:S(2)}) copy-start(f32[2,128]{1,0:T(2,128)} %param.13) | copy-start | bytes 3076
where the time goes:
time: 61.1 us; the launch traced here: 60.7 us
  blocking collectives  20.9 us (34%)
  other arithmetic  14.2 us (23%)
  local copies, waits for them, and re-layouts  13.5 us (22%)
  starting transfers between devices  7.56 us (12%)
  waiting for transfers between devices  3.25 us (5%)
  between operations  1.18 us (2%)
    all_gather x1, blocking collectives, extend(): shard_rows = lax.all_gather(top_rows, 'lon', axis=1, tiled=True)  20.9 us
    ppermute x2, starting transfers between devices, extended(): after = lax.ppermute(first, axis, down)  5.97 us
    unnamed x48, local copies, waits for them, and re-layouts  5.24 us
    sub x2, other arithmetic, advance(): tendency = lateral_mix - advection  3.19 us
    reshape x1, local copies, waits for them, and re-layouts, advance(): padded[:4 * layer_total]  3.09 us
    slice x3, other arithmetic, centre(): return array[..., 1:-1, 1:-1]  2.43 us
    unnamed x38, other arithmetic  2.01 us
    ppermute x2, waiting for transfers between devices, extended(): after = lax.ppermute(first, axis, down)  1.66 us
  transfers between devices with their start and end apart: 4, of which 2 were waited for; matrix products, arithmetic and copies ran while one was open for 1% of the time, Pallas kernels for 0%

commit v1 on v0

v1 whole, which is shorter than its diff:
```python
import functools

import jax
import jax.numpy as jnp
from jax import lax
from jax.experimental import pallas as pl
from jax.experimental.pallas import tpu as pltpu
from jax.sharding import PartitionSpec as P

SUBSTEPS = 2
DT = 0.05

LANES = 128
ROWS = 8
FLOOD_ROW = 0
MIX_ROW = 1


def density(temp, salt):
    return temp * (0.03 * salt - 0.05 * temp - 0.2) + 0.8 * salt


def parity():
    return lax.rem(lax.axis_index("lon"), 2)


def pack_kernel(levels, temp, salt, zonal, merid, flood, mix, tile, edge, sems):
    odd = parity()
    copies = []
    for f, field in enumerate((temp, salt, zonal, merid)):
        for c in range(2):
            slot = odd if c == 0 else 1 - odd
            copy = pltpu.make_async_copy(
                field.at[:, c, :], tile.at[slot, f, pl.ds(0, levels), :], sems.at[2 * f + c]
            )
            copy.start()
            copies.append(copy)
    padded = tile.shape[2]
    for copy in copies:
        copy.wait()
    zero = jnp.zeros((padded - levels, LANES), jnp.float32)
    for f in range(4):
        for s in range(2):
            tile[s, f, pl.ds(levels, padded - levels), :] = zero
    for c in range(2):
        slot = odd if c == 0 else 1 - odd
        tile[slot, 0, pl.ds(levels + FLOOD_ROW, 1), :] = flood[pl.ds(c, 1), :].astype(jnp.float32)
        tile[slot, 0, pl.ds(levels + MIX_ROW, 1), :] = mix[pl.ds(c, 1), :]
    lane = lax.broadcasted_iota(jnp.int32, (ROWS, LANES), 1)
    for b in range(padded // ROWS):
        rows = pl.ds(ROWS * b, ROWS)
        total = jnp.zeros((ROWS, LANES), jnp.float32)
        for f in range(4):
            for s in range(2):
                block = tile[s, f, rows, :]
                low = 8 * f + 2 * s
                total = jnp.where((lane >> 1) == low // 2, pltpu.roll(block, low, 1), total)
                high = low + 4
                total = jnp.where((lane >> 1) == high // 2, pltpu.roll(block, high + 2, 1), total)
        edge[rows, :] = total


def pack(fields, flood, mix):
    levels = fields[0].shape[0]
    padded = (levels + 2 + ROWS - 1) // ROWS * ROWS
    return pl.pallas_call(
        functools.partial(pack_kernel, levels),
        out_shape=(
            jax.ShapeDtypeStruct((2, 4, padded, LANES), jnp.float32),
            jax.ShapeDtypeStruct((padded, LANES), jnp.float32),
        ),
        in_specs=[pl.BlockSpec(memory_space=pltpu.HBM)] * 4 + [pl.BlockSpec(memory_space=pltpu.VMEM)] * 2,
        out_specs=(pl.BlockSpec(memory_space=pltpu.VMEM),) * 2,
        scratch_shapes=[pltpu.SemaphoreType.DMA((8,))],
    )(*fields, flood, mix)


def step_kernel(
    levels,
    lat_count,
    own,
    side_a,
    side_b,
    south,
    south_a,
    south_b,
    north,
    north_a,
    north_b,
    fold_1,
    fold_2,
    ambient,
    temp_out,
    salt_out,
    zonal_out,
    merid_out,
    edges,
    statics,
    columns,
    couple,
    state,
    ratio,
    sems,
):
    odd = parity()
    lat = lax.axis_index("lat")
    padded = own.shape[2]
    blocks = padded // ROWS
    lane = lax.broadcasted_iota(jnp.int32, (ROWS, LANES), 1)
    row = lax.broadcasted_iota(jnp.int32, (ROWS, LANES), 0)
    first_lane = lane == 0
    last_lane = lane == LANES - 1
    slot_1_lane = (lane == 1) | (lane == 2)
    south_lane = (lane == 0) | (lane == 2)

    def put_south(b, f, values):
        rows = pl.ds(pl.multiple_of(ROWS * b, ROWS), ROWS)
        for e in range(3):
            edges[e, f, rows, :] = values[e]

    def put_north(b, f, values):
        rows = pl.ds(pl.multiple_of(ROWS * b, ROWS), ROWS)
        for e in range(3):
            edges[e, f, rows, :] = jnp.where(south_lane, edges[e, f, rows, :], values[e])

    def each_block(body):
        @pl.loop(0, blocks)
        def _(b):
            body(b, pl.ds(pl.multiple_of(ROWS * b, ROWS), ROWS))

    def shift(x, source, target):
        return pltpu.roll(x, (target - source) % LANES, 1)

    @pl.when(lat == 0)
    def _():
        def body(b, rows):
            for f in range(4):
                put_south(b, f, [jnp.zeros((ROWS, LANES), jnp.float32)] * 3)

        each_block(body)

    @pl.when(lat > 0)
    def _():
        def body(b, rows):
            mid, at_a, at_b = south[rows, :], south_a[rows, :], south_b[rows, :]
            for f in range(4):
                far = shift(at_b, 8 * f + 5, 0)
                far = jnp.where(slot_1_lane, shift(at_a, 8 * f + 5, 0), far)
                put_south(b, f, [shift(mid, 8 * f + 5, 0), shift(mid, 8 * f + 4, 0), far])

        each_block(body)

    @pl.when(lat < lat_count - 1)
    def _():
        def body(b, rows):
            mid, at_a, at_b = north[rows, :], north_a[rows, :], north_b[rows, :]
            for f in range(4):
                far = shift(at_b, 8 * f, 127)
                far = jnp.where(slot_1_lane, shift(at_a, 8 * f, 127), far)
                put_north(b, f, [shift(mid, 8 * f, 127), shift(mid, 8 * f + 1, 127), far])

        each_block(body)

    for top_odd in range(2):

        @pl.when((lat == lat_count - 1) & (odd == top_odd))
        def _(top_odd=top_odd):
            def body(b, rows):
                near, other = fold_1[rows, :], fold_2[rows, :]
                if top_odd:
                    near, other = other, near
                for f in range(4):
                    mine = 8 * f + 4 + 2 * (1 - top_odd)
                    beside = 8 * f + 4 + 2 * top_odd
                    values = []
                    for source in (mine + 1, mine, beside + 1):
                        values.append(
                            jnp.where(slot_1_lane, shift(other, source, 1), shift(near, source, 127))
                        )
                    if f >= 2:
                        values = [-v for v in values]
                    put_north(b, f, values)

            each_block(body)

    def swap(x):
        return jnp.where(slot_1_lane, pltpu.roll(x, 2, 1), pltpu.roll(x, LANES - 2, 1))

    def to_slot(x, slot):
        return x if slot == 0 else pltpu.roll(x, LANES - 2, 1)

    def northern(x, edge):
        return jnp.where(last_lane, edge, pltpu.roll(x, LANES - 1, 1))

    def southern(x, edge):
        return jnp.where(first_lane, edge, pltpu.roll(x, 1, 1))

    def ring(own_0, own_1):
        return jnp.where(slot_1_lane, pltpu.roll(own_1, 2, 1), own_0)

    def static_row(ref, index, which):
        line = ref[index + (pl.ds(levels + which, 1), slice(None))]
        return jnp.broadcast_to(line, (ROWS, LANES))

    sigma = jnp.where(odd == 0, 1.0, -1.0).astype(jnp.float32)
    sources = {
        "own0": (own, (0, 0)),
        "own1": (own, (1, 0)),
        "near0": (side_b, (0, 0)),
        "near1": (side_a, (1, 0)),
        "far0": (side_b, (1, 0)),
        "far1": (side_a, (0, 0)),
        "rim": (edges, (0, 0)),
        "rim2": (edges, (1, 0)),
        "corner": (edges, (2, 0)),
    }
    held = {name: [static_row(r, i, w) for w in (FLOOD_ROW, MIX_ROW)] for name, (r, i) in sources.items()}

    def neighbours(get, name):
        if name == "rim":
            centre = get("rim")
            beside = ring(get("own0"), get("own1"))
            beyond = get("rim2")
            north_cell = jnp.where(south_lane, beside, beyond)
            south_cell = jnp.where(south_lane, beyond, beside)
            return swap(centre), get("corner"), north_cell, south_cell
        slot = int(name[-1])
        centre = get(name)
        if name.startswith("own"):
            inner, outer, edge = get("own%d" % (1 - slot)), get("near%d" % slot), get("rim")
        else:
            inner, outer, edge = get("own%d" % slot), get("far%d" % slot), get("corner")
        edge = to_slot(edge, slot)
        return inner, outer, northern(centre, edge), southern(centre, edge)

    cell_sets = ("own0", "own1", "near0", "near1", "rim")
    for n, name in enumerate(cell_sets):
        flood_at = neighbours(lambda k: held[k][0], name)
        mix_at = neighbours(lambda k: held[k][1], name)
        statics[n, 0] = held[name][0]
        for m in range(4):
            statics[n, 1 + m] = jnp.minimum(held[name][0], flood_at[m])
            statics[n, 5 + m] = (0.5 * DT) * (held[name][1] + mix_at[m])

    total_rows = LANES * lat_count
    place = lat * LANES + lane
    rim_place = lat * LANES + jnp.where(south_lane, -1, LANES)

    def turning(index):
        index = jnp.where(index >= total_rows, 2 * total_rows - 1 - index, index)
        return DT * (0.2 + index.astype(jnp.float32) / total_rows)

    planet = {True: turning(rim_place), False: turning(place)}
    sigma_of = {
        "own0": sigma,
        "near0": sigma,
        "own1": -sigma,
        "near1": -sigma,
        "rim": jnp.where(slot_1_lane, -sigma, sigma),
    }

    def running(x, carry):
        for step in (1, 2, 4):
            x = x + jnp.where(row >= step, pltpu.roll(x, step, 0), 0.0)
        x = x + carry
        return x, jnp.broadcast_to(x[ROWS - 1 :, :], (ROWS, LANES))

    def advance(name, level, fields, pressure):
        n = cell_sets.index(name)
        wet = level < statics[n, 0]
        weights = [jnp.where(level < statics[n, 1 + m], statics[n, 5 + m], 0.0) for m in range(4)]
        keep = jnp.where(wet, 1.0, 0.0)
        centre = keep - ((weights[0] + weights[1]) + (weights[2] + weights[3]))
        half = jnp.where(wet, 0.5 * DT, 0.0)
        along = half * sigma_of[name]
        flow_u, flow_v = fields[2][name], fields[3][name]
        drift_u = along * flow_u
        drift_v = half * flow_v
        inner, outer, north_w, south_w = (
            weights[0] - drift_u,
            weights[1] + drift_u,
            weights[2] - drift_v,
            weights[3] + drift_v,
        )
        out = []
        for f in range(4):
            cells = neighbours(lambda k, f=f: fields[f][k], name)
            value = centre * fields[f][name]
            value = value + ((inner * cells[0] + outer * cells[1]) + (north_w * cells[2] + south_w * cells[3]))
            out.append(value)
        cells = neighbours(lambda k: pressure[k], name)
        turn = keep * planet[name == "rim"]
        out[2] = out[2] + (turn * flow_v - (0.5 * along) * (cells[0] - cells[1]))
        out[3] = out[3] - (turn * flow_u + (0.5 * half) * (cells[2] - cells[3]))
        return out

    all_sets = ("own0", "own1", "near0", "near1", "far0", "far1", "rim", "rim2", "corner")
    zero = jnp.zeros((ROWS, LANES), jnp.float32)
    ambient_row = [
        jnp.broadcast_to(jnp.where(odd == s, ambient[0:1, :], ambient[1:2, :]), (ROWS, LANES)) for s in range(2)
    ]

    def block_body(b, carry):
        carry_1, carry_2, carry_3 = carry
        rows = pl.ds(pl.multiple_of(ROWS * b, ROWS), ROWS)
        level = (row + ROWS * b).astype(jnp.float32)
        fields = [{k: sources[k][0][sources[k][1][0], f, rows, :] for k in all_sets} for f in range(4)]
        pressure = {}
        next_1 = []
        for k, c in zip(all_sets, carry_1):
            pressure[k], c = running(density(fields[0][k], fields[1][k]), c)
            next_1.append(c)
        updated = {name: advance(name, level, fields, pressure) for name in cell_sets}
        fields = [{name: updated[name][f] for name in cell_sets} for f in range(4)]
        pressure = {}
        next_2 = []
        for k, c in zip(cell_sets, carry_2):
            pressure[k], c = running(density(fields[0][k], fields[1][k]), c)
            next_2.append(c)
        next_3 = []
        for s in range(2):
            final = advance("own%d" % s, level, fields, pressure)
            place_s = odd if s == 0 else 1 - odd
            dense = density(final[0], final[1])
            above = jnp.where(row == 0, carry_3[s], pltpu.roll(dense, 1, 0))
            next_3.append(jnp.broadcast_to(dense[ROWS - 1 :, :], (ROWS, LANES)))
            gate = (level < statics[s, 0]) & (level > 0.0)
            lower = ambient_row[s] * (0.2 + 1.0 / (1.0 + 10.0 * jnp.maximum(dense - above, 0.0)))
            lower = jnp.where(gate, lower, 0.0)
            for f in range(4):
                columns[2 * f + place_s, rows, :] = final[f]
                couple[2 * f + place_s, rows, :] = lower
        return tuple(next_1), tuple(next_2), tuple(next_3)

    lax.fori_loop(
        0, blocks, block_body, ((zero,) * len(all_sets), (zero,) * len(cell_sets), (zero,) * 2)
    )

    gain = jnp.ones((ROWS, LANES), jnp.float32)
    value = zero
    lower = zero
    for k in range(levels):
        upper = couple[:, k + 1, :]
        inverse = 1.0 / (gain + upper)
        value = (columns[:, k, :] + lower * value) * inverse
        share = upper * inverse
        state[k] = value
        ratio[k] = share
        gain = 1.0 + share * gain
        lower = upper
    current = value
    for k in range(levels - 2, -1, -1):
        current = state[k] + ratio[k] * current
        state[k] = current
    copies = []
    for f, out in enumerate((temp_out, salt_out, zonal_out, merid_out)):
        copy = pltpu.make_async_copy(state.at[:, pl.ds(2 * f, 2), :], out, sems.at[f])
        copy.start()
        copies.append(copy)
    for copy in copies:
        copy.wait()


def pairs_a(count):
    return [(i, i ^ 1) for i in range(count)]


def pairs_b(count, wrap):
    found = []
    for i in range(1, count - 1):
        found.append((i, i + 1 if i % 2 else i - 1))
    if wrap:
        found += [(0, count - 1), (count - 1, 0)]
    return found


def shards(temp, salt, zonal, merid, flood, mix, ambient):
    levels = temp.shape[0]
    lon_count = lax.axis_size("lon")
    lat_count = lax.axis_size("lat")
    axes = ("lon", "lat")
    tile, edge = pack((temp, salt, zonal, merid), flood, mix)
    lon_a, lon_b = pairs_a(lon_count), pairs_b(lon_count, True)

    def joint(lon_pairs, lat_pairs):
        return [
            (i * lat_count + m, j * lat_count + n) for i, j in lon_pairs for m, n in lat_pairs
        ]

    same = [(i, i) for i in range(lon_count)]
    side_b = lax.ppermute(tile, "lon", lon_b)
    side_a = lax.ppermute(tile, "lon", lon_a)
    rounds = [pairs_a(lat_count)] + ([pairs_b(lat_count, False)] if lat_count > 2 else [])
    got = [[lax.ppermute(edge, axes, joint(lon, lats)) for lon in (same, lon_a, lon_b)] for lats in rounds]
    if len(got) == 1:
        north = south = got[0]
    else:
        flip = lax.rem(lax.axis_index("lat"), 2) == 0
        north = [jnp.where(flip, x, y) for x, y in zip(*got)]
        south = [jnp.where(flip, y, x) for x, y in zip(*got)]
    top = [(lat_count - 1, lat_count - 1)]
    folds = [
        lax.ppermute(edge, axes, joint([(i, (lon_count - 1 - n - i) % lon_count) for i in range(lon_count)], top))
        for n in range(2)
    ]
    padded = tile.shape[2]
    vmem = pl.BlockSpec(memory_space=pltpu.VMEM)
    result = jax.ShapeDtypeStruct(temp.shape, jnp.float32)
    return pl.pallas_call(
        functools.partial(step_kernel, levels, lat_count),
        out_shape=(result,) * 4,
        in_specs=[vmem] * 12,
        out_specs=(pl.BlockSpec(memory_space=pltpu.HBM),) * 4,
        scratch_shapes=[
            pltpu.VMEM((3, 4, padded, LANES), jnp.float32),
            pltpu.VMEM((5, 9, ROWS, LANES), jnp.float32),
            pltpu.VMEM((ROWS, padded, LANES), jnp.float32),
            pltpu.VMEM((ROWS, padded, LANES), jnp.float32),
            pltpu.VMEM((levels, ROWS, LANES), jnp.float32),
            pltpu.VMEM((levels, ROWS, LANES), jnp.float32),
            pltpu.SemaphoreType.DMA((4,)),
        ],
    )(tile, side_a, side_b, *south, *north, *folds, ambient)


def solution(mesh):
    cube = P(None, "lon", "lat")
    plane = P("lon", "lat")
    return jax.shard_map(
        shards,
        mesh=mesh,
        in_specs=(cube,) * 4 + (plane,) * 3,
        out_specs=(cube,) * 4,
        check_vma=False,
    )
```

time: 61.1 us -> 31.9 us (0.52)
  the two profiles are of different devices: /device:TPU:0 before, /device:TPU:5 now
where the time goes in v1:
time: 31.9 us; the launch traced here: 31.3 us
  starting transfers between devices  15 us (47%)
  Pallas kernels  9.62 us (30%)
  waiting for transfers between devices  4.56 us (14%)
  local copies, waits for them, and re-layouts  1.42 us (4%)
  between operations  0.72 us (2%)
    ppermute x2, starting transfers between devices, shards(): lax.ppermute(edge, axes, joint([(i, (lon_count - 1 - n - i) % lon_count)...  8.13 us
    pallas_call x1, Pallas kernels, shards(): pl.pallas_call(functools.partial(step_kernel, levels, lat_count), out_sha...  7.1 us
    ppermute x3, waiting for transfers between devices, shards(): lax.ppermute(edge, axes, joint(lon, lats))  3.53 us
    ppermute x1, starting transfers between devices, shards(): side_a = lax.ppermute(tile, 'lon', lon_a)  2.87 us
    pallas_call x1, Pallas kernels, pack(): pl.pallas_call(functools.partial(pack_kernel, levels), out_shape=(jax.Sha...  2.53 us
    ppermute x3, starting transfers between devices, shards(): lax.ppermute(edge, axes, joint(lon, lats))  2.11 us
    ppermute x1, starting transfers between devices, shards(): side_b = lax.ppermute(tile, 'lon', lon_b)  1.84 us
    unnamed x14, local copies, waits for them, and re-layouts  1.42 us
  transfers between devices with their start and end apart: 7, of which 3 were waited for; matrix products, arithmetic and copies ran while one was open for 0% of the time, Pallas kernels for 0%

profile of v1, /device:TPU:5, one launch (start us, length us, event | category | flops | bytes accessed | tf_op | source)
XLA Modules:
  0.0 31.3 jit_solution(11387924465736304589)
XLA Ops:
  0.6 2.5 %shard_map.102 = (f32[2,4,80,128]{3,2,1,0:T(8,128)}, f32[80,128]{1,0:T(8,128)}) custom-call(f32[75,2,128]{2,1,0:T(2,128)} %temp.1, f32[75,2,128]{2,1,0:T(2,128)} %salt.1, f32[75,2,128]{2,1,0:T(2,128)} %zonal.1, f32[75,2,128]{2,1,0:T(2,128)} %merid.1, s32[2,128]{1,0:T(2,128)} %flood.1, f32[2,128]{1,0:T(2,128)} %mix.1), custom_call_target="tpu_custom_call" | custom-call | tf_op jit(solution)/shard_map/pallas_call | solution.py:66
  3.2 1.8 %collective-permute-start.1 = (f32[2,4,80,128]{3,2,1,0:T(8,128)}, f32[2,4,80,128]{3,2,1,0:T(8,128)S(1)}, u32[]{:S(2)}, u32[]{:S(2)}) collective-permute-start(f32[2,4,80,128]{3,2,1,0:T(8,128)} %get-tuple-element.6.own), channel_id=1, source_target_pairs={{2,4},{4,2},{6,8},{8,6},{10,12},{12,10},{14,16},{16,14},{18,20},{2... | collective-permute-start | bytes 983048 | tf_op jit(solution)/shard_map/ppermute | solution.py:391
  5.0 2.9 %collective-permute-start = (f32[2,4,80,128]{3,2,1,0:T(8,128)}, f32[2,4,80,128]{3,2,1,0:T(8,128)S(1)}, u32[]{:S(2)}, u32[]{:S(2)}) collective-permute-start(f32[2,4,80,128]{3,2,1,0:T(8,128)} %get-tuple-element.6.own), channel_id=1, source_target_pairs={{0,2},{2,0},{4,6},{6,4},{8,10},{10,8},{12,14},{14,12},{16,18},{18,... | collective-permute-start | bytes 983048 | tf_op jit(solution)/shard_map/ppermute | solution.py:392
  7.9 2.3 %collective-permute-start.6 = (f32[80,128]{1,0:T(8,128)}, f32[80,128]{1,0:T(8,128)S(1)}, u32[]{:S(2)}, u32[]{:S(2)}) collective-permute-start(f32[80,128]{1,0:T(8,128)} %get-tuple-element.7), channel_id=1, source_target_pairs={{1,29},{3,27},{5,25},{7,23},{9,21},{11,19},{13,17},{15,15},{17,13}... | collective-permute-start | bytes 122888 | tf_op jit(solution)/shard_map/ppermute | solution.py:403
  10.2 5.8 %collective-permute-start.5 = (f32[80,128]{1,0:T(8,128)}, f32[80,128]{1,0:T(8,128)S(1)}, u32[]{:S(2)}, u32[]{:S(2)}) collective-permute-start(f32[80,128]{1,0:T(8,128)} %get-tuple-element.7), channel_id=1, source_target_pairs={{1,31},{3,29},{5,27},{7,25},{9,23},{11,21},{13,19},{15,17},{17,15}... | collective-permute-start | bytes 122888 | tf_op jit(solution)/shard_map/ppermute | solution.py:403
  16.0 0.1 collective-permute-start.4
  16.1 0.0 collective-permute-done.6.fold_2
  16.1 0.0 copy-start.5
  16.1 2.0 %collective-permute-start.3 = (f32[80,128]{1,0:T(8,128)}, f32[80,128]{1,0:T(8,128)S(1)}, u32[]{:S(2)}, u32[]{:S(2)}) collective-permute-start(f32[80,128]{1,0:T(8,128)} %get-tuple-element.7), channel_id=1, source_target_pairs={{0,3},{1,2},{2,1},{3,0},{4,7},{5,6},{6,5},{7,4},{8,11},{9,10},{10,... | collective-permute-start | bytes 122888 | tf_op jit(solution)/shard_map/ppermute | solution.py:394
  18.2 1.0 %collective-permute-done.5.fold_1 = f32[80,128]{1,0:T(8,128)S(1)} collective-permute-done((f32[80,128]{1,0:T(8,128)}, f32[80,128]{1,0:T(8,128)S(1)}, u32[]{:S(2)}, u32[]{:S(2)}) %collective-permute-start.5) | collective-permute-done | bytes 40992 | tf_op jit(solution)/shard_map/ppermute | solution.py:403
  19.2 0.0 copy-start.6
  19.2 0.0 collective-permute-start.2
  19.2 1.4 %collective-permute-done.4.south_b.north_b = f32[80,128]{1,0:T(8,128)S(1)} collective-permute-done((f32[80,128]{1,0:T(8,128)}, f32[80,128]{1,0:T(8,128)S(1)}, u32[]{:S(2)}, u32[]{:S(2)}) %collective-permute-start.4) | collective-permute-done | bytes 40992 | tf_op jit(solution)/shard_map/ppermute | solution.py:394
  20.6 0.0 copy-start.2
  20.6 0.0 collective-permute-done.3.south_a.north_a
  20.6 0.0 copy-start.3
  20.6 2.1 %collective-permute-done.2.south.north = f32[80,128]{1,0:T(8,128)S(1)} collective-permute-done((f32[80,128]{1,0:T(8,128)}, f32[80,128]{1,0:T(8,128)S(1)}, u32[]{:S(2)}, u32[]{:S(2)}) %collective-permute-start.2) | collective-permute-done | bytes 40992 | tf_op jit(solution)/shard_map/ppermute | solution.py:394
  22.7 0.0 copy-start.4
  22.7 0.0 collective-permute-done.1.side_b
  22.7 0.0 copy-start
  22.7 0.0 collective-permute-done.side_a
  22.7 0.0 copy-done.5
  22.8 0.0 copy-done.6
  22.8 0.0 copy-done.2
  22.8 0.0 copy-done.3
  22.8 0.6 %copy-done.4 = f32[80,128]{1,0:T(8,128)} copy-done((f32[80,128]{1,0:T(8,128)}, f32[80,128]{1,0:T(8,128)S(1)}, u32[]{:S(2)}) %copy-start.4) | copy-done | bytes 40984
  23.3 0.1 copy-done
  23.5 0.0 copy-start.1
  23.5 0.7 %copy-done.1 = f32[2,4,80,128]{3,2,1,0:T(8,128)} copy-done((f32[2,4,80,128]{3,2,1,0:T(8,128)}, f32[2,4,80,128]{3,2,1,0:T(8,128)S(1)}, u32[]{:S(2)}) %copy-start.1) | copy-done | bytes 327704
  24.2 7.1 %shard_map.103 = (f32[75,2,128]{2,1,0:T(2,128)}, f32[75,2,128]{2,1,0:T(2,128)}, f32[75,2,128]{2,1,0:T(2,128)}, f32[75,2,128]{2,1,0:T(2,128)}) custom-call(f32[2,4,80,128]{3,2,1,0:T(8,128)} %get-tuple-element.6.own, f32[2,4,80,128]{3,2,1,0:T(8,128)} %copy-done.1, f32[2,4,80,128]{3,2,1,0:T(8,128)} %copy-done, f32[80,128]{1,0:T(8,128)} %copy-done.4, ...), custom_call_target="tpu_custom_call" | custom-call | tf_op jit(solution)/shard_map/pallas_call | solution.py:409
Async XLA Ops:
  3.2 19.6 %collective-permute-start.1 = (f32[2,4,80,128]{3,2,1,0:T(8,128)}, f32[2,4,80,128]{3,2,1,0:T(8,128)S(1)}, u32[]{:S(2)}, u32[]{:S(2)}) collective-permute-start(f32[2,4,80,128]{3,2,1,0:T(8,128)} %get-tuple-element.6.own), channel_id=1, source_target_pairs={{2,4},{4,2},{6,8},{8,6},{10,12},{12,10},{14,16},{16,14},{18,20},{2... | collective-permute-start | bytes 983048 | tf_op jit(solution)/shard_map/ppermute | solution.py:391
  5.0 17.7 %collective-permute-start = (f32[2,4,80,128]{3,2,1,0:T(8,128)}, f32[2,4,80,128]{3,2,1,0:T(8,128)S(1)}, u32[]{:S(2)}, u32[]{:S(2)}) collective-permute-start(f32[2,4,80,128]{3,2,1,0:T(8,128)} %get-tuple-element.6.own), channel_id=1, source_target_pairs={{0,2},{2,0},{4,6},{6,4},{8,10},{10,8},{12,14},{14,12},{16,18},{18,... | collective-permute-start | bytes 983048 | tf_op jit(solution)/shard_map/ppermute | solution.py:392
  7.9 8.2 %collective-permute-start.6 = (f32[80,128]{1,0:T(8,128)}, f32[80,128]{1,0:T(8,128)S(1)}, u32[]{:S(2)}, u32[]{:S(2)}) collective-permute-start(f32[80,128]{1,0:T(8,128)} %get-tuple-element.7), channel_id=1, source_target_pairs={{1,29},{3,27},{5,25},{7,23},{9,21},{11,19},{13,17},{15,15},{17,13}... | collective-permute-start | bytes 122888 | tf_op jit(solution)/shard_map/ppermute | solution.py:403
  10.2 9.0 %collective-permute-start.5 = (f32[80,128]{1,0:T(8,128)}, f32[80,128]{1,0:T(8,128)S(1)}, u32[]{:S(2)}, u32[]{:S(2)}) collective-permute-start(f32[80,128]{1,0:T(8,128)} %get-tuple-element.7), channel_id=1, source_target_pairs={{1,31},{3,29},{5,27},{7,25},{9,23},{11,21},{13,19},{15,17},{17,15}... | collective-permute-start | bytes 122888 | tf_op jit(solution)/shard_map/ppermute | solution.py:403
  16.0 4.6 %collective-permute-start.4 = (f32[80,128]{1,0:T(8,128)}, f32[80,128]{1,0:T(8,128)S(1)}, u32[]{:S(2)}, u32[]{:S(2)}) collective-permute-start(f32[80,128]{1,0:T(8,128)} %get-tuple-element.7), channel_id=1, source_target_pairs={{2,5},{3,4},{4,3},{5,2},{6,9},{7,8},{8,7},{9,6},{10,13},{11,12},{1... | collective-permute-start | bytes 122888 | tf_op jit(solution)/shard_map/ppermute | solution.py:394
  16.1 6.6 %copy-start.5 = (f32[80,128]{1,0:T(8,128)}, f32[80,128]{1,0:T(8,128)S(1)}, u32[]{:S(2)}) copy-start(f32[80,128]{1,0:T(8,128)S(1)} %collective-permute-done.6.fold_2) | copy-start | bytes 122884
  16.1 4.5 %collective-permute-start.3 = (f32[80,128]{1,0:T(8,128)}, f32[80,128]{1,0:T(8,128)S(1)}, u32[]{:S(2)}, u32[]{:S(2)}) collective-permute-start(f32[80,128]{1,0:T(8,128)} %get-tuple-element.7), channel_id=1, source_target_pairs={{0,3},{1,2},{2,1},{3,0},{4,7},{5,6},{6,5},{7,4},{8,11},{9,10},{10,... | collective-permute-start | bytes 122888 | tf_op jit(solution)/shard_map/ppermute | solution.py:394
  19.2 3.6 %copy-start.6 = (f32[80,128]{1,0:T(8,128)}, f32[80,128]{1,0:T(8,128)S(1)}, u32[]{:S(2)}) copy-start(f32[80,128]{1,0:T(8,128)S(1)} %collective-permute-done.5.fold_1) | copy-start | bytes 122884
  19.2 3.5 %collective-permute-start.2 = (f32[80,128]{1,0:T(8,128)}, f32[80,128]{1,0:T(8,128)S(1)}, u32[]{:S(2)}, u32[]{:S(2)}) collective-permute-start(f32[80,128]{1,0:T(8,128)} %get-tuple-element.7), channel_id=1, source_target_pairs={{0,1},{1,0},{2,3},{3,2},{4,5},{5,4},{6,7},{7,6},{8,9},{9,8},{10,11... | collective-permute-start | bytes 122888 | tf_op jit(solution)/shard_map/ppermute | solution.py:394
  20.6 2.1 %copy-start.2 = (f32[80,128]{1,0:T(8,128)}, f32[80,128]{1,0:T(8,128)S(1)}, u32[]{:S(2)}) copy-start(f32[80,128]{1,0:T(8,128)S(1)} %collective-permute-done.4.south_b.north_b) | copy-start | bytes 122884
  20.6 2.1 %copy-start.3 = (f32[80,128]{1,0:T(8,128)}, f32[80,128]{1,0:T(8,128)S(1)}, u32[]{:S(2)}) copy-start(f32[80,128]{1,0:T(8,128)S(1)} %collective-permute-done.3.south_a.north_a) | copy-start | bytes 122884
  22.7 0.6 %copy-start.4 = (f32[80,128]{1,0:T(8,128)}, f32[80,128]{1,0:T(8,128)S(1)}, u32[]{:S(2)}) copy-start(f32[80,128]{1,0:T(8,128)S(1)} %collective-permute-done.2.south.north) | copy-start | bytes 122884
  22.7 0.7 %copy-start = (f32[2,4,80,128]{3,2,1,0:T(8,128)}, f32[2,4,80,128]{3,2,1,0:T(8,128)S(1)}, u32[]{:S(2)}) copy-start(f32[2,4,80,128]{3,2,1,0:T(8,128)S(1)} %collective-permute-done.1.side_b) | copy-start | bytes 983044
  23.5 0.7 %copy-start.1 = (f32[2,4,80,128]{3,2,1,0:T(8,128)}, f32[2,4,80,128]{3,2,1,0:T(8,128)S(1)}, u32[]{:S(2)}) copy-start(f32[2,4,80,128]{3,2,1,0:T(8,128)S(1)} %collective-permute-done.side_a) | copy-start | bytes 983044

commit v2 on v1

--- a/solution.py
+++ b/solution.py
@@ -11,6 +11,7 @@
 DT = 0.05
 
 LANES = 128
+VMEM_LIMIT = 16 << 20
 ROWS = 8
 FLOOD_ROW = 0
 MIX_ROW = 1
@@ -24,9 +25,14 @@
     return lax.rem(lax.axis_index("lon"), 2)
 
 
-def pack_kernel(levels, temp, salt, zonal, merid, flood, mix, tile, edge, sems):
+def pack_kernel(levels, temp, salt, zonal, merid, flood, mix, tile, edge, flood_here, mix_here, sems):
     odd = parity()
-    copies = []
+    copies = [
+        pltpu.make_async_copy(flood, flood_here, sems.at[8]),
+        pltpu.make_async_copy(mix, mix_here, sems.at[9]),
+    ]
+    for copy in copies:
+        copy.start()
     for f, field in enumerate((temp, salt, zonal, merid)):
         for c in range(2):
             slot = odd if c == 0 else 1 - odd
@@ -44,8 +50,8 @@
             tile[s, f, pl.ds(levels, padded - levels), :] = zero
     for c in range(2):
         slot = odd if c == 0 else 1 - odd
-        tile[slot, 0, pl.ds(levels + FLOOD_ROW, 1), :] = flood[pl.ds(c, 1), :].astype(jnp.float32)
-        tile[slot, 0, pl.ds(levels + MIX_ROW, 1), :] = mix[pl.ds(c, 1), :]
+        tile[slot, 0, pl.ds(levels + FLOOD_ROW, 1), :] = flood_here[pl.ds(c, 1), :].astype(jnp.float32)
+        tile[slot, 0, pl.ds(levels + MIX_ROW, 1), :] = mix_here[pl.ds(c, 1), :]
     lane = lax.broadcasted_iota(jnp.int32, (ROWS, LANES), 1)
     for b in range(padded // ROWS):
         rows = pl.ds(ROWS * b, ROWS)
@@ -69,10 +75,15 @@
             jax.ShapeDtypeStruct((2, 4, padded, LANES), jnp.float32),
             jax.ShapeDtypeStruct((padded, LANES), jnp.float32),
         ),
-        in_specs=[pl.BlockSpec(memory_space=pltpu.HBM)] * 4 + [pl.BlockSpec(memory_space=pltpu.VMEM)] * 2,
+        in_specs=[pl.BlockSpec(memory_space=pltpu.HBM)] * 6,
         out_specs=(pl.BlockSpec(memory_space=pltpu.VMEM),) * 2,
-        scratch_shapes=[pltpu.SemaphoreType.DMA((8,))],
-    )(*fields, flood, mix)
+        scratch_shapes=[
+            pltpu.VMEM(flood.shape, flood.dtype),
+            pltpu.VMEM(mix.shape, mix.dtype),
+            pltpu.SemaphoreType.DMA((10,)),
+        ],
+        compiler_params=pltpu.CompilerParams(vmem_limit_bytes=VMEM_LIMIT),
+    )(*[pltpu.with_memory_space_constraint(x, pltpu.HBM) for x in (*fields, flood, mix)])
 
 
 def step_kernel(
@@ -88,7 +99,8 @@
     north_a,
     north_b,
     fold_1,
-    fold_2,
+    fold_even,
+    fold_odd,
     ambient,
     temp_out,
     salt_out,
@@ -166,9 +178,9 @@
         @pl.when((lat == lat_count - 1) & (odd == top_odd))
         def _(top_odd=top_odd):
             def body(b, rows):
-                near, other = fold_1[rows, :], fold_2[rows, :]
+                near, other = fold_1[rows, :], fold_even[rows, :]
                 if top_odd:
-                    near, other = other, near
+                    near, other = fold_odd[rows, :], near
                 for f in range(4):
                     mine = 8 * f + 4 + 2 * (1 - top_odd)
                     beside = 8 * f + 4 + 2 * top_odd
@@ -390,26 +402,30 @@
     same = [(i, i) for i in range(lon_count)]
     side_b = lax.ppermute(tile, "lon", lon_b)
     side_a = lax.ppermute(tile, "lon", lon_a)
+    top = [(lat_count - 1, lat_count - 1)]
+    mirror = [(i, lon_count - 1 - i) for i in range(lon_count)]
+    mirror_odd = [(i, (lon_count - 2 - i) % lon_count) for i in range(1, lon_count, 2)]
+    fold_1 = lax.ppermute(edge, axes, joint(mirror, top))
+    fold_2 = lax.ppermute(edge, axes, joint(mirror_odd, top))
     rounds = [pairs_a(lat_count)] + ([pairs_b(lat_count, False)] if lat_count > 2 else [])
-    got = [[lax.ppermute(edge, axes, joint(lon, lats)) for lon in (same, lon_a, lon_b)] for lats in rounds]
+    got = []
+    for lats in rounds:
+        at_b, mid = [lax.ppermute(edge, axes, joint(lon, lats)) for lon in (lon_b, same)]
+        got.append([mid, lax.ppermute(mid, "lon", lon_a), at_b])
     if len(got) == 1:
         north = south = got[0]
     else:
         flip = lax.rem(lax.axis_index("lat"), 2) == 0
         north = [jnp.where(flip, x, y) for x, y in zip(*got)]
         south = [jnp.where(flip, y, x) for x, y in zip(*got)]
-    top = [(lat_count - 1, lat_count - 1)]
-    folds = [
-        lax.ppermute(edge, axes, joint([(i, (lon_count - 1 - n - i) % lon_count) for i in range(lon_count)], top))
-        for n in range(2)
-    ]
+    folds = [fold_1, lax.ppermute(fold_1, "lon", lon_a), fold_2]
     padded = tile.shape[2]
     vmem = pl.BlockSpec(memory_space=pltpu.VMEM)
     result = jax.ShapeDtypeStruct(temp.shape, jnp.float32)
     return pl.pallas_call(
         functools.partial(step_kernel, levels, lat_count),
         out_shape=(result,) * 4,
-        in_specs=[vmem] * 12,
+        in_specs=[vmem] * 13,
         out_specs=(pl.BlockSpec(memory_space=pltpu.HBM),) * 4,
         scratch_shapes=[
             pltpu.VMEM((3, 4, padded, LANES), jnp.float32),
@@ -420,6 +436,7 @@
             pltpu.VMEM((levels, ROWS, LANES), jnp.float32),
             pltpu.SemaphoreType.DMA((4,)),
         ],
+        compiler_params=pltpu.CompilerParams(vmem_limit_bytes=VMEM_LIMIT),
     )(tile, side_a, side_b, *south, *north, *folds, ambient)
 
 

time: 31.9 us -> 25.1 us (0.79)
  Pallas kernels: 9.62 us -> 7.12 us
  starting transfers between devices: 15 us -> 13.1 us
  local copies, waits for them, and re-layouts: 1.42 us -> 0.01 us
  waiting for transfers between devices: 4.56 us -> 3.78 us
    ppermute x2 -> x4, starting transfers between devices: 8.13 us -> 4.78 us  [the longest x1 2.35 us: shards(): fold_2 = lax.ppermute(edge, axes, joint(mirror_odd, top))]
    ppermute x3 -> x2, waiting for transfers between devices: 3.53 us -> 0.43 us  [shards(): lax.ppermute(edge, axes, joint(lon, lats))]
    ppermute x2 -> x4, waiting for transfers between devices: 1.03 us -> 3.35 us  [the longest x1 2.17 us: shards(): fold_2 = lax.ppermute(edge, axes, joint(mirror_odd, top))]
    ppermute x3 -> x2, starting transfers between devices: 2.11 us -> 3.62 us  [shards(): lax.ppermute(edge, axes, joint(lon, lats))]
    unnamed x14 -> x2, local copies, waits for them, and re-layouts: 1.42 us -> 0.01 us
    pallas_call x1, Pallas kernels: 2.53 us -> 1.24 us  [pack(): pl.pallas_call(functools.partial(pack_kernel, levels), out_shape=(jax.Sha...]
    pallas_call x1, Pallas kernels: 7.1 us -> 5.88 us  [shards(): pl.pallas_call(functools.partial(step_kernel, levels, lat_count), out_sha...]
  transfers between devices with their start and end apart: 7 -> 8, of which waited for: 3 -> 5; matrix products, arithmetic and copies ran while one was open for 0% -> 0% of each run, Pallas kernels for 0% -> 0%
where the time goes in v2:
time: 25.1 us; the launch traced here: 24.7 us
  starting transfers between devices  13.1 us (52%)
  Pallas kernels  7.12 us (28%)
  waiting for transfers between devices  3.78 us (15%)
  between operations  0.68 us (3%)
    pallas_call x1, Pallas kernels, shards(): pl.pallas_call(functools.partial(step_kernel, levels, lat_count), out_sha...  5.88 us
    ppermute x2, starting transfers between devices, shards(): lax.ppermute(edge, axes, joint(lon, lats))  3.62 us
    ppermute x1, starting transfers between devices, shards(): side_a = lax.ppermute(tile, 'lon', lon_a)  2.87 us
    ppermute x1, starting transfers between devices, shards(): fold_2 = lax.ppermute(edge, axes, joint(mirror_odd, top))  2.35 us
    ppermute x1, waiting for transfers between devices, shards(): fold_2 = lax.ppermute(edge, axes, joint(mirror_odd, top))  2.17 us
    ppermute x1, starting transfers between devices, shards(): fold_1 = lax.ppermute(edge, axes, joint(mirror, top))  1.92 us
    ppermute x1, starting transfers between devices, shards(): side_b = lax.ppermute(tile, 'lon', lon_b)  1.84 us
    pallas_call x1, Pallas kernels, pack(): pl.pallas_call(functools.partial(pack_kernel, levels), out_shape=(jax.Sha...  1.24 us
  transfers between devices with their start and end apart: 8, of which 5 were waited for; matrix products, arithmetic and copies ran while one was open for 0% of the time, Pallas kernels for 0%

profile of v2, /device:TPU:5, one launch (start us, length us, event | category | flops | bytes accessed | tf_op | source)
XLA Modules:
  0.0 24.7 jit_solution(15294326345548062411)
XLA Ops:
  0.6 1.2 %shard_map.102 = (f32[2,4,80,128]{3,2,1,0:T(8,128)S(1)}, f32[80,128]{1,0:T(8,128)S(1)}) custom-call(f32[75,2,128]{2,1,0:T(2,128)} %temp.1, f32[75,2,128]{2,1,0:T(2,128)} %salt.1, f32[75,2,128]{2,1,0:T(2,128)} %zonal.1, f32[75,2,128]{2,1,0:T(2,128)} %merid.1, s32[2,128]{1,0:T(2,128)} %flood.1, f32[2,128]{1,0:T(2,128)} %mix.1), custom_call_target="tpu_custom_call" | custom-call | tf_op jit(solution)/shard_map/pallas_call | solution.py:72
  1.9 0.0 copy-start
  1.9 1.8 %collective-permute-start.1 = (f32[2,4,80,128]{3,2,1,0:T(8,128)S(1)}, f32[2,4,80,128]{3,2,1,0:T(8,128)S(1)}, u32[]{:S(2)}, u32[]{:S(2)}) collective-permute-start(f32[2,4,80,128]{3,2,1,0:T(8,128)S(1)} %get-tuple-element.6.own), channel_id=1, source_target_pairs={{2,4},{4,2},{6,8},{8,6},{10,12},{12,10},{14,16},{16,14},{18,20},{2... | collective-permute-start | bytes 983048 | tf_op jit(solution)/shard_map/ppermute | solution.py:403
  3.7 2.9 %collective-permute-start = (f32[2,4,80,128]{3,2,1,0:T(8,128)S(1)}, f32[2,4,80,128]{3,2,1,0:T(8,128)S(1)}, u32[]{:S(2)}, u32[]{:S(2)}) collective-permute-start(f32[2,4,80,128]{3,2,1,0:T(8,128)S(1)} %get-tuple-element.6.own), channel_id=1, source_target_pairs={{0,2},{2,0},{4,6},{6,4},{8,10},{10,8},{12,14},{14,12},{16,18},{18,... | collective-permute-start | bytes 983048 | tf_op jit(solution)/shard_map/ppermute | solution.py:404
  6.6 2.3 %collective-permute-start.7 = (f32[80,128]{1,0:T(8,128)S(1)}, f32[80,128]{1,0:T(8,128)S(1)}, u32[]{:S(2)}, u32[]{:S(2)}) collective-permute-start(f32[80,128]{1,0:T(8,128)S(1)} %get-tuple-element.7), channel_id=1, source_target_pairs={{3,27},{7,23},{11,19},{15,15},{19,11},{23,7},{27,3},{31,31}} | collective-permute-start | bytes 122888 | tf_op jit(solution)/shard_map/ppermute | solution.py:409
  9.0 1.9 %collective-permute-start.5 = (f32[80,128]{1,0:T(8,128)S(1)}, f32[80,128]{1,0:T(8,128)S(1)}, u32[]{:S(2)}, u32[]{:S(2)}) collective-permute-start(f32[80,128]{1,0:T(8,128)S(1)} %get-tuple-element.7), channel_id=1, source_target_pairs={{1,31},{3,29},{5,27},{7,25},{9,23},{11,21},{13,19},{15,17},{17,15}... | collective-permute-start | bytes 122888 | tf_op jit(solution)/shard_map/ppermute | solution.py:408
  10.9 0.1 collective-permute-start.2
  11.0 2.2 %collective-permute-done.7.fold_odd = f32[80,128]{1,0:T(8,128)S(1)} collective-permute-done((f32[80,128]{1,0:T(8,128)S(1)}, f32[80,128]{1,0:T(8,128)S(1)}, u32[]{:S(2)}, u32[]{:S(2)}) %collective-permute-start.7) | collective-permute-done | bytes 40992 | tf_op jit(solution)/shard_map/ppermute | solution.py:409
  13.1 3.5 %collective-permute-start.4 = (f32[80,128]{1,0:T(8,128)S(1)}, f32[80,128]{1,0:T(8,128)S(1)}, u32[]{:S(2)}, u32[]{:S(2)}) collective-permute-start(f32[80,128]{1,0:T(8,128)S(1)} %get-tuple-element.7), channel_id=1, source_target_pairs={{2,5},{3,4},{4,3},{5,2},{6,9},{7,8},{8,7},{9,6},{10,13},{11,12},{1... | collective-permute-start | bytes 122888 | tf_op jit(solution)/shard_map/ppermute | solution.py:413
  16.7 0.7 %collective-permute-done.5.fold_1 = f32[80,128]{1,0:T(8,128)S(1)} collective-permute-done((f32[80,128]{1,0:T(8,128)S(1)}, f32[80,128]{1,0:T(8,128)S(1)}, u32[]{:S(2)}, u32[]{:S(2)}) %collective-permute-start.5) | collective-permute-done | bytes 40992 | tf_op jit(solution)/shard_map/ppermute | solution.py:408
  17.4 0.0 collective-permute-start.6
  17.4 0.0 collective-permute-done.2.south.north
  17.4 0.5 %collective-permute-start.3 = (f32[80,128]{1,0:T(8,128)S(1)}, f32[80,128]{1,0:T(8,128)S(1)}, u32[]{:S(2)}, u32[]{:S(2)}) collective-permute-start(f32[80,128]{1,0:T(8,128)S(1)} %collective-permute-done.2.south.north), channel_id=1, source_target_pairs={{0,2},{2,0},{4,6},{6,4},{8,10},{10,8},{12,14},{14,12},{16,18},{18,... | collective-permute-start | bytes 122888 | tf_op jit(solution)/shard_map/ppermute | solution.py:414
  17.9 0.4 %collective-permute-done.4.south_b.north_b = f32[80,128]{1,0:T(8,128)S(1)} collective-permute-done((f32[80,128]{1,0:T(8,128)S(1)}, f32[80,128]{1,0:T(8,128)S(1)}, u32[]{:S(2)}, u32[]{:S(2)}) %collective-permute-start.4) | collective-permute-done | bytes 40992 | tf_op jit(solution)/shard_map/ppermute | solution.py:413
  18.4 0.3 %collective-permute-done.6.fold_even = f32[80,128]{1,0:T(8,128)S(1)} collective-permute-done((f32[80,128]{1,0:T(8,128)S(1)}, f32[80,128]{1,0:T(8,128)S(1)}, u32[]{:S(2)}, u32[]{:S(2)}) %collective-permute-start.6) | collective-permute-done | bytes 40992 | tf_op jit(solution)/shard_map/ppermute | solution.py:421
  18.6 0.2 collective-permute-done.3.south_a.north_a
  18.8 0.0 collective-permute-done.1.side_b
  18.8 0.0 collective-permute-done.side_a
  18.8 0.0 copy-done
  18.8 5.9 %shard_map.103 = (f32[75,2,128]{2,1,0:T(2,128)}, f32[75,2,128]{2,1,0:T(2,128)}, f32[75,2,128]{2,1,0:T(2,128)}, f32[75,2,128]{2,1,0:T(2,128)}) custom-call(f32[2,4,80,128]{3,2,1,0:T(8,128)S(1)} %get-tuple-element.6.own, f32[2,4,80,128]{3,2,1,0:T(8,128)S(1)} %collective-permute-done.side_a, f32[2,4,80,128]{3,2,1,0:T(8,128)S(1)} %collective-permute-done.1.side_b, ...), custom_call_target="tpu_custom_call" | custom-call | tf_op jit(solution)/shard_map/pallas_call | solution.py:425
Async XLA Ops:
  1.9 16.9 %copy-start = (f32[2,128]{1,0:T(2,128)S(1)}, f32[2,128]{1,0:T(2,128)}, u32[]{:S(2)}) copy-start(f32[2,128]{1,0:T(2,128)} %ambient.1) | copy-start | bytes 3076
  1.9 16.9 %collective-permute-start.1 = (f32[2,4,80,128]{3,2,1,0:T(8,128)S(1)}, f32[2,4,80,128]{3,2,1,0:T(8,128)S(1)}, u32[]{:S(2)}, u32[]{:S(2)}) collective-permute-start(f32[2,4,80,128]{3,2,1,0:T(8,128)S(1)} %get-tuple-element.6.own), channel_id=1, source_target_pairs={{2,4},{4,2},{6,8},{8,6},{10,12},{12,10},{14,16},{16,14},{18,20},{2... | collective-permute-start | bytes 983048 | tf_op jit(solution)/shard_map/ppermute | solution.py:403
  3.7 15.1 %collective-permute-start = (f32[2,4,80,128]{3,2,1,0:T(8,128)S(1)}, f32[2,4,80,128]{3,2,1,0:T(8,128)S(1)}, u32[]{:S(2)}, u32[]{:S(2)}) collective-permute-start(f32[2,4,80,128]{3,2,1,0:T(8,128)S(1)} %get-tuple-element.6.own), channel_id=1, source_target_pairs={{0,2},{2,0},{4,6},{6,4},{8,10},{10,8},{12,14},{14,12},{16,18},{18,... | collective-permute-start | bytes 983048 | tf_op jit(solution)/shard_map/ppermute | solution.py:404
  6.6 6.5 %collective-permute-start.7 = (f32[80,128]{1,0:T(8,128)S(1)}, f32[80,128]{1,0:T(8,128)S(1)}, u32[]{:S(2)}, u32[]{:S(2)}) collective-permute-start(f32[80,128]{1,0:T(8,128)S(1)} %get-tuple-element.7), channel_id=1, source_target_pairs={{3,27},{7,23},{11,19},{15,15},{19,11},{23,7},{27,3},{31,31}} | collective-permute-start | bytes 122888 | tf_op jit(solution)/shard_map/ppermute | solution.py:409
  9.0 8.5 %collective-permute-start.5 = (f32[80,128]{1,0:T(8,128)S(1)}, f32[80,128]{1,0:T(8,128)S(1)}, u32[]{:S(2)}, u32[]{:S(2)}) collective-permute-start(f32[80,128]{1,0:T(8,128)S(1)} %get-tuple-element.7), channel_id=1, source_target_pairs={{1,31},{3,29},{5,27},{7,25},{9,23},{11,21},{13,19},{15,17},{17,15}... | collective-permute-start | bytes 122888 | tf_op jit(solution)/shard_map/ppermute | solution.py:408
  10.9 6.5 %collective-permute-start.2 = (f32[80,128]{1,0:T(8,128)S(1)}, f32[80,128]{1,0:T(8,128)S(1)}, u32[]{:S(2)}, u32[]{:S(2)}) collective-permute-start(f32[80,128]{1,0:T(8,128)S(1)} %get-tuple-element.7), channel_id=1, source_target_pairs={{0,1},{1,0},{2,3},{3,2},{4,5},{5,4},{6,7},{7,6},{8,9},{9,8},{10,11... | collective-permute-start | bytes 122888 | tf_op jit(solution)/shard_map/ppermute | solution.py:413
  13.1 5.2 %collective-permute-start.4 = (f32[80,128]{1,0:T(8,128)S(1)}, f32[80,128]{1,0:T(8,128)S(1)}, u32[]{:S(2)}, u32[]{:S(2)}) collective-permute-start(f32[80,128]{1,0:T(8,128)S(1)} %get-tuple-element.7), channel_id=1, source_target_pairs={{2,5},{3,4},{4,3},{5,2},{6,9},{7,8},{8,7},{9,6},{10,13},{11,12},{1... | collective-permute-start | bytes 122888 | tf_op jit(solution)/shard_map/ppermute | solution.py:413
  17.4 1.2 %collective-permute-start.6 = (f32[80,128]{1,0:T(8,128)S(1)}, f32[80,128]{1,0:T(8,128)S(1)}, u32[]{:S(2)}, u32[]{:S(2)}) collective-permute-start(f32[80,128]{1,0:T(8,128)S(1)} %collective-permute-done.5.fold_1), channel_id=1, source_target_pairs={{0,2},{2,0},{4,6},{6,4},{8,10},{10,8},{12,14},{14,12},{16,18},{18,... | collective-permute-start | bytes 122888 | tf_op jit(solution)/shard_map/ppermute | solution.py:421
  17.4 1.4 %collective-permute-start.3 = (f32[80,128]{1,0:T(8,128)S(1)}, f32[80,128]{1,0:T(8,128)S(1)}, u32[]{:S(2)}, u32[]{:S(2)}) collective-permute-start(f32[80,128]{1,0:T(8,128)S(1)} %collective-permute-done.2.south.north), channel_id=1, source_target_pairs={{0,2},{2,0},{4,6},{6,4},{8,10},{10,8},{12,14},{14,12},{16,18},{18,... | collective-permute-start | bytes 122888 | tf_op jit(solution)/shard_map/ppermute | solution.py:414

commit v3 on v2

--- a/solution.py
+++ b/solution.py
@@ -12,6 +12,7 @@
 
 LANES = 128
 VMEM_LIMIT = 16 << 20
+RESCALE = 16
 ROWS = 8
 FLOOD_ROW = 0
 MIX_ROW = 1
@@ -126,19 +127,18 @@
     south_lane = (lane == 0) | (lane == 2)
 
     def put_south(b, f, values):
-        rows = pl.ds(pl.multiple_of(ROWS * b, ROWS), ROWS)
+        rows = pl.ds(ROWS * b, ROWS)
         for e in range(3):
             edges[e, f, rows, :] = values[e]
 
     def put_north(b, f, values):
-        rows = pl.ds(pl.multiple_of(ROWS * b, ROWS), ROWS)
+        rows = pl.ds(ROWS * b, ROWS)
         for e in range(3):
             edges[e, f, rows, :] = jnp.where(south_lane, edges[e, f, rows, :], values[e])
 
     def each_block(body):
-        @pl.loop(0, blocks)
-        def _(b):
-            body(b, pl.ds(pl.multiple_of(ROWS * b, ROWS), ROWS))
+        for b in range(blocks):
+            body(b, pl.ds(ROWS * b, ROWS))
 
     def shift(x, source, target):
         return pltpu.roll(x, (target - source) % LANES, 1)
@@ -340,25 +340,30 @@
             lower = ambient_row[s] * (0.2 + 1.0 / (1.0 + 10.0 * jnp.maximum(dense - above, 0.0)))
             lower = jnp.where(gate, lower, 0.0)
             for f in range(4):
-                columns[2 * f + place_s, rows, :] = final[f]
-                couple[2 * f + place_s, rows, :] = lower
+                columns[rows, 2 * f + place_s, :] = final[f]
+                couple[rows, 2 * f + place_s, :] = lower
         return tuple(next_1), tuple(next_2), tuple(next_3)
 
     lax.fori_loop(
-        0, blocks, block_body, ((zero,) * len(all_sets), (zero,) * len(cell_sets), (zero,) * 2)
+        0, blocks, block_body, ((zero,) * len(all_sets), (zero,) * len(cell_sets), (zero,) * 2), unroll=blocks
     )
 
-    gain = jnp.ones((ROWS, LANES), jnp.float32)
+    top = jnp.ones((ROWS, LANES), jnp.float32)
+    bottom = top
     value = zero
     lower = zero
     for k in range(levels):
-        upper = couple[:, k + 1, :]
-        inverse = 1.0 / (gain + upper)
-        value = (columns[:, k, :] + lower * value) * inverse
-        share = upper * inverse
+        upper = couple[k + 1]
+        grown = top + upper * bottom
+        inverse = bottom / grown
+        value = columns[k] * inverse + (lower * inverse) * value
         state[k] = value
-        ratio[k] = share
-        gain = 1.0 + share * gain
+        ratio[k] = upper * inverse
+        top = grown + upper * top
+        bottom = grown
+        if k % RESCALE == RESCALE - 1:
+            scale = 1.0 / bottom
+            top, bottom = top * scale, jnp.ones_like(bottom)
         lower = upper
     current = value
     for k in range(levels - 2, -1, -1):
@@ -430,8 +435,8 @@
         scratch_shapes=[
             pltpu.VMEM((3, 4, padded, LANES), jnp.float32),
             pltpu.VMEM((5, 9, ROWS, LANES), jnp.float32),
-            pltpu.VMEM((ROWS, padded, LANES), jnp.float32),
-            pltpu.VMEM((ROWS, padded, LANES), jnp.float32),
+            pltpu.VMEM((padded, ROWS, LANES), jnp.float32),
+            pltpu.VMEM((padded, ROWS, LANES), jnp.float32),
             pltpu.VMEM((levels, ROWS, LANES), jnp.float32),
             pltpu.VMEM((levels, ROWS, LANES), jnp.float32),
             pltpu.SemaphoreType.DMA((4,)),

time: 25.1 us -> 23 us (0.916)
  the two profiles are of different devices: /device:TPU:5 before, /device:TPU:0 now
where the time goes in v3:
time: 23 us; the launch traced here: 22.8 us
  starting transfers between devices  15.7 us (68%)
  Pallas kernels  4.21 us (18%)
  waiting for transfers between devices  2.15 us (9%)
  between operations  0.69 us (3%)
    ppermute x2, starting transfers between devices, shards(): lax.ppermute(edge, axes, joint(lon, lats))  6.79 us
    ppermute x1, starting transfers between devices, shards(): side_b = lax.ppermute(tile, 'lon', lon_b)  5.48 us
    pallas_call x1, Pallas kernels, shards(): pl.pallas_call(functools.partial(step_kernel, levels, lat_count), out_sha...  2.97 us
    ppermute x2, waiting for transfers between devices, shards(): lax.ppermute(edge, axes, joint(lon, lats))  2.13 us
    ppermute x1, starting transfers between devices, shards(): folds = [fold_1, lax.ppermute(fold_1, 'lon', lon_a), fold_2]  2.04 us
    pallas_call x1, Pallas kernels, pack(): pl.pallas_call(functools.partial(pack_kernel, levels), out_shape=(jax.Sha...  1.24 us
    ppermute x1, starting transfers between devices, shards(): fold_1 = lax.ppermute(edge, axes, joint(mirror, top))  0.66 us
    ppermute x1, starting transfers between devices, shards(): fold_2 = lax.ppermute(edge, axes, joint(mirror_odd, top))  0.65 us
  transfers between devices with their start and end apart: 8, of which 1 were waited for; matrix products, arithmetic and copies ran while one was open for 0% of the time, Pallas kernels for 0%

profile of v3, /device:TPU:0, one launch (start us, length us, event | category | flops | bytes accessed | tf_op | source)
XLA Modules:
  0.0 22.8 jit_solution(5491969348544333549)
XLA Ops:
  0.6 1.2 %shard_map.102 = (f32[2,4,80,128]{3,2,1,0:T(8,128)S(1)}, f32[80,128]{1,0:T(8,128)S(1)}) custom-call(f32[75,2,128]{2,1,0:T(2,128)} %temp.1, f32[75,2,128]{2,1,0:T(2,128)} %salt.1, f32[75,2,128]{2,1,0:T(2,128)} %zonal.1, f32[75,2,128]{2,1,0:T(2,128)} %merid.1, s32[2,128]{1,0:T(2,128)} %flood.1, f32[2,128]{1,0:T(2,128)} %mix.1), custom_call_target="tpu_custom_call" | custom-call | tf_op jit(solution)/shard_map/pallas_call | solution.py:73
  1.9 0.0 copy-start
  1.9 5.5 %collective-permute-start.1 = (f32[2,4,80,128]{3,2,1,0:T(8,128)S(1)}, f32[2,4,80,128]{3,2,1,0:T(8,128)S(1)}, u32[]{:S(2)}, u32[]{:S(2)}) collective-permute-start(f32[2,4,80,128]{3,2,1,0:T(8,128)S(1)} %get-tuple-element.6.own), channel_id=1, source_target_pairs={{2,4},{4,2},{6,8},{8,6},{10,12},{12,10},{14,16},{16,14},{18,20},{2... | collective-permute-start | bytes 983048 | tf_op jit(solution)/shard_map/ppermute | solution.py:408
  7.4 0.0 collective-permute-start
  7.4 0.7 %collective-permute-start.7 = (f32[80,128]{1,0:T(8,128)S(1)}, f32[80,128]{1,0:T(8,128)S(1)}, u32[]{:S(2)}, u32[]{:S(2)}) collective-permute-start(f32[80,128]{1,0:T(8,128)S(1)} %get-tuple-element.7), channel_id=1, source_target_pairs={{3,27},{7,23},{11,19},{15,15},{19,11},{23,7},{27,3},{31,31}} | collective-permute-start | bytes 122888 | tf_op jit(solution)/shard_map/ppermute | solution.py:414
  8.0 0.7 %collective-permute-start.5 = (f32[80,128]{1,0:T(8,128)S(1)}, f32[80,128]{1,0:T(8,128)S(1)}, u32[]{:S(2)}, u32[]{:S(2)}) collective-permute-start(f32[80,128]{1,0:T(8,128)S(1)} %get-tuple-element.7), channel_id=1, source_target_pairs={{1,31},{3,29},{5,27},{7,25},{9,23},{11,21},{13,19},{15,17},{17,15}... | collective-permute-start | bytes 122888 | tf_op jit(solution)/shard_map/ppermute | solution.py:413
  8.7 3.6 %collective-permute-start.2 = (f32[80,128]{1,0:T(8,128)S(1)}, f32[80,128]{1,0:T(8,128)S(1)}, u32[]{:S(2)}, u32[]{:S(2)}) collective-permute-start(f32[80,128]{1,0:T(8,128)S(1)} %get-tuple-element.7), channel_id=1, source_target_pairs={{0,1},{1,0},{2,3},{3,2},{4,5},{5,4},{6,7},{7,6},{8,9},{9,8},{10,11... | collective-permute-start | bytes 122888 | tf_op jit(solution)/shard_map/ppermute | solution.py:418
  12.3 0.0 collective-permute-done.7.fold_odd
  12.3 3.2 %collective-permute-start.4 = (f32[80,128]{1,0:T(8,128)S(1)}, f32[80,128]{1,0:T(8,128)S(1)}, u32[]{:S(2)}, u32[]{:S(2)}) collective-permute-start(f32[80,128]{1,0:T(8,128)S(1)} %get-tuple-element.7), channel_id=1, source_target_pairs={{2,5},{3,4},{4,3},{5,2},{6,9},{7,8},{8,7},{9,6},{10,13},{11,12},{1... | collective-permute-start | bytes 122888 | tf_op jit(solution)/shard_map/ppermute | solution.py:418
  15.5 0.0 collective-permute-done.5.fold_1
  15.5 2.0 %collective-permute-start.6 = (f32[80,128]{1,0:T(8,128)S(1)}, f32[80,128]{1,0:T(8,128)S(1)}, u32[]{:S(2)}, u32[]{:S(2)}) collective-permute-start(f32[80,128]{1,0:T(8,128)S(1)} %collective-permute-done.5.fold_1), channel_id=1, source_target_pairs={{0,2},{2,0},{4,6},{6,4},{8,10},{10,8},{12,14},{14,12},{16,18},{18,... | collective-permute-start | bytes 122888 | tf_op jit(solution)/shard_map/ppermute | solution.py:426
  17.6 0.0 collective-permute-done.2.south.north
  17.6 0.1 collective-permute-start.3
  17.6 2.1 %collective-permute-done.4.south_b.north_b = f32[80,128]{1,0:T(8,128)S(1)} collective-permute-done((f32[80,128]{1,0:T(8,128)S(1)}, f32[80,128]{1,0:T(8,128)S(1)}, u32[]{:S(2)}, u32[]{:S(2)}) %collective-permute-start.4) | collective-permute-done | bytes 40992 | tf_op jit(solution)/shard_map/ppermute | solution.py:418
  19.8 0.0 collective-permute-done.6.fold_even
  19.8 0.0 collective-permute-done.3.south_a.north_a
  19.8 0.0 collective-permute-done.1.side_b
  19.8 0.0 collective-permute-done.side_a
  19.8 0.0 copy-done
  19.8 3.0 %shard_map.103 = (f32[75,2,128]{2,1,0:T(2,128)}, f32[75,2,128]{2,1,0:T(2,128)}, f32[75,2,128]{2,1,0:T(2,128)}, f32[75,2,128]{2,1,0:T(2,128)}) custom-call(f32[2,4,80,128]{3,2,1,0:T(8,128)S(1)} %get-tuple-element.6.own, f32[2,4,80,128]{3,2,1,0:T(8,128)S(1)} %collective-permute-done.side_a, f32[2,4,80,128]{3,2,1,0:T(8,128)S(1)} %collective-permute-done.1.side_b, ...), custom_call_target="tpu_custom_call" | custom-call | tf_op jit(solution)/shard_map/pallas_call | solution.py:430
Async XLA Ops:
  1.9 17.9 %copy-start = (f32[2,128]{1,0:T(2,128)S(1)}, f32[2,128]{1,0:T(2,128)}, u32[]{:S(2)}) copy-start(f32[2,128]{1,0:T(2,128)} %ambient.1) | copy-start | bytes 3076
  1.9 17.9 %collective-permute-start.1 = (f32[2,4,80,128]{3,2,1,0:T(8,128)S(1)}, f32[2,4,80,128]{3,2,1,0:T(8,128)S(1)}, u32[]{:S(2)}, u32[]{:S(2)}) collective-permute-start(f32[2,4,80,128]{3,2,1,0:T(8,128)S(1)} %get-tuple-element.6.own), channel_id=1, source_target_pairs={{2,4},{4,2},{6,8},{8,6},{10,12},{12,10},{14,16},{16,14},{18,20},{2... | collective-permute-start | bytes 983048 | tf_op jit(solution)/shard_map/ppermute | solution.py:408
  7.4 12.4 %collective-permute-start = (f32[2,4,80,128]{3,2,1,0:T(8,128)S(1)}, f32[2,4,80,128]{3,2,1,0:T(8,128)S(1)}, u32[]{:S(2)}, u32[]{:S(2)}) collective-permute-start(f32[2,4,80,128]{3,2,1,0:T(8,128)S(1)} %get-tuple-element.6.own), channel_id=1, source_target_pairs={{0,2},{2,0},{4,6},{6,4},{8,10},{10,8},{12,14},{14,12},{16,18},{18,... | collective-permute-start | bytes 983048 | tf_op jit(solution)/shard_map/ppermute | solution.py:409
  7.4 4.9 %collective-permute-start.7 = (f32[80,128]{1,0:T(8,128)S(1)}, f32[80,128]{1,0:T(8,128)S(1)}, u32[]{:S(2)}, u32[]{:S(2)}) collective-permute-start(f32[80,128]{1,0:T(8,128)S(1)} %get-tuple-element.7), channel_id=1, source_target_pairs={{3,27},{7,23},{11,19},{15,15},{19,11},{23,7},{27,3},{31,31}} | collective-permute-start | bytes 122888 | tf_op jit(solution)/shard_map/ppermute | solution.py:414
  8.0 7.5 %collective-permute-start.5 = (f32[80,128]{1,0:T(8,128)S(1)}, f32[80,128]{1,0:T(8,128)S(1)}, u32[]{:S(2)}, u32[]{:S(2)}) collective-permute-start(f32[80,128]{1,0:T(8,128)S(1)} %get-tuple-element.7), channel_id=1, source_target_pairs={{1,31},{3,29},{5,27},{7,25},{9,23},{11,21},{13,19},{15,17},{17,15}... | collective-permute-start | bytes 122888 | tf_op jit(solution)/shard_map/ppermute | solution.py:413
  8.7 8.8 %collective-permute-start.2 = (f32[80,128]{1,0:T(8,128)S(1)}, f32[80,128]{1,0:T(8,128)S(1)}, u32[]{:S(2)}, u32[]{:S(2)}) collective-permute-start(f32[80,128]{1,0:T(8,128)S(1)} %get-tuple-element.7), channel_id=1, source_target_pairs={{0,1},{1,0},{2,3},{3,2},{4,5},{5,4},{6,7},{7,6},{8,9},{9,8},{10,11... | collective-permute-start | bytes 122888 | tf_op jit(solution)/shard_map/ppermute | solution.py:418
  12.3 7.5 %collective-permute-start.4 = (f32[80,128]{1,0:T(8,128)S(1)}, f32[80,128]{1,0:T(8,128)S(1)}, u32[]{:S(2)}, u32[]{:S(2)}) collective-permute-start(f32[80,128]{1,0:T(8,128)S(1)} %get-tuple-element.7), channel_id=1, source_target_pairs={{2,5},{3,4},{4,3},{5,2},{6,9},{7,8},{8,7},{9,6},{10,13},{11,12},{1... | collective-permute-start | bytes 122888 | tf_op jit(solution)/shard_map/ppermute | solution.py:418
  15.5 4.2 %collective-permute-start.6 = (f32[80,128]{1,0:T(8,128)S(1)}, f32[80,128]{1,0:T(8,128)S(1)}, u32[]{:S(2)}, u32[]{:S(2)}) collective-permute-start(f32[80,128]{1,0:T(8,128)S(1)} %collective-permute-done.5.fold_1), channel_id=1, source_target_pairs={{0,2},{2,0},{4,6},{6,4},{8,10},{10,8},{12,14},{14,12},{16,18},{18,... | collective-permute-start | bytes 122888 | tf_op jit(solution)/shard_map/ppermute | solution.py:426
  17.6 2.2 %collective-permute-start.3 = (f32[80,128]{1,0:T(8,128)S(1)}, f32[80,128]{1,0:T(8,128)S(1)}, u32[]{:S(2)}, u32[]{:S(2)}) collective-permute-start(f32[80,128]{1,0:T(8,128)S(1)} %collective-permute-done.2.south.north), channel_id=1, source_target_pairs={{0,2},{2,0},{4,6},{6,4},{8,10},{10,8},{12,14},{14,12},{16,18},{18,... | collective-permute-start | bytes 122888 | tf_op jit(solution)/shard_map/ppermute | solution.py:419

commit v4 on v3

--- a/solution.py
+++ b/solution.py
@@ -87,27 +87,104 @@
     )(*[pltpu.with_memory_space_constraint(x, pltpu.HBM) for x in (*fields, flood, mix)])
 
 
+def edge_kernel(lat_count, *refs):
+    readers = [lambda rows, ref=ref: ref[rows, :] for ref in refs[:-1]]
+    south = [readers[i] for i in (5, 7, 3)]
+    north = [readers[i] for i in (6, 8, 4)]
+    folds = [readers[i] for i in (1, 2, 0)]
+    fill_edges(lat_count, south, north, folds, refs[-1])
+
+
+def fill_edges(lat_count, south, north, folds, edges):
+    odd = parity()
+    lat = lax.axis_index("lat")
+    blocks = edges.shape[2] // ROWS
+    lane = lax.broadcasted_iota(jnp.int32, (ROWS, LANES), 1)
+    slot_1_lane = (lane == 1) | (lane == 2)
+    south_lane = (lane == 0) | (lane == 2)
+
+    def put_south(b, f, values):
+        rows = pl.ds(ROWS * b, ROWS)
+        for e in range(3):
+            edges[e, f, rows, :] = values[e]
+
+    def put_north(b, f, values):
+        rows = pl.ds(ROWS * b, ROWS)
+        for e in range(3):
+            edges[e, f, rows, :] = jnp.where(south_lane, edges[e, f, rows, :], values[e])
+
+    def each_block(body):
+        for b in range(blocks):
+            body(b, pl.ds(ROWS * b, ROWS))
+
+    def shift(x, source, target):
+        return pltpu.roll(x, (target - source) % LANES, 1)
+
+    @pl.when(lat == 0)
+    def _():
+        def body(b, rows):
+            for f in range(4):
+                put_south(b, f, [jnp.zeros((ROWS, LANES), jnp.float32)] * 3)
+
+        each_block(body)
+
+    @pl.when(lat > 0)
+    def _():
+        def body(b, rows):
+            mid, at_a, at_b = [read(rows) for read in south]
+            for f in range(4):
+                far = shift(at_b, 8 * f + 5, 0)
+                far = jnp.where(slot_1_lane, shift(at_a, 8 * f + 5, 0), far)
+                put_south(b, f, [shift(mid, 8 * f + 5, 0), shift(mid, 8 * f + 4, 0), far])
+
+        each_block(body)
+
+    @pl.when(lat < lat_count - 1)
+    def _():
+        def body(b, rows):
+            mid, at_a, at_b = [read(rows) for read in north]
+            for f in range(4):
+                far = shift(at_b, 8 * f, 127)
+                far = jnp.where(slot_1_lane, shift(at_a, 8 * f, 127), far)
+                put_north(b, f, [shift(mid, 8 * f, 127), shift(mid, 8 * f + 1, 127), far])
+
+        each_block(body)
+
+    for top_odd in range(2):
+
+        @pl.when((lat == lat_count - 1) & (odd == top_odd))
+        def _(top_odd=top_odd):
+            def body(b, rows):
+                near, other = folds[0](rows), folds[1 + top_odd](rows)
+                if top_odd:
+                    near, other = other, near
+                for f in range(4):
+                    mine = 8 * f + 4 + 2 * (1 - top_odd)
+                    beside = 8 * f + 4 + 2 * top_odd
+                    values = []
+                    for source in (mine + 1, mine, beside + 1):
+                        values.append(
+                            jnp.where(slot_1_lane, shift(other, source, 1), shift(near, source, 127))
+                        )
+                    if f >= 2:
+                        values = [-v for v in values]
+                    put_north(b, f, values)
+
+            each_block(body)
+
+
 def step_kernel(
     levels,
     lat_count,
     own,
     side_a,
     side_b,
-    south,
-    south_a,
-    south_b,
-    north,
-    north_a,
-    north_b,
-    fold_1,
-    fold_even,
-    fold_odd,
+    edges,
     ambient,
     temp_out,
     salt_out,
     zonal_out,
     merid_out,
-    edges,
     statics,
     columns,
     couple,
@@ -125,75 +202,6 @@
     last_lane = lane == LANES - 1
     slot_1_lane = (lane == 1) | (lane == 2)
     south_lane = (lane == 0) | (lane == 2)
-
-    def put_south(b, f, values):
-        rows = pl.ds(ROWS * b, ROWS)
-        for e in range(3):
-            edges[e, f, rows, :] = values[e]
-
-    def put_north(b, f, values):
-        rows = pl.ds(ROWS * b, ROWS)
-        for e in range(3):
-            edges[e, f, rows, :] = jnp.where(south_lane, edges[e, f, rows, :], values[e])
-
-    def each_block(body):
-        for b in range(blocks):
-            body(b, pl.ds(ROWS * b, ROWS))
-
-    def shift(x, source, target):
-        return pltpu.roll(x, (target - source) % LANES, 1)
-
-    @pl.when(lat == 0)
-    def _():
-        def body(b, rows):
-            for f in range(4):
-                put_south(b, f, [jnp.zeros((ROWS, LANES), jnp.float32)] * 3)
-
-        each_block(body)
-
-    @pl.when(lat > 0)
-    def _():
-        def body(b, rows):
-            mid, at_a, at_b = south[rows, :], south_a[rows, :], south_b[rows, :]
-            for f in range(4):
-                far = shift(at_b, 8 * f + 5, 0)
-                far = jnp.where(slot_1_lane, shift(at_a, 8 * f + 5, 0), far)
-                put_south(b, f, [shift(mid, 8 * f + 5, 0), shift(mid, 8 * f + 4, 0), far])
-
-        each_block(body)
-
-    @pl.when(lat < lat_count - 1)
-    def _():
-        def body(b, rows):
-            mid, at_a, at_b = north[rows, :], north_a[rows, :], north_b[rows, :]
-            for f in range(4):
-                far = shift(at_b, 8 * f, 127)
-                far = jnp.where(slot_1_lane, shift(at_a, 8 * f, 127), far)
-                put_north(b, f, [shift(mid, 8 * f, 127), shift(mid, 8 * f + 1, 127), far])
-
-        each_block(body)
-
-    for top_odd in range(2):
-
-        @pl.when((lat == lat_count - 1) & (odd == top_odd))
-        def _(top_odd=top_odd):
-            def body(b, rows):
-                near, other = fold_1[rows, :], fold_even[rows, :]
-                if top_odd:
-                    near, other = fold_odd[rows, :], near
-                for f in range(4):
-                    mine = 8 * f + 4 + 2 * (1 - top_odd)
-                    beside = 8 * f + 4 + 2 * top_odd
-                    values = []
-                    for source in (mine + 1, mine, beside + 1):
-                        values.append(
-                            jnp.where(slot_1_lane, shift(other, source, 1), shift(near, source, 127))
-                        )
-                    if f >= 2:
-                        values = [-v for v in values]
-                    put_north(b, f, values)
-
-            each_block(body)
 
     def swap(x):
         return jnp.where(slot_1_lane, pltpu.roll(x, 2, 1), pltpu.roll(x, LANES - 2, 1))
@@ -407,15 +415,17 @@
     same = [(i, i) for i in range(lon_count)]
     side_b = lax.ppermute(tile, "lon", lon_b)
     side_a = lax.ppermute(tile, "lon", lon_a)
-    top = [(lat_count - 1, lat_count - 1)]
+    last = lat_count - 1
     mirror = [(i, lon_count - 1 - i) for i in range(lon_count)]
     mirror_odd = [(i, (lon_count - 2 - i) % lon_count) for i in range(1, lon_count, 2)]
-    fold_1 = lax.ppermute(edge, axes, joint(mirror, top))
-    fold_2 = lax.ppermute(edge, axes, joint(mirror_odd, top))
+    fold_2 = lax.ppermute(edge, axes, joint(mirror_odd, [(last, last)]))
+    same = [(i, i) for i in range(lon_count)]
     rounds = [pairs_a(lat_count)] + ([pairs_b(lat_count, False)] if lat_count > 2 else [])
+    fold_1 = lax.ppermute(edge, axes, joint(mirror, [(last, last)]))
     got = []
     for lats in rounds:
-        at_b, mid = [lax.ppermute(edge, axes, joint(lon, lats)) for lon in (lon_b, same)]
+        mid = lax.ppermute(edge, axes, joint(same, lats))
+        at_b = lax.ppermute(edge, axes, joint(lon_b, lats))
         got.append([mid, lax.ppermute(mid, "lon", lon_a), at_b])
     if len(got) == 1:
         north = south = got[0]
@@ -423,17 +433,24 @@
         flip = lax.rem(lax.axis_index("lat"), 2) == 0
         north = [jnp.where(flip, x, y) for x, y in zip(*got)]
         south = [jnp.where(flip, y, x) for x, y in zip(*got)]
-    folds = [fold_1, lax.ppermute(fold_1, "lon", lon_a), fold_2]
+    fold_even = lax.ppermute(fold_1, "lon", lon_a)
+    arrays = [fold_2, fold_1, fold_even, south[2], north[2], south[0], north[0], south[1], north[1]]
     padded = tile.shape[2]
     vmem = pl.BlockSpec(memory_space=pltpu.VMEM)
+    edges = pl.pallas_call(
+        functools.partial(edge_kernel, lat_count),
+        out_shape=jax.ShapeDtypeStruct((3, 4, padded, LANES), jnp.float32),
+        in_specs=[vmem] * len(arrays),
+        out_specs=vmem,
+        compiler_params=pltpu.CompilerParams(vmem_limit_bytes=VMEM_LIMIT),
+    )(*arrays)
     result = jax.ShapeDtypeStruct(temp.shape, jnp.float32)
     return pl.pallas_call(
         functools.partial(step_kernel, levels, lat_count),
         out_shape=(result,) * 4,
-        in_specs=[vmem] * 13,
+        in_specs=[vmem] * 5,
         out_specs=(pl.BlockSpec(memory_space=pltpu.HBM),) * 4,
         scratch_shapes=[
-            pltpu.VMEM((3, 4, padded, LANES), jnp.float32),
             pltpu.VMEM((5, 9, ROWS, LANES), jnp.float32),
             pltpu.VMEM((padded, ROWS, LANES), jnp.float32),
             pltpu.VMEM((padded, ROWS, LANES), jnp.float32),
@@ -442,7 +459,7 @@
             pltpu.SemaphoreType.DMA((4,)),
         ],
         compiler_params=pltpu.CompilerParams(vmem_limit_bytes=VMEM_LIMIT),
-    )(tile, side_a, side_b, *south, *north, *folds, ambient)
+    )(tile, side_a, side_b, edges, ambient)
 
 
 def solution(mesh):

time: 23 us -> 21.7 us (0.943)
  the two profiles are of different devices: /device:TPU:0 before, /device:TPU:5 now
where the time goes in v4:
time: 21.7 us; the launch traced here: 21.5 us
  starting transfers between devices  15 us (69%)
  Pallas kernels  4.5 us (21%)
  waiting for transfers between devices  1.24 us (6%)
  between operations  0.72 us (3%)
    ppermute x1, starting transfers between devices, shards(): fold_1 = lax.ppermute(edge, axes, joint(mirror, [(last, last)]))  4.74 us
    ppermute x1, starting transfers between devices, shards(): fold_2 = lax.ppermute(edge, axes, joint(mirror_odd, [(last, last)]))  4.72 us
    ppermute x1, starting transfers between devices, shards(): side_a = lax.ppermute(tile, 'lon', lon_a)  2.87 us
    pallas_call x1, Pallas kernels, shards(): pl.pallas_call(functools.partial(step_kernel, levels, lat_count), out_sha...  2.69 us
    ppermute x1, starting transfers between devices, shards(): side_b = lax.ppermute(tile, 'lon', lon_b)  1.84 us
    pallas_call x1, Pallas kernels, pack(): pl.pallas_call(functools.partial(pack_kernel, levels), out_shape=(jax.Sha...  1.24 us
    ppermute x1, waiting for transfers between devices, shards(): fold_2 = lax.ppermute(edge, axes, joint(mirror_odd, [(last, last)]))  1.23 us
    pallas_call x1, Pallas kernels, shards(): pl.pallas_call(functools.partial(edge_kernel, lat_count), out_shape=jax.S...  0.57 us
  transfers between devices with their start and end apart: 8, of which 1 were waited for; matrix products, arithmetic and copies ran while one was open for 0% of the time, Pallas kernels for 3%

profile of v4, /device:TPU:5, one launch (start us, length us, event | category | flops | bytes accessed | tf_op | source)
XLA Modules:
  0.0 21.5 jit_solution(204823001337623538)
XLA Ops:
  0.6 1.2 %shard_map.102 = (f32[2,4,80,128]{3,2,1,0:T(8,128)S(1)}, f32[80,128]{1,0:T(8,128)S(1)}) custom-call(f32[75,2,128]{2,1,0:T(2,128)} %temp.1, f32[75,2,128]{2,1,0:T(2,128)} %salt.1, f32[75,2,128]{2,1,0:T(2,128)} %zonal.1, f32[75,2,128]{2,1,0:T(2,128)} %merid.1, s32[2,128]{1,0:T(2,128)} %flood.1, f32[2,128]{1,0:T(2,128)} %mix.1), custom_call_target="tpu_custom_call" | custom-call | tf_op jit(solution)/shard_map/pallas_call | solution.py:73
  1.9 1.8 %collective-permute-start.1 = (f32[2,4,80,128]{3,2,1,0:T(8,128)S(1)}, f32[2,4,80,128]{3,2,1,0:T(8,128)S(1)}, u32[]{:S(2)}, u32[]{:S(2)}) collective-permute-start(f32[2,4,80,128]{3,2,1,0:T(8,128)S(1)} %get-tuple-element.6.own), channel_id=1, source_target_pairs={{2,4},{4,2},{6,8},{8,6},{10,12},{12,10},{14,16},{16,14},{18,20},{2... | collective-permute-start | bytes 983048 | tf_op jit(solution)/shard_map/ppermute | solution.py:416
  3.7 2.9 %collective-permute-start = (f32[2,4,80,128]{3,2,1,0:T(8,128)S(1)}, f32[2,4,80,128]{3,2,1,0:T(8,128)S(1)}, u32[]{:S(2)}, u32[]{:S(2)}) collective-permute-start(f32[2,4,80,128]{3,2,1,0:T(8,128)S(1)} %get-tuple-element.6.own), channel_id=1, source_target_pairs={{0,2},{2,0},{4,6},{6,4},{8,10},{10,8},{12,14},{14,12},{16,18},{18,... | collective-permute-start | bytes 983048 | tf_op jit(solution)/shard_map/ppermute | solution.py:417
  6.6 0.0 copy-start
  6.6 0.2 %collective-permute-start.6 = (f32[80,128]{1,0:T(8,128)S(1)}, f32[80,128]{1,0:T(8,128)S(1)}, u32[]{:S(2)}, u32[]{:S(2)}) collective-permute-start(f32[80,128]{1,0:T(8,128)S(1)} %get-tuple-element.7), channel_id=1, source_target_pairs={{0,1},{1,0},{2,3},{3,2},{4,5},{5,4},{6,7},{7,6},{8,9},{9,8},{10,11... | collective-permute-start | bytes 122888 | tf_op jit(solution)/shard_map/ppermute | solution.py:427
  6.8 0.0 collective-permute-start.5
  6.8 4.7 %collective-permute-start.3 = (f32[80,128]{1,0:T(8,128)S(1)}, f32[80,128]{1,0:T(8,128)S(1)}, u32[]{:S(2)}, u32[]{:S(2)}) collective-permute-start(f32[80,128]{1,0:T(8,128)S(1)} %get-tuple-element.7), channel_id=1, source_target_pairs={{1,31},{3,29},{5,27},{7,25},{9,23},{11,21},{13,19},{15,17},{17,15}... | collective-permute-start | bytes 122888 | tf_op jit(solution)/shard_map/ppermute | solution.py:424
  11.6 0.0 collective-permute-done.6.refs_5_.refs_6_
  11.6 4.7 %collective-permute-start.2 = (f32[80,128]{1,0:T(8,128)S(1)}, f32[80,128]{1,0:T(8,128)S(1)}, u32[]{:S(2)}, u32[]{:S(2)}) collective-permute-start(f32[80,128]{1,0:T(8,128)S(1)} %get-tuple-element.7), channel_id=1, source_target_pairs={{3,27},{7,23},{11,19},{15,15},{19,11},{23,7},{27,3},{31,31}} | collective-permute-start | bytes 122888 | tf_op jit(solution)/shard_map/ppermute | solution.py:421
  16.3 0.0 collective-permute-done.5.refs_3_.refs_4_
  16.3 0.1 collective-permute-start.7
  16.4 0.0 collective-permute-done.3.refs_1_
  16.4 0.5 %collective-permute-start.4 = (f32[80,128]{1,0:T(8,128)S(1)}, f32[80,128]{1,0:T(8,128)S(1)}, u32[]{:S(2)}, u32[]{:S(2)}) collective-permute-start(f32[80,128]{1,0:T(8,128)S(1)} %collective-permute-done.3.refs_1_), channel_id=1, source_target_pairs={{0,2},{2,0},{4,6},{6,4},{8,10},{10,8},{12,14},{14,12},{16,18},{18,... | collective-permute-start | bytes 122888 | tf_op jit(solution)/shard_map/ppermute | solution.py:436
  16.9 1.2 %collective-permute-done.2.refs_0_ = f32[80,128]{1,0:T(8,128)S(1)} collective-permute-done((f32[80,128]{1,0:T(8,128)S(1)}, f32[80,128]{1,0:T(8,128)S(1)}, u32[]{:S(2)}, u32[]{:S(2)}) %collective-permute-start.2) | collective-permute-done | bytes 40992 | tf_op jit(solution)/shard_map/ppermute | solution.py:421
  18.2 0.0 collective-permute-done.7.refs_7_.refs_8_
  18.2 0.0 collective-permute-done.4.refs_2_
  18.2 0.6 %shard_map.103.edges = f32[3,4,80,128]{3,2,1,0:T(8,128)S(1)} custom-call(f32[80,128]{1,0:T(8,128)S(1)} %collective-permute-done.2.refs_0_, f32[80,128]{1,0:T(8,128)S(1)} %collective-permute-done.3.refs_1_, f32[80,128]{1,0:T(8,128)S(1)} %collective-permute-done.4.refs_2_, f32[80,128]{1,0:T(8,128)S(1)} %collective-permute-done.5.refs_3_.refs_4_, ...), custom_call_target="tpu_custom_call" | custom-call | tf_op jit(solution)/shard_map/pallas_call | solution.py:440
  18.7 0.0 collective-permute-done.1.side_b
  18.7 0.0 collective-permute-done.side_a
  18.8 0.0 copy-done
  18.8 2.7 %shard_map.104 = (f32[75,2,128]{2,1,0:T(2,128)}, f32[75,2,128]{2,1,0:T(2,128)}, f32[75,2,128]{2,1,0:T(2,128)}, f32[75,2,128]{2,1,0:T(2,128)}) custom-call(f32[2,4,80,128]{3,2,1,0:T(8,128)S(1)} %get-tuple-element.6.own, f32[2,4,80,128]{3,2,1,0:T(8,128)S(1)} %collective-permute-done.side_a, f32[2,4,80,128]{3,2,1,0:T(8,128)S(1)} %collective-permute-done.1.side_b, ...), custom_call_target="tpu_custom_call" | custom-call | tf_op jit(solution)/shard_map/pallas_call | solution.py:448
Async XLA Ops:
  1.9 16.9 %collective-permute-start.1 = (f32[2,4,80,128]{3,2,1,0:T(8,128)S(1)}, f32[2,4,80,128]{3,2,1,0:T(8,128)S(1)}, u32[]{:S(2)}, u32[]{:S(2)}) collective-permute-start(f32[2,4,80,128]{3,2,1,0:T(8,128)S(1)} %get-tuple-element.6.own), channel_id=1, source_target_pairs={{2,4},{4,2},{6,8},{8,6},{10,12},{12,10},{14,16},{16,14},{18,20},{2... | collective-permute-start | bytes 983048 | tf_op jit(solution)/shard_map/ppermute | solution.py:416
  3.7 15.0 %collective-permute-start = (f32[2,4,80,128]{3,2,1,0:T(8,128)S(1)}, f32[2,4,80,128]{3,2,1,0:T(8,128)S(1)}, u32[]{:S(2)}, u32[]{:S(2)}) collective-permute-start(f32[2,4,80,128]{3,2,1,0:T(8,128)S(1)} %get-tuple-element.6.own), channel_id=1, source_target_pairs={{0,2},{2,0},{4,6},{6,4},{8,10},{10,8},{12,14},{14,12},{16,18},{18,... | collective-permute-start | bytes 983048 | tf_op jit(solution)/shard_map/ppermute | solution.py:417
  6.6 12.2 %copy-start = (f32[2,128]{1,0:T(2,128)S(1)}, f32[2,128]{1,0:T(2,128)}, u32[]{:S(2)}) copy-start(f32[2,128]{1,0:T(2,128)} %ambient.1) | copy-start | bytes 3076
  6.6 5.0 %collective-permute-start.6 = (f32[80,128]{1,0:T(8,128)S(1)}, f32[80,128]{1,0:T(8,128)S(1)}, u32[]{:S(2)}, u32[]{:S(2)}) collective-permute-start(f32[80,128]{1,0:T(8,128)S(1)} %get-tuple-element.7), channel_id=1, source_target_pairs={{0,1},{1,0},{2,3},{3,2},{4,5},{5,4},{6,7},{7,6},{8,9},{9,8},{10,11... | collective-permute-start | bytes 122888 | tf_op jit(solution)/shard_map/ppermute | solution.py:427
  6.8 9.5 %collective-permute-start.5 = (f32[80,128]{1,0:T(8,128)S(1)}, f32[80,128]{1,0:T(8,128)S(1)}, u32[]{:S(2)}, u32[]{:S(2)}) collective-permute-start(f32[80,128]{1,0:T(8,128)S(1)} %get-tuple-element.7), channel_id=1, source_target_pairs={{2,5},{3,4},{4,3},{5,2},{6,9},{7,8},{8,7},{9,6},{10,13},{11,12},{1... | collective-permute-start | bytes 122888 | tf_op jit(solution)/shard_map/ppermute | solution.py:428
  6.8 9.6 %collective-permute-start.3 = (f32[80,128]{1,0:T(8,128)S(1)}, f32[80,128]{1,0:T(8,128)S(1)}, u32[]{:S(2)}, u32[]{:S(2)}) collective-permute-start(f32[80,128]{1,0:T(8,128)S(1)} %get-tuple-element.7), channel_id=1, source_target_pairs={{1,31},{3,29},{5,27},{7,25},{9,23},{11,21},{13,19},{15,17},{17,15}... | collective-permute-start | bytes 122888 | tf_op jit(solution)/shard_map/ppermute | solution.py:424
  11.6 6.5 %collective-permute-start.2 = (f32[80,128]{1,0:T(8,128)S(1)}, f32[80,128]{1,0:T(8,128)S(1)}, u32[]{:S(2)}, u32[]{:S(2)}) collective-permute-start(f32[80,128]{1,0:T(8,128)S(1)} %get-tuple-element.7), channel_id=1, source_target_pairs={{3,27},{7,23},{11,19},{15,15},{19,11},{23,7},{27,3},{31,31}} | collective-permute-start | bytes 122888 | tf_op jit(solution)/shard_map/ppermute | solution.py:421
  16.3 1.8 %collective-permute-start.7 = (f32[80,128]{1,0:T(8,128)S(1)}, f32[80,128]{1,0:T(8,128)S(1)}, u32[]{:S(2)}, u32[]{:S(2)}) collective-permute-start(f32[80,128]{1,0:T(8,128)S(1)} %collective-permute-done.6.refs_5_.refs_6_), channel_id=1, source_target_pairs={{0,2},{2,0},{4,6},{6,4},{8,10},{10,8},{12,14},{14,12},{16,18},{18,... | collective-permute-start | bytes 122888 | tf_op jit(solution)/shard_map/ppermute | solution.py:429
  16.4 1.7 %collective-permute-start.4 = (f32[80,128]{1,0:T(8,128)S(1)}, f32[80,128]{1,0:T(8,128)S(1)}, u32[]{:S(2)}, u32[]{:S(2)}) collective-permute-start(f32[80,128]{1,0:T(8,128)S(1)} %collective-permute-done.3.refs_1_), channel_id=1, source_target_pairs={{0,2},{2,0},{4,6},{6,4},{8,10},{10,8},{12,14},{14,12},{16,18},{18,... | collective-permute-start | bytes 122888 | tf_op jit(solution)/shard_map/ppermute | solution.py:436

commit v5 on v4

v5 whole, which is shorter than its diff:
```python
import functools

import jax
import jax.numpy as jnp
from jax import lax
from jax.experimental import pallas as pl
from jax.experimental.pallas import tpu as pltpu
from jax.sharding import PartitionSpec as P

SUBSTEPS = 2
DT = 0.05

LANES = 128
VMEM_LIMIT = 16 << 20
SPAN = 32
PER_ROW = LANES // SPAN
WIDEN_COST = 1 << 32
RESCALE = 16
ROWS = 8
FLOOD_ROW = 0
MIX_ROW = 1


def density(temp, salt):
    return temp * (0.03 * salt - 0.05 * temp - 0.2) + 0.8 * salt


def pack_kernel(levels, temp, salt, zonal, merid, flood, mix, tile, edge, flood_here, mix_here, sems):
    copies = [
        pltpu.make_async_copy(flood, flood_here, sems.at[8]),
        pltpu.make_async_copy(mix, mix_here, sems.at[9]),
    ]
    for copy in copies:
        copy.start()
    for f, field in enumerate((temp, salt, zonal, merid)):
        for c in range(2):
            copy = pltpu.make_async_copy(
                field.at[:, c, :], tile.at[c, f, pl.ds(0, levels), :], sems.at[2 * f + c]
            )
            copy.start()
            copies.append(copy)
    padded = tile.shape[2]
    zero = jnp.zeros((padded - levels, LANES), jnp.float32)
    for f in range(4):
        for s in range(2):
            tile[s, f, pl.ds(levels, padded - levels), :] = zero
    for copy in copies[:2]:
        copy.wait()
    for c in range(2):
        tile[c, 0, pl.ds(levels + FLOOD_ROW, 1), :] = flood_here[pl.ds(c, 1), :].astype(jnp.float32)
        tile[c, 0, pl.ds(levels + MIX_ROW, 1), :] = mix_here[pl.ds(c, 1), :]
    lane = lax.broadcasted_iota(jnp.int32, (ROWS, LANES), 1)
    totals = [jnp.zeros((ROWS, LANES), jnp.float32)] * (edge.shape[0] // ROWS)
    for f in range(4):
        for copy in copies[2 + 2 * f : 4 + 2 * f]:
            copy.wait()
        for s in range(2):
            for b in range(padded // ROWS):
                place = SPAN * (b % PER_ROW) + 8 * f + 4 * s
                moved = pltpu.roll(tile[s, f, pl.ds(ROWS * b, ROWS), :], (place + 2) % LANES, 1)
                totals[b // PER_ROW] = jnp.where((lane >> 2) == place // 4, moved, totals[b // PER_ROW])
    for b, total in enumerate(totals):
        edge[pl.ds(ROWS * b, ROWS), :] = total


def compact_rows(padded):
    return -(-padded // (ROWS * PER_ROW)) * ROWS


def pack(fields, flood, mix):
    levels = fields[0].shape[0]
    padded = (levels + 2 + ROWS - 1) // ROWS * ROWS
    return pl.pallas_call(
        functools.partial(pack_kernel, levels),
        out_shape=(
            jax.ShapeDtypeStruct((2, 4, padded, LANES), jnp.float32),
            jax.ShapeDtypeStruct((compact_rows(padded), LANES), jnp.float32),
        ),
        in_specs=[pl.BlockSpec(memory_space=pltpu.HBM)] * 6,
        out_specs=(pl.BlockSpec(memory_space=pltpu.VMEM),) * 2,
        scratch_shapes=[
            pltpu.VMEM(flood.shape, flood.dtype),
            pltpu.VMEM(mix.shape, mix.dtype),
            pltpu.SemaphoreType.DMA((10,)),
        ],
        compiler_params=pltpu.CompilerParams(vmem_limit_bytes=VMEM_LIMIT),
    )(*[pltpu.with_memory_space_constraint(x, pltpu.HBM) for x in (*fields, flood, mix)])


def compact_place(b):
    return pl.ds(ROWS * (b // PER_ROW), ROWS), SPAN * (b % PER_ROW)


def widen_kernel(rounds, blocks, own, west, *messages):
    *messages, own_again = messages
    own_again[...] = own[...]
    lane = lax.broadcasted_iota(jnp.int32, (ROWS, LANES), 1)
    totals = [[jnp.zeros((ROWS, LANES), jnp.float32)] * (own.shape[0] // ROWS) for _ in messages]
    for b in range(blocks):
        rows, start = compact_place(b)
        line = pltpu.roll(own[rows, :], -start % LANES, 1)
        beside = pltpu.roll(west[rows, :], -start % LANES, 1)
        found = []
        for n in range(rounds):
            northward = lax.rem(lax.axis_index("lat") + n, 2) == 0
            pair = jnp.where(northward, line, pltpu.roll(line, LANES - 2, 1))
            corner = jnp.where(northward, pltpu.roll(beside, LANES - 3, 1), pltpu.roll(beside, LANES - 4, 1))
            found.append(jnp.where((lane & 2) == 0, pair, corner))
        found.append(jnp.where((lane & 2) == 0, line, pltpu.roll(beside, 2, 1)))
        for total, values in zip(totals, found):
            moved = pltpu.roll(values, start, 1)
            total[b // PER_ROW] = jnp.where((lane >> 5) == b % PER_ROW, moved, total[b // PER_ROW])
    for message, total in zip(messages, totals):
        for b, values in enumerate(total):
            message[pl.ds(ROWS * b, ROWS), :] = values


def widen(rounds, blocks, edge, west):
    vmem = pl.BlockSpec(memory_space=pltpu.VMEM)
    return pl.pallas_call(
        functools.partial(widen_kernel, rounds, blocks),
        out_shape=(jax.ShapeDtypeStruct(edge.shape, jnp.float32),) * (rounds + 2),
        in_specs=[vmem] * 2,
        out_specs=(vmem,) * (rounds + 2),
        compiler_params=pltpu.CompilerParams(vmem_limit_bytes=VMEM_LIMIT),
        cost_estimate=pl.CostEstimate(flops=WIDEN_COST, bytes_accessed=0, transcendentals=0),
    )(edge, west)


def edge_kernel(lat_count, south_east, north_east, south, north, fold, edges, lines):
    lat = lax.axis_index("lat")
    blocks = edges.shape[2] // ROWS
    lane = lax.broadcasted_iota(jnp.int32, (ROWS, LANES), 1)
    first_slot = (lane & 4) == 0

    def back(x, lanes):
        return pltpu.roll(x, -lanes % LANES, 1)

    def unpacked(ref, b, lanes=0):
        rows, start = compact_place(b)
        return back(ref[rows, :], start + lanes)

    def corners(b, beside, east, lanes):
        return jnp.where(first_slot, unpacked(beside, b, lanes), unpacked(east, b, 2 * lanes - 6))

    def put(b, ones, twos, sides):
        rows = pl.ds(ROWS * b, ROWS)
        below = lat > 0
        cells = jnp.where(below, unpacked(south, b), 0.0)
        beside = jnp.where(below, corners(b, south, south_east, 1), 0.0)
        lines[0, rows, :] = jnp.where((lane & 3) == 1, cells, ones)
        lines[1, rows, :] = jnp.where((lane & 3) == 0, cells, twos)
        lines[2, rows, :] = jnp.where((lane & 3) == 1, beside, sides)

    @pl.when(lat < lat_count - 1)
    def _():
        for b in range(blocks):
            put(b, unpacked(north, b), unpacked(north, b, 2), corners(b, north, north_east, 2))

    @pl.when(lat == lat_count - 1)
    def _():
        turned = jnp.where(lane >= 16, -1.0, 1.0)
        turned_two = jnp.where((lane >= 15) & (lane < LANES - 1), -1.0, 1.0)
        for b in range(blocks):
            near, other = unpacked(fold, b, 1), unpacked(fold, b, 3)
            sides = jnp.where(first_slot, unpacked(fold, b, 5), unpacked(fold, b, -1))
            put(
                b,
                turned * jnp.where(first_slot, near, other),
                turned_two * jnp.where(first_slot, other, near),
                turned * sides,
            )

    for b in range(blocks):
        rows = pl.ds(ROWS * b, ROWS)
        for f in range(4):
            edges[0, f, rows, :] = back(lines[0, rows, :], 8 * f + 1)
            edges[1, f, rows, :] = back(lines[1, rows, :], 8 * f)
            edges[2, f, rows, :] = back(lines[2, rows, :], 8 * f + 1)


def step_kernel(
    levels,
    lat_count,
    own,
    east,
    west,
    edges,
    ambient,
    temp_out,
    salt_out,
    zonal_out,
    merid_out,
    statics,
    columns,
    couple,
    state,
    ratio,
    sems,
):
    lat = lax.axis_index("lat")
    padded = own.shape[2]
    blocks = padded // ROWS
    lane = lax.broadcasted_iota(jnp.int32, (ROWS, LANES), 1)
    row = lax.broadcasted_iota(jnp.int32, (ROWS, LANES), 0)
    first_lane = lane == 0
    last_lane = lane == LANES - 1
    slot_1_lane = (lane == 3) | (lane == 4)
    south_lane = (lane == 0) | (lane == 4)

    def swap(x):
        return jnp.where(slot_1_lane, pltpu.roll(x, 4, 1), pltpu.roll(x, LANES - 4, 1))

    def to_slot(x, slot):
        return x if slot == 0 else pltpu.roll(x, LANES - 4, 1)

    def northern(x, edge):
        return jnp.where(last_lane, edge, pltpu.roll(x, LANES - 1, 1))

    def southern(x, edge):
        return jnp.where(first_lane, edge, pltpu.roll(x, 1, 1))

    def ring(own_0, own_1):
        return jnp.where(slot_1_lane, pltpu.roll(own_1, 4, 1), own_0)

    def static_row(ref, index, which):
        line = ref[index + (pl.ds(levels + which, 1), slice(None))]
        return jnp.broadcast_to(line, (ROWS, LANES))

    sources = {
        "own0": (own, (0, 0)),
        "own1": (own, (1, 0)),
        "near0": (west, (1, 0)),
        "near1": (east, (0, 0)),
        "far0": (west, (0, 0)),
        "far1": (east, (1, 0)),
        "rim": (edges, (0, 0)),
        "rim2": (edges, (1, 0)),
        "corner": (edges, (2, 0)),
    }
    held = {name: [static_row(r, i, w) for w in (FLOOD_ROW, MIX_ROW)] for name, (r, i) in sources.items()}

    def neighbours(get, name):
        if name == "rim":
            centre = get("rim")
            beside = ring(get("own0"), get("own1"))
            beyond = get("rim2")
            north_cell = jnp.where(south_lane, beside, beyond)
            south_cell = jnp.where(south_lane, beyond, beside)
            return swap(centre), get("corner"), north_cell, south_cell
        slot = int(name[-1])
        centre = get(name)
        if name.startswith("own"):
            inner, outer, edge = get("own%d" % (1 - slot)), get("near%d" % slot), get("rim")
        else:
            inner, outer, edge = get("own%d" % slot), get("far%d" % slot), get("corner")
        edge = to_slot(edge, slot)
        return inner, outer, northern(centre, edge), southern(centre, edge)

    cell_sets = ("own0", "own1", "near0", "near1", "rim")
    for n, name in enumerate(cell_sets):
        flood_at = neighbours(lambda k: held[k][0], name)
        mix_at = neighbours(lambda k: held[k][1], name)
        statics[n, 0] = held[name][0]
        for m in range(4):
            statics[n, 1 + m] = jnp.minimum(held[name][0], flood_at[m])
            statics[n, 5 + m] = (0.5 * DT) * (held[name][1] + mix_at[m])

    total_rows = LANES * lat_count
    place = lat * LANES + lane
    rim_place = lat * LANES + jnp.where(south_lane, -1, LANES)

    def turning(index):
        index = jnp.where(index >= total_rows, 2 * total_rows - 1 - index, index)
        return DT * (0.2 + index.astype(jnp.float32) / total_rows)

    planet = {True: turning(rim_place), False: turning(place)}
    sigma_of = {
        "own0": 1.0,
        "near0": 1.0,
        "own1": -1.0,
        "near1": -1.0,
        "rim": jnp.where(slot_1_lane, -1.0, 1.0),
    }

    def running(x, carry):
        for step in (1, 2, 4):
            x = x + jnp.where(row >= step, pltpu.roll(x, step, 0), 0.0)
        x = x + carry
        return x, jnp.broadcast_to(x[ROWS - 1 :, :], (ROWS, LANES))

    def advance(name, level, fields, pressure):
        n = cell_sets.index(name)
        wet = level < statics[n, 0]
        weights = [jnp.where(level < statics[n, 1 + m], statics[n, 5 + m], 0.0) for m in range(4)]
        keep = jnp.where(wet, 1.0, 0.0)
        centre = keep - ((weights[0] + weights[1]) + (weights[2] + weights[3]))
        half = jnp.where(wet, 0.5 * DT, 0.0)
        along = half * sigma_of[name]
        flow_u, flow_v = fields[2][name], fields[3][name]
        drift_u = along * flow_u
        drift_v = half * flow_v
        inner, outer, north_w, south_w = (
            weights[0] - drift_u,
            weights[1] + drift_u,
            weights[2] - drift_v,
            weights[3] + drift_v,
        )
        out = []
        for f in range(4):
            cells = neighbours(lambda k, f=f: fields[f][k], name)
            value = centre * fields[f][name]
            value = value + ((inner * cells[0] + outer * cells[1]) + (north_w * cells[2] + south_w * cells[3]))
            out.append(value)
        cells = neighbours(lambda k: pressure[k], name)
        turn = keep * planet[name == "rim"]
        out[2] = out[2] + (turn * flow_v - (0.5 * along) * (cells[0] - cells[1]))
        out[3] = out[3] - (turn * flow_u + (0.5 * half) * (cells[2] - cells[3]))
        return out

    all_sets = ("own0", "own1", "near0", "near1", "far0", "far1", "rim", "rim2", "corner")
    zero = jnp.zeros((ROWS, LANES), jnp.float32)
    ambient_row = [
        jnp.broadcast_to(ambient[s : s + 1, :], (ROWS, LANES)) for s in range(2)
    ]

    def block_body(b, carry):
        carry_1, carry_2, carry_3 = carry
        rows = pl.ds(pl.multiple_of(ROWS * b, ROWS), ROWS)
        level = (row + ROWS * b).astype(jnp.float32)
        fields = [{k: sources[k][0][sources[k][1][0], f, rows, :] for k in all_sets} for f in range(4)]
        pressure = {}
        next_1 = []
        for k, c in zip(all_sets, carry_1):
            pressure[k], c = running(density(fields[0][k], fields[1][k]), c)
            next_1.append(c)
        updated = {name: advance(name, level, fields, pressure) for name in cell_sets}
        fields = [{name: updated[name][f] for name in cell_sets} for f in range(4)]
        pressure = {}
        next_2 = []
        for k, c in zip(cell_sets, carry_2):
            pressure[k], c = running(density(fields[0][k], fields[1][k]), c)
            next_2.append(c)
        next_3 = []
        for s in range(2):
            final = advance("own%d" % s, level, fields, pressure)
            dense = density(final[0], final[1])
            above = jnp.where(row == 0, carry_3[s], pltpu.roll(dense, 1, 0))
            next_3.append(jnp.broadcast_to(dense[ROWS - 1 :, :], (ROWS, LANES)))
            gate = (level < statics[s, 0]) & (level > 0.0)
            lower = ambient_row[s] * (0.2 + 1.0 / (1.0 + 10.0 * jnp.maximum(dense - above, 0.0)))
            lower = jnp.where(gate, lower, 0.0)
            for f in range(4):
                columns[rows, 2 * f + s, :] = final[f]
                couple[rows, 2 * f + s, :] = lower
        return tuple(next_1), tuple(next_2), tuple(next_3)

    lax.fori_loop(
        0, blocks, block_body, ((zero,) * len(all_sets), (zero,) * len(cell_sets), (zero,) * 2), unroll=blocks
    )

    top = jnp.ones((ROWS, LANES), jnp.float32)
    bottom = top
    value = zero
    lower = zero
    for k in range(levels):
        upper = couple[k + 1]
        grown = top + upper * bottom
        inverse = bottom / grown
        value = columns[k] * inverse + (lower * inverse) * value
        state[k] = value
        ratio[k] = upper * inverse
        top = grown + upper * top
        bottom = grown
        if k % RESCALE == RESCALE - 1:
            scale = 1.0 / bottom
            top, bottom = top * scale, jnp.ones_like(bottom)
        lower = upper
    current = value
    copies = []

    def send(start, stop, group):
        for f, out in enumerate((temp_out, salt_out, zonal_out, merid_out)):
            part = pl.ds(start, stop - start)
            copy = pltpu.make_async_copy(state.at[part, pl.ds(2 * f, 2), :], out.at[part], sems.at[4 * group + f])
            copy.start()
            copies.append(copy)

    half = levels // 2
    for k in range(levels - 2, -1, -1):
        current = state[k] + ratio[k] * current
        state[k] = current
        if k == half:
            send(half, levels, 0)
    send(0, half, 1)
    for copy in copies:
        copy.wait()


def lat_rounds(count):
    rounds = [[(i, i ^ 1) for i in range(count) if i ^ 1 < count]]
    if count > 2:
        rounds.append([(i, j) for i in range(1, count) for j in [i + 1 if i % 2 else i - 1] if j < count])
    return rounds


def shards(temp, salt, zonal, merid, flood, mix, ambient):
    levels = temp.shape[0]
    lon_count = lax.axis_size("lon")
    lat_count = lax.axis_size("lat")
    axes = ("lon", "lat")
    tile, edge = pack((temp, salt, zonal, merid), flood, mix)
    def joint(lon_pairs, lat_pairs):
        return [
            (i * lat_count + m, j * lat_count + n) for i, j in lon_pairs for m, n in lat_pairs
        ]

    same = [(i, i) for i in range(lon_count)]
    around = [(0, lon_count - 1), (lon_count - 1, 0)]
    eastward = [(i, (i + 1) % lon_count) for i in range(lon_count)]
    westward = [(j, i) for i, j in eastward]
    same = [(i, i) for i in range(lon_count)]
    mirror = [(i, lon_count - 1 - i) for i in range(lon_count)]
    edge_west = lax.ppermute(edge, "lon", eastward)
    west = lax.ppermute(tile, "lon", eastward)
    east = lax.ppermute(tile, "lon", westward)
    rounds = lat_rounds(lat_count)
    *bands, top_edge, edge = widen(len(rounds), tile.shape[2] // ROWS, edge, edge_west)
    got = [
        (lax.ppermute(band, axes, joint(same, lats)), lax.ppermute(edge, axes, joint(westward, lats)))
        for band, lats in zip(bands, rounds)
    ]
    chip = [(i, i ^ 1) for i in range(lon_count)]
    pairs = joint(mirror, [(lat_count - 1, lat_count - 1)]) + joint(chip, [(i, i) for i in range(lat_count - 1)])
    fold = lax.ppermute(top_edge, axes, pairs)
    if len(got) == 1:
        south = north = got[0]
    else:
        flip = lax.rem(lax.axis_index("lat"), 2) == 0
        north = [jnp.where(flip, x, y) for x, y in zip(*got)]
        south = [jnp.where(flip, y, x) for x, y in zip(*got)]
    padded = tile.shape[2]
    vmem = pl.BlockSpec(memory_space=pltpu.VMEM)
    edges = pl.pallas_call(
        functools.partial(edge_kernel, lat_count),
        out_shape=jax.ShapeDtypeStruct((3, 4, padded, LANES), jnp.float32),
        in_specs=[vmem] * 5,
        out_specs=vmem,
        scratch_shapes=[pltpu.VMEM((3, padded, LANES), jnp.float32)],
        compiler_params=pltpu.CompilerParams(vmem_limit_bytes=VMEM_LIMIT),
    )(south[1], north[1], south[0], north[0], fold)
    result = jax.ShapeDtypeStruct(temp.shape, jnp.float32)
    return pl.pallas_call(
        functools.partial(step_kernel, levels, lat_count),
        out_shape=(result,) * 4,
        in_specs=[vmem] * 5,
        out_specs=(pl.BlockSpec(memory_space=pltpu.HBM),) * 4,
        scratch_shapes=[
            pltpu.VMEM((5, 9, ROWS, LANES), jnp.float32),
            pltpu.VMEM((padded, ROWS, LANES), jnp.float32),
            pltpu.VMEM((padded, ROWS, LANES), jnp.float32),
            pltpu.VMEM((levels, ROWS, LANES), jnp.float32),
            pltpu.VMEM((levels, ROWS, LANES), jnp.float32),
            pltpu.SemaphoreType.DMA((8,)),
        ],
        compiler_params=pltpu.CompilerParams(vmem_limit_bytes=VMEM_LIMIT),
    )(tile, east, west, edges, ambient)


def solution(mesh):
    cube = P(None, "lon", "lat")
    plane = P("lon", "lat")
    return jax.shard_map(
        shards,
        mesh=mesh,
        in_specs=(cube,) * 4 + (plane,) * 3,
        out_specs=(cube,) * 4,
        check_vma=False,
    )
```

time: 21.7 us -> 19.1 us (0.88)
  starting transfers between devices: 15 us -> 8.63 us
  waiting for transfers between devices: 1.24 us -> 5.23 us
    ppermute x8 -> x6, starting transfers between devices: 15 us -> 8.63 us  [the longest x1 3.69 us: shards(): lax.ppermute(edge, axes, joint(westward, lats))]
    ppermute x8 -> x6, waiting for transfers between devices: 1.24 us -> 5.23 us  [the longest x1 3.2 us: shards(): lax.ppermute(edge, axes, joint(westward, lats))]
    pallas_call x1, Pallas kernels: 0.57 us -> 0.31 us  [shards(): pl.pallas_call(functools.partial(edge_kernel, lat_count), out_shape=jax.S...]
    pallas_call x0 -> x1, Pallas kernels: none -> 0.24 us  [widen(): pl.pallas_call(functools.partial(widen_kernel, rounds, blocks), out_shape...]
  transfers between devices with their start and end apart: 8 -> 6, of which waited for: 1 -> 3; matrix products, arithmetic and copies ran while one was open for 0% -> 0% of each run, Pallas kernels for 3% -> 3%
where the time goes in v5:
time: 19.1 us; the launch traced here: 19 us
  starting transfers between devices  8.63 us (45%)
  waiting for transfers between devices  5.23 us (27%)
  Pallas kernels  4.4 us (23%)
  between operations  0.69 us (4%)
    ppermute x1, starting transfers between devices, shards(): lax.ppermute(edge, axes, joint(westward, lats))  3.69 us
    ppermute x1, waiting for transfers between devices, shards(): lax.ppermute(edge, axes, joint(westward, lats))  3.2 us
    pallas_call x1, Pallas kernels, shards(): pl.pallas_call(functools.partial(step_kernel, levels, lat_count), out_sha...  2.58 us
    ppermute x1, starting transfers between devices, shards(): edge_west = lax.ppermute(edge, 'lon', eastward)  1.82 us
    ppermute x1, waiting for transfers between devices, shards(): fold = lax.ppermute(top_edge, axes, pairs)  1.71 us
    ppermute x1, starting transfers between devices, shards(): lax.ppermute(band, axes, joint(same, lats))  1.71 us
    pallas_call x1, Pallas kernels, pack(): pl.pallas_call(functools.partial(pack_kernel, levels), out_shape=(jax.Sha...  1.27 us
    ppermute x1, starting transfers between devices, shards(): fold = lax.ppermute(top_edge, axes, pairs)  0.91 us
  transfers between devices with their start and end apart: 6, of which 3 were waited for; matrix products, arithmetic and copies ran while one was open for 0% of the time, Pallas kernels for 3%

profile of v5, /device:TPU:5, one launch (start us, length us, event | category | flops | bytes accessed | tf_op | source)
XLA Modules:
  0.0 19.0 jit_solution(6343276853956779458)
XLA Ops:
  0.6 1.3 %shard_map.102 = (f32[2,4,80,128]{3,2,1,0:T(8,128)S(1)}, f32[24,128]{1,0:T(8,128)S(1)}) custom-call(f32[75,2,128]{2,1,0:T(2,128)} %temp.1, f32[75,2,128]{2,1,0:T(2,128)} %salt.1, f32[75,2,128]{2,1,0:T(2,128)} %zonal.1, f32[75,2,128]{2,1,0:T(2,128)} %merid.1, s32[2,128]{1,0:T(2,128)} %flood.1, f32[2,128]{1,0:T(2,128)} %mix.1), custom_call_target="tpu_custom_call" | custom-call | tf_op jit(solution)/shard_map/pallas_call | solution.py:73
  1.9 1.8 %collective-permute-start.2 = (f32[24,128]{1,0:T(8,128)S(1)}, f32[24,128]{1,0:T(8,128)S(1)}, u32[]{:S(2)}, u32[]{:S(2)}) collective-permute-start(f32[24,128]{1,0:T(8,128)S(1)} %get-tuple-element.10.own), channel_id=1, source_target_pairs={{0,2},{2,4},{4,6},{6,8},{8,10},{10,12},{12,14},{14,16},{16,18},{18... | collective-permute-start | bytes 36872 | tf_op jit(solution)/shard_map/ppermute | solution.py:424
  3.7 0.1 collective-permute-start.1
  3.8 0.4 %collective-permute-start = (f32[2,4,80,128]{3,2,1,0:T(8,128)S(1)}, f32[2,4,80,128]{3,2,1,0:T(8,128)S(1)}, u32[]{:S(2)}, u32[]{:S(2)}) collective-permute-start(f32[2,4,80,128]{3,2,1,0:T(8,128)S(1)} %get-tuple-element.9.own), channel_id=1, source_target_pairs={{2,0},{4,2},{6,4},{8,6},{10,8},{12,10},{14,12},{16,14},{18,16},{20... | collective-permute-start | bytes 983048 | tf_op jit(solution)/shard_map/ppermute | solution.py:426
  4.2 0.3 %collective-permute-done.2.west = f32[24,128]{1,0:T(8,128)S(1)} collective-permute-done((f32[24,128]{1,0:T(8,128)S(1)}, f32[24,128]{1,0:T(8,128)S(1)}, u32[]{:S(2)}, u32[]{:S(2)}) %collective-permute-start.2) | collective-permute-done | bytes 12320 | tf_op jit(solution)/shard_map/ppermute | solution.py:424
  4.6 0.2 %shard_map.103 = (f32[24,128]{1,0:T(8,128)S(1)}, f32[24,128]{1,0:T(8,128)S(1)}, f32[24,128]{1,0:T(8,128)S(1)}) custom-call(f32[24,128]{1,0:T(8,128)S(1)} %get-tuple-element.10.own, f32[24,128]{1,0:T(8,128)S(1)} %collective-permute-done.2.west), custom_call_target="tpu_custom_call" | custom-call | flops 4294967296 | tf_op jit(solution)/shard_map/pallas_call | solution.py:120
  4.8 3.7 %collective-permute-start.3 = (f32[24,128]{1,0:T(8,128)S(1)}, f32[24,128]{1,0:T(8,128)S(1)}, u32[]{:S(2)}, u32[]{:S(2)}) collective-permute-start(f32[24,128]{1,0:T(8,128)S(1)} %get-tuple-element.11), channel_id=1, source_target_pairs={{2,1},{3,0},{4,3},{5,2},{6,5},{7,4},{8,7},{9,6},{10,9},{11,8},{12,... | collective-permute-start | bytes 36872 | tf_op jit(solution)/shard_map/ppermute | solution.py:430
  8.5 1.7 %collective-permute-start.4 = (f32[24,128]{1,0:T(8,128)S(1)}, f32[24,128]{1,0:T(8,128)S(1)}, u32[]{:S(2)}, u32[]{:S(2)}) collective-permute-start(f32[24,128]{1,0:T(8,128)S(1)} %get-tuple-element.12), channel_id=1, source_target_pairs={{0,1},{1,0},{2,3},{3,2},{4,5},{5,4},{6,7},{7,6},{8,9},{9,8},{10,11... | collective-permute-start | bytes 36872 | tf_op jit(solution)/shard_map/ppermute | solution.py:430
  10.2 0.0 copy-start
  10.2 0.9 %collective-permute-start.5 = (f32[24,128]{1,0:T(8,128)S(1)}, f32[24,128]{1,0:T(8,128)S(1)}, u32[]{:S(2)}, u32[]{:S(2)}) collective-permute-start(f32[24,128]{1,0:T(8,128)S(1)} %get-tuple-element.13), channel_id=1, source_target_pairs={{1,31},{3,29},{5,27},{7,25},{9,23},{11,21},{13,19},{15,17},{17,15}... | collective-permute-start | bytes 36872 | tf_op jit(solution)/shard_map/ppermute | solution.py:435
  11.1 3.2 %collective-permute-done.3.south_east.north_east = f32[24,128]{1,0:T(8,128)S(1)} collective-permute-done((f32[24,128]{1,0:T(8,128)S(1)}, f32[24,128]{1,0:T(8,128)S(1)}, u32[]{:S(2)}, u32[]{:S(2)}) %collective-permute-start.3) | collective-permute-done | bytes 12320 | tf_op jit(solution)/shard_map/ppermute | solution.py:430
  14.3 0.0 collective-permute-done.4.south.north
  14.3 1.7 %collective-permute-done.5.fold = f32[24,128]{1,0:T(8,128)S(1)} collective-permute-done((f32[24,128]{1,0:T(8,128)S(1)}, f32[24,128]{1,0:T(8,128)S(1)}, u32[]{:S(2)}, u32[]{:S(2)}) %collective-permute-start.5) | collective-permute-done | bytes 12320 | tf_op jit(solution)/shard_map/ppermute | solution.py:435
  16.0 0.3 %shard_map.104.edges = f32[3,4,80,128]{3,2,1,0:T(8,128)S(1)} custom-call(f32[24,128]{1,0:T(8,128)S(1)} %collective-permute-done.3.south_east.north_east, f32[24,128]{1,0:T(8,128)S(1)} %collective-permute-done.3.south_east.north_east, f32[24,128]{1,0:T(8,128)S(1)} %collective-permute-done.4.south.north, f32[24,128]{1,0:T(8,128)S(1)} %collective-permute-done.4.south.north, ...), custom_call_target="tpu_custom_call" | custom-call | tf_op jit(solution)/shard_map/pallas_call | solution.py:444
  16.3 0.0 collective-permute-done.1.west
  16.4 0.0 collective-permute-done.east
  16.4 0.0 copy-done
  16.4 2.6 %shard_map.105 = (f32[75,2,128]{2,1,0:T(2,128)}, f32[75,2,128]{2,1,0:T(2,128)}, f32[75,2,128]{2,1,0:T(2,128)}, f32[75,2,128]{2,1,0:T(2,128)}) custom-call(f32[2,4,80,128]{3,2,1,0:T(8,128)S(1)} %get-tuple-element.9.own, f32[2,4,80,128]{3,2,1,0:T(8,128)S(1)} %collective-permute-done.east, f32[2,4,80,128]{3,2,1,0:T(8,128)S(1)} %collective-permute-done.1.west, ...), custom_call_target="tpu_custom_call" | custom-call | tf_op jit(solution)/shard_map/pallas_call | solution.py:453
Async XLA Ops:
  1.9 2.7 %collective-permute-start.2 = (f32[24,128]{1,0:T(8,128)S(1)}, f32[24,128]{1,0:T(8,128)S(1)}, u32[]{:S(2)}, u32[]{:S(2)}) collective-permute-start(f32[24,128]{1,0:T(8,128)S(1)} %get-tuple-element.10.own), channel_id=1, source_target_pairs={{0,2},{2,4},{4,6},{6,8},{8,10},{10,12},{12,14},{14,16},{16,18},{18... | collective-permute-start | bytes 36872 | tf_op jit(solution)/shard_map/ppermute | solution.py:424
  3.7 12.6 %collective-permute-start.1 = (f32[2,4,80,128]{3,2,1,0:T(8,128)S(1)}, f32[2,4,80,128]{3,2,1,0:T(8,128)S(1)}, u32[]{:S(2)}, u32[]{:S(2)}) collective-permute-start(f32[2,4,80,128]{3,2,1,0:T(8,128)S(1)} %get-tuple-element.9.own), channel_id=1, source_target_pairs={{0,2},{2,4},{4,6},{6,8},{8,10},{10,12},{12,14},{14,16},{16,18},{18... | collective-permute-start | bytes 983048 | tf_op jit(solution)/shard_map/ppermute | solution.py:425
  3.8 12.6 %collective-permute-start = (f32[2,4,80,128]{3,2,1,0:T(8,128)S(1)}, f32[2,4,80,128]{3,2,1,0:T(8,128)S(1)}, u32[]{:S(2)}, u32[]{:S(2)}) collective-permute-start(f32[2,4,80,128]{3,2,1,0:T(8,128)S(1)} %get-tuple-element.9.own), channel_id=1, source_target_pairs={{2,0},{4,2},{6,4},{8,6},{10,8},{12,10},{14,12},{16,14},{18,16},{20... | collective-permute-start | bytes 983048 | tf_op jit(solution)/shard_map/ppermute | solution.py:426
  4.8 9.5 %collective-permute-start.3 = (f32[24,128]{1,0:T(8,128)S(1)}, f32[24,128]{1,0:T(8,128)S(1)}, u32[]{:S(2)}, u32[]{:S(2)}) collective-permute-start(f32[24,128]{1,0:T(8,128)S(1)} %get-tuple-element.11), channel_id=1, source_target_pairs={{2,1},{3,0},{4,3},{5,2},{6,5},{7,4},{8,7},{9,6},{10,9},{11,8},{12,... | collective-permute-start | bytes 36872 | tf_op jit(solution)/shard_map/ppermute | solution.py:430
  8.5 5.8 %collective-permute-start.4 = (f32[24,128]{1,0:T(8,128)S(1)}, f32[24,128]{1,0:T(8,128)S(1)}, u32[]{:S(2)}, u32[]{:S(2)}) collective-permute-start(f32[24,128]{1,0:T(8,128)S(1)} %get-tuple-element.12), channel_id=1, source_target_pairs={{0,1},{1,0},{2,3},{3,2},{4,5},{5,4},{6,7},{7,6},{8,9},{9,8},{10,11... | collective-permute-start | bytes 36872 | tf_op jit(solution)/shard_map/ppermute | solution.py:430
  10.2 6.2 %copy-start = (f32[2,128]{1,0:T(2,128)S(1)}, f32[2,128]{1,0:T(2,128)}, u32[]{:S(2)}) copy-start(f32[2,128]{1,0:T(2,128)} %ambient.1) | copy-start | bytes 3076
  10.2 5.8 %collective-permute-start.5 = (f32[24,128]{1,0:T(8,128)S(1)}, f32[24,128]{1,0:T(8,128)S(1)}, u32[]{:S(2)}, u32[]{:S(2)}) collective-permute-start(f32[24,128]{1,0:T(8,128)S(1)} %get-tuple-element.13), channel_id=1, source_target_pairs={{1,31},{3,29},{5,27},{7,25},{9,23},{11,21},{13,19},{15,17},{17,15}... | collective-permute-start | bytes 36872 | tf_op jit(solution)/shard_map/ppermute | solution.py:435

commit v6 on v5

--- a/solution.py
+++ b/solution.py
@@ -1,4 +1,5 @@
 import functools
+import types
 
 import jax
 import jax.numpy as jnp
@@ -14,6 +15,7 @@
 VMEM_LIMIT = 16 << 20
 SPAN = 32
 PER_ROW = LANES // SPAN
+INNER_COST = 1 << 30
 WIDEN_COST = 1 << 32
 RESCALE = 16
 ROWS = 8
@@ -25,7 +27,7 @@
     return temp * (0.03 * salt - 0.05 * temp - 0.2) + 0.8 * salt
 
 
-def pack_kernel(levels, temp, salt, zonal, merid, flood, mix, tile, edge, flood_here, mix_here, sems):
+def pack_kernel(levels, temp, salt, zonal, merid, flood, mix, ambient, tile, edge, ambient_here, flood_here, mix_here, sems):
     copies = [
         pltpu.make_async_copy(flood, flood_here, sems.at[8]),
         pltpu.make_async_copy(mix, mix_here, sems.at[9]),
@@ -39,6 +41,8 @@
             )
             copy.start()
             copies.append(copy)
+    last_copy = pltpu.make_async_copy(ambient, ambient_here, sems.at[10])
+    last_copy.start()
     padded = tile.shape[2]
     zero = jnp.zeros((padded - levels, LANES), jnp.float32)
     for f in range(4):
@@ -61,13 +65,14 @@
                 totals[b // PER_ROW] = jnp.where((lane >> 2) == place // 4, moved, totals[b // PER_ROW])
     for b, total in enumerate(totals):
         edge[pl.ds(ROWS * b, ROWS), :] = total
+    last_copy.wait()
 
 
 def compact_rows(padded):
     return -(-padded // (ROWS * PER_ROW)) * ROWS
 
 
-def pack(fields, flood, mix):
+def pack(fields, flood, mix, ambient):
     levels = fields[0].shape[0]
     padded = (levels + 2 + ROWS - 1) // ROWS * ROWS
     return pl.pallas_call(
@@ -75,16 +80,17 @@
         out_shape=(
             jax.ShapeDtypeStruct((2, 4, padded, LANES), jnp.float32),
             jax.ShapeDtypeStruct((compact_rows(padded), LANES), jnp.float32),
+            jax.ShapeDtypeStruct(ambient.shape, jnp.float32),
         ),
-        in_specs=[pl.BlockSpec(memory_space=pltpu.HBM)] * 6,
-        out_specs=(pl.BlockSpec(memory_space=pltpu.VMEM),) * 2,
+        in_specs=[pl.BlockSpec(memory_space=pltpu.HBM)] * 7,
+        out_specs=(pl.BlockSpec(memory_space=pltpu.VMEM),) * 3,
         scratch_shapes=[
             pltpu.VMEM(flood.shape, flood.dtype),
             pltpu.VMEM(mix.shape, mix.dtype),
-            pltpu.SemaphoreType.DMA((10,)),
+            pltpu.SemaphoreType.DMA((11,)),
         ],
         compiler_params=pltpu.CompilerParams(vmem_limit_bytes=VMEM_LIMIT),
-    )(*[pltpu.with_memory_space_constraint(x, pltpu.HBM) for x in (*fields, flood, mix)])
+    )(*[pltpu.with_memory_space_constraint(x, pltpu.HBM) for x in (*fields, flood, mix, ambient)])
 
 
 def compact_place(b):
@@ -127,7 +133,7 @@
     )(edge, west)
 
 
-def edge_kernel(lat_count, south_east, north_east, south, north, fold, edges, lines):
+def edge_kernel(lat_count, south_east, north_east, south, north, fold, _, edges, lines):
     lat = lax.axis_index("lat")
     blocks = edges.shape[2] // ROWS
     lane = lax.broadcasted_iota(jnp.int32, (ROWS, LANES), 1)
@@ -179,28 +185,8 @@
             edges[2, f, rows, :] = back(lines[2, rows, :], 8 * f + 1)
 
 
-def step_kernel(
-    levels,
-    lat_count,
-    own,
-    east,
-    west,
-    edges,
-    ambient,
-    temp_out,
-    salt_out,
-    zonal_out,
-    merid_out,
-    statics,
-    columns,
-    couple,
-    state,
-    ratio,
-    sems,
-):
+def stencil(levels, lat_count, statics):
     lat = lax.axis_index("lat")
-    padded = own.shape[2]
-    blocks = padded // ROWS
     lane = lax.broadcasted_iota(jnp.int32, (ROWS, LANES), 1)
     row = lax.broadcasted_iota(jnp.int32, (ROWS, LANES), 0)
     first_lane = lane == 0
@@ -226,19 +212,6 @@
     def static_row(ref, index, which):
         line = ref[index + (pl.ds(levels + which, 1), slice(None))]
         return jnp.broadcast_to(line, (ROWS, LANES))
-
-    sources = {
-        "own0": (own, (0, 0)),
-        "own1": (own, (1, 0)),
-        "near0": (west, (1, 0)),
-        "near1": (east, (0, 0)),
-        "far0": (west, (0, 0)),
-        "far1": (east, (1, 0)),
-        "rim": (edges, (0, 0)),
-        "rim2": (edges, (1, 0)),
-        "corner": (edges, (2, 0)),
-    }
-    held = {name: [static_row(r, i, w) for w in (FLOOD_ROW, MIX_ROW)] for name, (r, i) in sources.items()}
 
     def neighbours(get, name):
         if name == "rim":
@@ -258,13 +231,16 @@
         return inner, outer, northern(centre, edge), southern(centre, edge)
 
     cell_sets = ("own0", "own1", "near0", "near1", "rim")
-    for n, name in enumerate(cell_sets):
-        flood_at = neighbours(lambda k: held[k][0], name)
-        mix_at = neighbours(lambda k: held[k][1], name)
-        statics[n, 0] = held[name][0]
-        for m in range(4):
-            statics[n, 1 + m] = jnp.minimum(held[name][0], flood_at[m])
-            statics[n, 5 + m] = (0.5 * DT) * (held[name][1] + mix_at[m])
+
+    def hold(held, names):
+        for name in names:
+            n = cell_sets.index(name)
+            flood_at = neighbours(lambda k: held[k][0], name)
+            mix_at = neighbours(lambda k: held[k][1], name)
+            statics[n, 0] = held[name][0]
+            for m in range(4):
+                statics[n, 1 + m] = jnp.minimum(held[name][0], flood_at[m])
+                statics[n, 5 + m] = (0.5 * DT) * (held[name][1] + mix_at[m])
 
     total_rows = LANES * lat_count
     place = lat * LANES + lane
@@ -318,23 +294,114 @@
         out[3] = out[3] - (turn * flow_u + (0.5 * half) * (cells[2] - cells[3]))
         return out
 
-    all_sets = ("own0", "own1", "near0", "near1", "far0", "far1", "rim", "rim2", "corner")
+    def whole(sources):
+        return {name: [static_row(r, i, w) for w in (FLOOD_ROW, MIX_ROW)] for name, (r, i) in sources.items()}
+
+    turn_lane = jnp.where(last_lane, -1.0, jnp.where(first_lane, 1.0, 0.0))
+    return types.SimpleNamespace(
+        row=row, cell_sets=cell_sets, to_slot=to_slot, running=running, advance=advance, hold=hold, whole=whole, turn_lane=turn_lane
+    )
+
+
+def tile_sources(own, east, west):
+    return {
+        "own0": (own, (0, 0)),
+        "own1": (own, (1, 0)),
+        "near0": (west, (1, 0)),
+        "near1": (east, (0, 0)),
+        "far0": (west, (0, 0)),
+        "far1": (east, (1, 0)),
+    }
+
+
+def inner_kernel(levels, lat_count, own, east, west, partial, pressure_out, statics):
+    use = stencil(levels, lat_count, statics)
+    blocks = own.shape[2] // ROWS
     zero = jnp.zeros((ROWS, LANES), jnp.float32)
-    ambient_row = [
-        jnp.broadcast_to(ambient[s : s + 1, :], (ROWS, LANES)) for s in range(2)
-    ]
+    beyond = {"rim": zero, "corner": zero}
+    sources = tile_sources(own, east, west)
+    held = use.whole(sources)
+    held.update({name: (zero, zero) for name in beyond})
+    names = use.cell_sets[:4]
+    use.hold(held, names)
+    carry = {name: zero for name in sources}
+    for b in range(blocks):
+        rows = pl.ds(ROWS * b, ROWS)
+        level = (use.row + ROWS * b).astype(jnp.float32)
+        fields = [{k: r[i[0], f, rows, :] for k, (r, i) in sources.items()} | beyond for f in range(4)]
+        pressure = dict(beyond)
+        for k in sources:
+            pressure[k], carry[k] = use.running(density(fields[0][k], fields[1][k]), carry[k])
+        for s in range(2):
+            pressure_out[s, rows, :] = pressure["own%d" % s]
+        for n, name in enumerate(names):
+            for f, value in enumerate(use.advance(name, level, fields, pressure)):
+                partial[n, f, rows, :] = value
+
+
+def step_kernel(
+    levels,
+    lat_count,
+    own,
+    east,
+    west,
+    partial,
+    own_pressure,
+    edges,
+    ambient,
+    temp_out,
+    salt_out,
+    zonal_out,
+    merid_out,
+    statics,
+    ends,
+    columns,
+    couple,
+    state,
+    ratio,
+    sems,
+):
+    use = stencil(levels, lat_count, statics)
+    row, cell_sets, running = use.row, use.cell_sets, use.running
+    blocks = own.shape[2] // ROWS
+    zero = jnp.zeros((ROWS, LANES), jnp.float32)
+    sources = tile_sources(own, east, west)
+    sources.update({"rim": (edges, (0, 0)), "rim2": (edges, (1, 0)), "corner": (edges, (2, 0))})
+    held = use.whole(sources)
+    use.hold(held, ("own0", "own1", "rim"))
+    names = cell_sets[:4]
+    edge_of = ("rim", "rim", "corner", "corner")
+    at_end = use.turn_lane != 0.0
+    for n, name in enumerate(names):
+        flood, mix = [use.to_slot(x, n % 2) for x in held[edge_of[n]]]
+        ends[n, 0] = held[name][0]
+        ends[n, 1] = jnp.where(at_end, jnp.minimum(held[name][0], flood), 0.0)
+        ends[n, 2] = (0.5 * DT) * (held[name][1] + mix)
+    half_turn = (0.5 * DT) * use.turn_lane
+    ambient_row = [jnp.broadcast_to(ambient[s : s + 1, :], (ROWS, LANES)) for s in range(2)]
+    rim_sets = ("rim", "rim2", "corner")
 
     def block_body(b, carry):
         carry_1, carry_2, carry_3 = carry
         rows = pl.ds(pl.multiple_of(ROWS * b, ROWS), ROWS)
         level = (row + ROWS * b).astype(jnp.float32)
-        fields = [{k: sources[k][0][sources[k][1][0], f, rows, :] for k in all_sets} for f in range(4)]
-        pressure = {}
+        fields = [{k: sources[k][0][sources[k][1][0], f, rows, :] for k in names + rim_sets} for f in range(4)]
+        pressure = {"own%d" % s: own_pressure[s, rows, :] for s in range(2)}
         next_1 = []
-        for k, c in zip(all_sets, carry_1):
+        for k, c in zip(rim_sets, carry_1):
             pressure[k], c = running(density(fields[0][k], fields[1][k]), c)
             next_1.append(c)
-        updated = {name: advance(name, level, fields, pressure) for name in cell_sets}
+        updated = {"rim": use.advance("rim", level, fields, pressure)}
+        for n, name in enumerate(names):
+            weight = jnp.where(level < ends[n, 1], ends[n, 2], 0.0)
+            half = jnp.where(level < ends[n, 0], half_turn, 0.0)
+            reach = weight + half * fields[3][name]
+            out = []
+            for f in range(4):
+                beyond = use.to_slot(fields[f][edge_of[n]], n % 2)
+                out.append(partial[n, f, rows, :] + (reach * beyond - weight * fields[f][name]))
+            out[3] = out[3] + (0.5 * half) * use.to_slot(pressure[edge_of[n]], n % 2)
+            updated[name] = out
         fields = [{name: updated[name][f] for name in cell_sets} for f in range(4)]
         pressure = {}
         next_2 = []
@@ -343,7 +410,7 @@
             next_2.append(c)
         next_3 = []
         for s in range(2):
-            final = advance("own%d" % s, level, fields, pressure)
+            final = use.advance("own%d" % s, level, fields, pressure)
             dense = density(final[0], final[1])
             above = jnp.where(row == 0, carry_3[s], pltpu.roll(dense, 1, 0))
             next_3.append(jnp.broadcast_to(dense[ROWS - 1 :, :], (ROWS, LANES)))
@@ -356,7 +423,7 @@
         return tuple(next_1), tuple(next_2), tuple(next_3)
 
     lax.fori_loop(
-        0, blocks, block_body, ((zero,) * len(all_sets), (zero,) * len(cell_sets), (zero,) * 2), unroll=blocks
+        0, blocks, block_body, ((zero,) * len(rim_sets), (zero,) * len(cell_sets), (zero,) * 2), unroll=blocks
     )
 
     top = jnp.ones((ROWS, LANES), jnp.float32)
@@ -409,7 +476,7 @@
     lon_count = lax.axis_size("lon")
     lat_count = lax.axis_size("lat")
     axes = ("lon", "lat")
-    tile, edge = pack((temp, salt, zonal, merid), flood, mix)
+    tile, edge, ambient = pack((temp, salt, zonal, merid), flood, mix, ambient)
     def joint(lon_pairs, lat_pairs):
         return [
             (i * lat_count + m, j * lat_count + n) for i, j in lon_pairs for m, n in lat_pairs
@@ -441,22 +508,35 @@
         south = [jnp.where(flip, y, x) for x, y in zip(*got)]
     padded = tile.shape[2]
     vmem = pl.BlockSpec(memory_space=pltpu.VMEM)
+    partial, own_pressure = pl.pallas_call(
+        functools.partial(inner_kernel, levels, lat_count),
+        out_shape=(
+            jax.ShapeDtypeStruct((4, 4, padded, LANES), jnp.float32),
+            jax.ShapeDtypeStruct((2, padded, LANES), jnp.float32),
+        ),
+        in_specs=[vmem] * 3,
+        out_specs=(vmem, vmem),
+        scratch_shapes=[pltpu.VMEM((5, 9, ROWS, LANES), jnp.float32)],
+        compiler_params=pltpu.CompilerParams(vmem_limit_bytes=VMEM_LIMIT),
+        cost_estimate=pl.CostEstimate(flops=INNER_COST, bytes_accessed=0, transcendentals=0),
+    )(tile, east, west)
     edges = pl.pallas_call(
         functools.partial(edge_kernel, lat_count),
         out_shape=jax.ShapeDtypeStruct((3, 4, padded, LANES), jnp.float32),
-        in_specs=[vmem] * 5,
+        in_specs=[vmem] * 5 + [pl.BlockSpec(memory_space=pl.ANY)],
         out_specs=vmem,
         scratch_shapes=[pltpu.VMEM((3, padded, LANES), jnp.float32)],
         compiler_params=pltpu.CompilerParams(vmem_limit_bytes=VMEM_LIMIT),
-    )(south[1], north[1], south[0], north[0], fold)
+    )(south[1], north[1], south[0], north[0], fold, own_pressure)
     result = jax.ShapeDtypeStruct(temp.shape, jnp.float32)
     return pl.pallas_call(
         functools.partial(step_kernel, levels, lat_count),
         out_shape=(result,) * 4,
-        in_specs=[vmem] * 5,
+        in_specs=[vmem] * 7,
         out_specs=(pl.BlockSpec(memory_space=pltpu.HBM),) * 4,
         scratch_shapes=[
             pltpu.VMEM((5, 9, ROWS, LANES), jnp.float32),
+            pltpu.VMEM((4, 3, ROWS, LANES), jnp.float32),
             pltpu.VMEM((padded, ROWS, LANES), jnp.float32),
             pltpu.VMEM((padded, ROWS, LANES), jnp.float32),
             pltpu.VMEM((levels, ROWS, LANES), jnp.float32),
@@ -464,7 +544,7 @@
             pltpu.SemaphoreType.DMA((8,)),
         ],
         compiler_params=pltpu.CompilerParams(vmem_limit_bytes=VMEM_LIMIT),
-    )(tile, east, west, edges, ambient)
+    )(tile, east, west, partial, own_pressure, edges, ambient)
 
 
 def solution(mesh):

time: 19.1 us -> 18.7 us (0.979)
  waiting for transfers between devices: 5.23 us -> 4.57 us
  Pallas kernels: 4.4 us -> 4.61 us
    ppermute x1, waiting for transfers between devices: 3.2 us -> 0.01 us  [shards(): lax.ppermute(edge, axes, joint(westward, lats))]
    ppermute x1, waiting for transfers between devices: 0.01 us -> 2.71 us  [shards(): east = lax.ppermute(tile, 'lon', westward)]
    pallas_call x0 -> x1, Pallas kernels: none -> 0.64 us  [shards(): pl.pallas_call(functools.partial(inner_kernel, levels, lat_count), out_sh...]
    ppermute x1, waiting for transfers between devices: 1.71 us -> 1.12 us  [shards(): fold = lax.ppermute(top_edge, axes, pairs)]
    pallas_call x1, Pallas kernels: 2.58 us -> 2.15 us  [shards(): pl.pallas_call(functools.partial(step_kernel, levels, lat_count), out_sha...]
    ppermute x1, waiting for transfers between devices: 0.01 us -> 0.42 us  [shards(): west = lax.ppermute(tile, 'lon', eastward)]
  transfers between devices with their start and end apart: 6 -> 6, of which waited for: 3 -> 4; matrix products, arithmetic and copies ran while one was open for 0% -> 0% of each run, Pallas kernels for 3% -> 5%
where the time goes in v6:
time: 18.7 us; the launch traced here: 18.5 us
  starting transfers between devices  8.63 us (46%)
  Pallas kernels  4.61 us (25%)
  waiting for transfers between devices  4.57 us (24%)
  between operations  0.68 us (4%)
    ppermute x1, starting transfers between devices, shards(): lax.ppermute(edge, axes, joint(westward, lats))  3.69 us
    ppermute x1, waiting for transfers between devices, shards(): east = lax.ppermute(tile, 'lon', westward)  2.71 us
    pallas_call x1, Pallas kernels, shards(): pl.pallas_call(functools.partial(step_kernel, levels, lat_count), out_sha...  2.15 us
    ppermute x1, starting transfers between devices, shards(): edge_west = lax.ppermute(edge, 'lon', eastward)  1.82 us
    ppermute x1, starting transfers between devices, shards(): lax.ppermute(band, axes, joint(same, lats))  1.71 us
    pallas_call x1, Pallas kernels, pack(): pl.pallas_call(functools.partial(pack_kernel, levels), out_shape=(jax.Sha...  1.28 us
    ppermute x1, waiting for transfers between devices, shards(): fold = lax.ppermute(top_edge, axes, pairs)  1.12 us
    ppermute x1, starting transfers between devices, shards(): fold = lax.ppermute(top_edge, axes, pairs)  0.91 us
  transfers between devices with their start and end apart: 6, of which 4 were waited for; matrix products, arithmetic and copies ran while one was open for 0% of the time, Pallas kernels for 5%

profile of v6, /device:TPU:5, one launch (start us, length us, event | category | flops | bytes accessed | tf_op | source)
XLA Modules:
  0.0 18.5 jit_solution(1183255910970918481)
XLA Ops:
  0.6 1.3 %shard_map.102 = (f32[2,4,80,128]{3,2,1,0:T(8,128)S(1)}, f32[24,128]{1,0:T(8,128)S(1)}, f32[2,128]{1,0:T(2,128)S(1)}) custom-call(f32[75,2,128]{2,1,0:T(2,128)} %temp.1, f32[75,2,128]{2,1,0:T(2,128)} %salt.1, f32[75,2,128]{2,1,0:T(2,128)} %zonal.1, f32[75,2,128]{2,1,0:T(2,128)} %merid.1, s32[2,128]{1,0:T(2,128)} %flood.1, f32[2,128]{1,0:T(2,128)} %mix.1, ...), custom_call_target="tpu_custom_call" | custom-call | tf_op jit(solution)/shard_map/pallas_call | solution.py:78
  1.9 1.8 %collective-permute-start.2 = (f32[24,128]{1,0:T(8,128)S(1)}, f32[24,128]{1,0:T(8,128)S(1)}, u32[]{:S(2)}, u32[]{:S(2)}) collective-permute-start(f32[24,128]{1,0:T(8,128)S(1)} %get-tuple-element.15.own), channel_id=1, source_target_pairs={{0,2},{2,4},{4,6},{6,8},{8,10},{10,12},{12,14},{14,16},{16,18},{18... | collective-permute-start | bytes 36872 | tf_op jit(solution)/shard_map/ppermute | solution.py:491
  3.7 0.1 collective-permute-start.1
  3.8 0.4 %collective-permute-start = (f32[2,4,80,128]{3,2,1,0:T(8,128)S(1)}, f32[2,4,80,128]{3,2,1,0:T(8,128)S(1)}, u32[]{:S(2)}, u32[]{:S(2)}) collective-permute-start(f32[2,4,80,128]{3,2,1,0:T(8,128)S(1)} %get-tuple-element.12.own), channel_id=1, source_target_pairs={{2,0},{4,2},{6,4},{8,6},{10,8},{12,10},{14,12},{16,14},{18,16},{20... | collective-permute-start | bytes 983048 | tf_op jit(solution)/shard_map/ppermute | solution.py:493
  4.3 0.3 %collective-permute-done.2.west = f32[24,128]{1,0:T(8,128)S(1)} collective-permute-done((f32[24,128]{1,0:T(8,128)S(1)}, f32[24,128]{1,0:T(8,128)S(1)}, u32[]{:S(2)}, u32[]{:S(2)}) %collective-permute-start.2) | collective-permute-done | bytes 12320 | tf_op jit(solution)/shard_map/ppermute | solution.py:491
  4.6 0.2 %shard_map.104 = (f32[24,128]{1,0:T(8,128)S(1)}, f32[24,128]{1,0:T(8,128)S(1)}, f32[24,128]{1,0:T(8,128)S(1)}) custom-call(f32[24,128]{1,0:T(8,128)S(1)} %get-tuple-element.15.own, f32[24,128]{1,0:T(8,128)S(1)} %collective-permute-done.2.west), custom_call_target="tpu_custom_call" | custom-call | flops 4294967296 | tf_op jit(solution)/shard_map/pallas_call | solution.py:126
  4.8 3.7 %collective-permute-start.3 = (f32[24,128]{1,0:T(8,128)S(1)}, f32[24,128]{1,0:T(8,128)S(1)}, u32[]{:S(2)}, u32[]{:S(2)}) collective-permute-start(f32[24,128]{1,0:T(8,128)S(1)} %get-tuple-element.16), channel_id=1, source_target_pairs={{2,1},{3,0},{4,3},{5,2},{6,5},{7,4},{8,7},{9,6},{10,9},{11,8},{12,... | collective-permute-start | bytes 36872 | tf_op jit(solution)/shard_map/ppermute | solution.py:497
  8.5 1.7 %collective-permute-start.4 = (f32[24,128]{1,0:T(8,128)S(1)}, f32[24,128]{1,0:T(8,128)S(1)}, u32[]{:S(2)}, u32[]{:S(2)}) collective-permute-start(f32[24,128]{1,0:T(8,128)S(1)} %get-tuple-element.17), channel_id=1, source_target_pairs={{0,1},{1,0},{2,3},{3,2},{4,5},{5,4},{6,7},{7,6},{8,9},{9,8},{10,11... | collective-permute-start | bytes 36872 | tf_op jit(solution)/shard_map/ppermute | solution.py:497
  10.2 0.9 %collective-permute-start.5 = (f32[24,128]{1,0:T(8,128)S(1)}, f32[24,128]{1,0:T(8,128)S(1)}, u32[]{:S(2)}, u32[]{:S(2)}) collective-permute-start(f32[24,128]{1,0:T(8,128)S(1)} %get-tuple-element.18), channel_id=1, source_target_pairs={{1,31},{3,29},{5,27},{7,25},{9,23},{11,21},{13,19},{15,17},{17,15}... | collective-permute-start | bytes 36872 | tf_op jit(solution)/shard_map/ppermute | solution.py:502
  11.1 0.4 %collective-permute-done.1.west = f32[2,4,80,128]{3,2,1,0:T(8,128)S(1)} collective-permute-done((f32[2,4,80,128]{3,2,1,0:T(8,128)S(1)}, f32[2,4,80,128]{3,2,1,0:T(8,128)S(1)}, u32[]{:S(2)}, u32[]{:S(2)}) %collective-permute-start.1) | collective-permute-done | bytes 327712 | tf_op jit(solution)/shard_map/ppermute | solution.py:492
  11.5 2.7 %collective-permute-done.east = f32[2,4,80,128]{3,2,1,0:T(8,128)S(1)} collective-permute-done((f32[2,4,80,128]{3,2,1,0:T(8,128)S(1)}, f32[2,4,80,128]{3,2,1,0:T(8,128)S(1)}, u32[]{:S(2)}, u32[]{:S(2)}) %collective-permute-start) | collective-permute-done | bytes 327712 | tf_op jit(solution)/shard_map/ppermute | solution.py:493
  14.2 0.6 %shard_map.103 = (f32[4,4,80,128]{3,2,1,0:T(8,128)S(1)}, f32[2,80,128]{2,1,0:T(8,128)S(1)}) custom-call(f32[2,4,80,128]{3,2,1,0:T(8,128)S(1)} %get-tuple-element.12.own, f32[2,4,80,128]{3,2,1,0:T(8,128)S(1)} %collective-permute-done.east, f32[2,4,80,128]{3,2,1,0:T(8,128)S(1)} %collective-permute-done.1.west), custom_call_target="tpu_custom_call" | custom-call | flops 1073741824 | tf_op jit(solution)/shard_map/pallas_call | solution.py:511
  14.9 0.0 collective-permute-done.3.south_east.north_east
  14.9 0.0 collective-permute-done.4.south.north
  14.9 1.1 %collective-permute-done.5.fold = f32[24,128]{1,0:T(8,128)S(1)} collective-permute-done((f32[24,128]{1,0:T(8,128)S(1)}, f32[24,128]{1,0:T(8,128)S(1)}, u32[]{:S(2)}, u32[]{:S(2)}) %collective-permute-start.5) | collective-permute-done | bytes 12320 | tf_op jit(solution)/shard_map/ppermute | solution.py:502
  16.0 0.3 %shard_map.105.edges = f32[3,4,80,128]{3,2,1,0:T(8,128)S(1)} custom-call(f32[24,128]{1,0:T(8,128)S(1)} %collective-permute-done.3.south_east.north_east, f32[24,128]{1,0:T(8,128)S(1)} %collective-permute-done.3.south_east.north_east, f32[24,128]{1,0:T(8,128)S(1)} %collective-permute-done.4.south.north, f32[24,128]{1,0:T(8,128)S(1)} %collective-permute-done.4.south.north, ...), custom_call_target="tpu_custom_call" | custom-call | tf_op jit(solution)/shard_map/pallas_call | solution.py:523
  16.4 2.1 %shard_map.106 = (f32[75,2,128]{2,1,0:T(2,128)}, f32[75,2,128]{2,1,0:T(2,128)}, f32[75,2,128]{2,1,0:T(2,128)}, f32[75,2,128]{2,1,0:T(2,128)}) custom-call(f32[2,4,80,128]{3,2,1,0:T(8,128)S(1)} %get-tuple-element.12.own, f32[2,4,80,128]{3,2,1,0:T(8,128)S(1)} %collective-permute-done.east, f32[2,4,80,128]{3,2,1,0:T(8,128)S(1)} %collective-permute-done.1.west, ...), custom_call_target="tpu_custom_call" | custom-call | tf_op jit(solution)/shard_map/pallas_call | solution.py:532
Async XLA Ops:
  1.9 2.7 %collective-permute-start.2 = (f32[24,128]{1,0:T(8,128)S(1)}, f32[24,128]{1,0:T(8,128)S(1)}, u32[]{:S(2)}, u32[]{:S(2)}) collective-permute-start(f32[24,128]{1,0:T(8,128)S(1)} %get-tuple-element.15.own), channel_id=1, source_target_pairs={{0,2},{2,4},{4,6},{6,8},{8,10},{10,12},{12,14},{14,16},{16,18},{18... | collective-permute-start | bytes 36872 | tf_op jit(solution)/shard_map/ppermute | solution.py:491
  3.7 7.8 %collective-permute-start.1 = (f32[2,4,80,128]{3,2,1,0:T(8,128)S(1)}, f32[2,4,80,128]{3,2,1,0:T(8,128)S(1)}, u32[]{:S(2)}, u32[]{:S(2)}) collective-permute-start(f32[2,4,80,128]{3,2,1,0:T(8,128)S(1)} %get-tuple-element.12.own), channel_id=1, source_target_pairs={{0,2},{2,4},{4,6},{6,8},{8,10},{10,12},{12,14},{14,16},{16,18},{18... | collective-permute-start | bytes 983048 | tf_op jit(solution)/shard_map/ppermute | solution.py:492
  3.8 10.4 %collective-permute-start = (f32[2,4,80,128]{3,2,1,0:T(8,128)S(1)}, f32[2,4,80,128]{3,2,1,0:T(8,128)S(1)}, u32[]{:S(2)}, u32[]{:S(2)}) collective-permute-start(f32[2,4,80,128]{3,2,1,0:T(8,128)S(1)} %get-tuple-element.12.own), channel_id=1, source_target_pairs={{2,0},{4,2},{6,4},{8,6},{10,8},{12,10},{14,12},{16,14},{18,16},{20... | collective-permute-start | bytes 983048 | tf_op jit(solution)/shard_map/ppermute | solution.py:493
  4.8 10.1 %collective-permute-start.3 = (f32[24,128]{1,0:T(8,128)S(1)}, f32[24,128]{1,0:T(8,128)S(1)}, u32[]{:S(2)}, u32[]{:S(2)}) collective-permute-start(f32[24,128]{1,0:T(8,128)S(1)} %get-tuple-element.16), channel_id=1, source_target_pairs={{2,1},{3,0},{4,3},{5,2},{6,5},{7,4},{8,7},{9,6},{10,9},{11,8},{12,... | collective-permute-start | bytes 36872 | tf_op jit(solution)/shard_map/ppermute | solution.py:497
  8.5 6.4 %collective-permute-start.4 = (f32[24,128]{1,0:T(8,128)S(1)}, f32[24,128]{1,0:T(8,128)S(1)}, u32[]{:S(2)}, u32[]{:S(2)}) collective-permute-start(f32[24,128]{1,0:T(8,128)S(1)} %get-tuple-element.17), channel_id=1, source_target_pairs={{0,1},{1,0},{2,3},{3,2},{4,5},{5,4},{6,7},{7,6},{8,9},{9,8},{10,11... | collective-permute-start | bytes 36872 | tf_op jit(solution)/shard_map/ppermute | solution.py:497
  10.2 5.8 %collective-permute-start.5 = (f32[24,128]{1,0:T(8,128)S(1)}, f32[24,128]{1,0:T(8,128)S(1)}, u32[]{:S(2)}, u32[]{:S(2)}) collective-permute-start(f32[24,128]{1,0:T(8,128)S(1)} %get-tuple-element.18), channel_id=1, source_target_pairs={{1,31},{3,29},{5,27},{7,25},{9,23},{11,21},{13,19},{15,17},{17,15}... | collective-permute-start | bytes 36872 | tf_op jit(solution)/shard_map/ppermute | solution.py:502

commit v7 on v6

--- a/solution.py
+++ b/solution.py
@@ -133,7 +133,7 @@
     )(edge, west)
 
 
-def edge_kernel(lat_count, south_east, north_east, south, north, fold, _, edges, lines):
+def edge_kernel(lat_count, south_east, north_east, fold, south, north, _, edges, lines):
     lat = lax.axis_index("lat")
     blocks = edges.shape[2] // ROWS
     lane = lax.broadcasted_iota(jnp.int32, (ROWS, LANES), 1)
@@ -426,24 +426,31 @@
         0, blocks, block_body, ((zero,) * len(rim_sets), (zero,) * len(cell_sets), (zero,) * 2), unroll=blocks
     )
 
-    top = jnp.ones((ROWS, LANES), jnp.float32)
-    bottom = top
-    value = zero
-    lower = zero
-    for k in range(levels):
-        upper = couple[k + 1]
-        grown = top + upper * bottom
-        inverse = bottom / grown
-        value = columns[k] * inverse + (lower * inverse) * value
-        state[k] = value
-        ratio[k] = upper * inverse
-        top = grown + upper * top
-        bottom = grown
-        if k % RESCALE == RESCALE - 1:
-            scale = 1.0 / bottom
-            top, bottom = top * scale, jnp.ones_like(bottom)
-        lower = upper
-    current = value
+    middle = levels // 2
+    one = jnp.ones((ROWS, LANES), jnp.float32)
+    chains = [
+        {"levels": range(start, stop, step), "step": step, "top": one, "bottom": one, "value": zero, "before": zero}
+        for start, stop, step in ((0, middle + 1, 1), (levels - 1, middle, -1))
+    ]
+    for n in range(middle + 1):
+        for chain in chains:
+            if n >= len(chain["levels"]):
+                continue
+            k = chain["levels"][n]
+            ahead = couple[k + 1] if chain["step"] > 0 else couple[k]
+            grown = chain["top"] + ahead * chain["bottom"]
+            inverse = chain["bottom"] / grown
+            chain["value"] = columns[k] * inverse + (chain["before"] * inverse) * chain["value"]
+            chain["share"] = ahead * inverse
+            state[k] = chain["value"]
+            ratio[k] = chain["share"]
+            chain["top"] = grown + ahead * chain["top"]
+            chain["bottom"] = grown
+            if n % RESCALE == RESCALE - 1:
+                chain["top"], chain["bottom"] = chain["top"] * (1.0 / grown), jnp.ones_like(grown)
+            chain["before"] = ahead
+    upper, lower = chains
+    middle_value = (upper["value"] + upper["share"] * lower["value"]) / (1.0 - upper["share"] * lower["share"])
     copies = []
 
     def send(start, stop, group):
@@ -453,13 +460,19 @@
             copy.start()
             copies.append(copy)
 
-    half = levels // 2
-    for k in range(levels - 2, -1, -1):
-        current = state[k] + ratio[k] * current
-        state[k] = current
-        if k == half:
-            send(half, levels, 0)
-    send(0, half, 1)
+    state[middle] = middle_value
+    above = below = middle_value
+    quarter = middle // 2
+    for n in range(1, levels - middle):
+        if middle - n >= 0:
+            above = state[middle - n] + ratio[middle - n] * above
+            state[middle - n] = above
+        below = state[middle + n] + ratio[middle + n] * below
+        state[middle + n] = below
+        if n == quarter:
+            send(middle - quarter, middle + quarter + 1, 0)
+    send(0, middle - quarter, 1)
+    send(middle + quarter + 1, levels, 2)
     for copy in copies:
         copy.wait()
 
@@ -527,7 +540,7 @@
         out_specs=vmem,
         scratch_shapes=[pltpu.VMEM((3, padded, LANES), jnp.float32)],
         compiler_params=pltpu.CompilerParams(vmem_limit_bytes=VMEM_LIMIT),
-    )(south[1], north[1], south[0], north[0], fold, own_pressure)
+    )(south[1], north[1], fold, south[0], north[0], own_pressure)
     result = jax.ShapeDtypeStruct(temp.shape, jnp.float32)
     return pl.pallas_call(
         functools.partial(step_kernel, levels, lat_count),
@@ -541,7 +554,7 @@
             pltpu.VMEM((padded, ROWS, LANES), jnp.float32),
             pltpu.VMEM((levels, ROWS, LANES), jnp.float32),
             pltpu.VMEM((levels, ROWS, LANES), jnp.float32),
-            pltpu.SemaphoreType.DMA((8,)),
+            pltpu.SemaphoreType.DMA((12,)),
         ],
         compiler_params=pltpu.CompilerParams(vmem_limit_bytes=VMEM_LIMIT),
     )(tile, east, west, partial, own_pressure, edges, ambient)

time: 18.7 us -> 18.7 us (level)
  the two profiles are of different devices: /device:TPU:5 before, /device:TPU:1 now
where the time goes in v7:
time: 18.7 us; the launch traced here: 18.6 us
  starting transfers between devices  9.86 us (53%)
  Pallas kernels  4.56 us (24%)
  waiting for transfers between devices  3.47 us (19%)
  between operations  0.67 us (4%)
    ppermute x1, starting transfers between devices, shards(): lax.ppermute(edge, axes, joint(westward, lats))  5.17 us
    ppermute x1, starting transfers between devices, shards(): edge_west = lax.ppermute(edge, 'lon', eastward)  2.65 us
    ppermute x1, waiting for transfers between devices, shards(): east = lax.ppermute(tile, 'lon', westward)  2.41 us
    pallas_call x1, Pallas kernels, shards(): pl.pallas_call(functools.partial(step_kernel, levels, lat_count), out_sha...  2.11 us
    ppermute x1, starting transfers between devices, shards(): lax.ppermute(band, axes, joint(same, lats))  1.53 us
    pallas_call x1, Pallas kernels, pack(): pl.pallas_call(functools.partial(pack_kernel, levels), out_shape=(jax.Sha...  1.28 us
    ppermute x1, waiting for transfers between devices, shards(): lax.ppermute(edge, axes, joint(westward, lats))  0.71 us
    pallas_call x1, Pallas kernels, shards(): pl.pallas_call(functools.partial(inner_kernel, levels, lat_count), out_sh...  0.64 us
  transfers between devices with their start and end apart: 6, of which 3 were waited for; matrix products, arithmetic and copies ran while one was open for 0% of the time, Pallas kernels for 5%

profile of v7, /device:TPU:1, one launch (start us, length us, event | category | flops | bytes accessed | tf_op | source)
XLA Modules:
  0.0 18.6 jit_solution(12977804680866356356)
XLA Ops:
  0.6 1.3 %shard_map.102 = (f32[2,4,80,128]{3,2,1,0:T(8,128)S(1)}, f32[24,128]{1,0:T(8,128)S(1)}, f32[2,128]{1,0:T(2,128)S(1)}) custom-call(f32[75,2,128]{2,1,0:T(2,128)} %temp.1, f32[75,2,128]{2,1,0:T(2,128)} %salt.1, f32[75,2,128]{2,1,0:T(2,128)} %zonal.1, f32[75,2,128]{2,1,0:T(2,128)} %merid.1, s32[2,128]{1,0:T(2,128)} %flood.1, f32[2,128]{1,0:T(2,128)} %mix.1, ...), custom_call_target="tpu_custom_call" | custom-call | tf_op jit(solution)/shard_map/pallas_call | solution.py:78
  1.9 2.7 %collective-permute-start.2 = (f32[24,128]{1,0:T(8,128)S(1)}, f32[24,128]{1,0:T(8,128)S(1)}, u32[]{:S(2)}, u32[]{:S(2)}) collective-permute-start(f32[24,128]{1,0:T(8,128)S(1)} %get-tuple-element.15.own), channel_id=1, source_target_pairs={{0,2},{2,4},{4,6},{6,8},{8,10},{10,12},{12,14},{14,16},{16,18},{18... | collective-permute-start | bytes 36872 | tf_op jit(solution)/shard_map/ppermute | solution.py:504
  4.6 0.1 collective-permute-start.1
  4.6 0.4 %collective-permute-start = (f32[2,4,80,128]{3,2,1,0:T(8,128)S(1)}, f32[2,4,80,128]{3,2,1,0:T(8,128)S(1)}, u32[]{:S(2)}, u32[]{:S(2)}) collective-permute-start(f32[2,4,80,128]{3,2,1,0:T(8,128)S(1)} %get-tuple-element.12.own), channel_id=1, source_target_pairs={{2,0},{4,2},{6,4},{8,6},{10,8},{12,10},{14,12},{16,14},{18,16},{20... | collective-permute-start | bytes 983048 | tf_op jit(solution)/shard_map/ppermute | solution.py:506
  5.1 0.3 %collective-permute-done.2.west = f32[24,128]{1,0:T(8,128)S(1)} collective-permute-done((f32[24,128]{1,0:T(8,128)S(1)}, f32[24,128]{1,0:T(8,128)S(1)}, u32[]{:S(2)}, u32[]{:S(2)}) %collective-permute-start.2) | collective-permute-done | bytes 12320 | tf_op jit(solution)/shard_map/ppermute | solution.py:504
  5.4 0.2 %shard_map.104 = (f32[24,128]{1,0:T(8,128)S(1)}, f32[24,128]{1,0:T(8,128)S(1)}, f32[24,128]{1,0:T(8,128)S(1)}) custom-call(f32[24,128]{1,0:T(8,128)S(1)} %get-tuple-element.15.own, f32[24,128]{1,0:T(8,128)S(1)} %collective-permute-done.2.west), custom_call_target="tpu_custom_call" | custom-call | flops 4294967296 | tf_op jit(solution)/shard_map/pallas_call | solution.py:126
  5.6 5.2 %collective-permute-start.3 = (f32[24,128]{1,0:T(8,128)S(1)}, f32[24,128]{1,0:T(8,128)S(1)}, u32[]{:S(2)}, u32[]{:S(2)}) collective-permute-start(f32[24,128]{1,0:T(8,128)S(1)} %get-tuple-element.16), channel_id=1, source_target_pairs={{2,1},{3,0},{4,3},{5,2},{6,5},{7,4},{8,7},{9,6},{10,9},{11,8},{12,... | collective-permute-start | bytes 36872 | tf_op jit(solution)/shard_map/ppermute | solution.py:510
  10.8 0.0 collective-permute-start.4
  10.8 1.5 %collective-permute-start.5 = (f32[24,128]{1,0:T(8,128)S(1)}, f32[24,128]{1,0:T(8,128)S(1)}, u32[]{:S(2)}, u32[]{:S(2)}) collective-permute-start(f32[24,128]{1,0:T(8,128)S(1)} %get-tuple-element.18), channel_id=1, source_target_pairs={{0,1},{1,0},{2,3},{3,2},{4,5},{5,4},{6,7},{7,6},{8,9},{9,8},{10,11... | collective-permute-start | bytes 36872 | tf_op jit(solution)/shard_map/ppermute | solution.py:510
  12.3 0.0 collective-permute-done.1.west
  12.4 2.4 %collective-permute-done.east = f32[2,4,80,128]{3,2,1,0:T(8,128)S(1)} collective-permute-done((f32[2,4,80,128]{3,2,1,0:T(8,128)S(1)}, f32[2,4,80,128]{3,2,1,0:T(8,128)S(1)}, u32[]{:S(2)}, u32[]{:S(2)}) %collective-permute-start) | collective-permute-done | bytes 327712 | tf_op jit(solution)/shard_map/ppermute | solution.py:506
  14.8 0.6 %shard_map.103 = (f32[4,4,80,128]{3,2,1,0:T(8,128)S(1)}, f32[2,80,128]{2,1,0:T(8,128)S(1)}) custom-call(f32[2,4,80,128]{3,2,1,0:T(8,128)S(1)} %get-tuple-element.12.own, f32[2,4,80,128]{3,2,1,0:T(8,128)S(1)} %collective-permute-done.east, f32[2,4,80,128]{3,2,1,0:T(8,128)S(1)} %collective-permute-done.1.west), custom_call_target="tpu_custom_call" | custom-call | flops 1073741824 | tf_op jit(solution)/shard_map/pallas_call | solution.py:524
  15.4 0.7 %collective-permute-done.3.south_east.north_east = f32[24,128]{1,0:T(8,128)S(1)} collective-permute-done((f32[24,128]{1,0:T(8,128)S(1)}, f32[24,128]{1,0:T(8,128)S(1)}, u32[]{:S(2)}, u32[]{:S(2)}) %collective-permute-start.3) | collective-permute-done | bytes 12320 | tf_op jit(solution)/shard_map/ppermute | solution.py:510
  16.1 0.0 collective-permute-done.4.fold
  16.1 0.0 collective-permute-done.5.south.north
  16.1 0.3 %shard_map.105.edges = f32[3,4,80,128]{3,2,1,0:T(8,128)S(1)} custom-call(f32[24,128]{1,0:T(8,128)S(1)} %collective-permute-done.3.south_east.north_east, f32[24,128]{1,0:T(8,128)S(1)} %collective-permute-done.3.south_east.north_east, f32[24,128]{1,0:T(8,128)S(1)} %collective-permute-done.4.fold, f32[24,128]{1,0:T(8,128)S(1)} %collective-permute-done.5.south.north, ...), custom_call_target="tpu_custom_call" | custom-call | tf_op jit(solution)/shard_map/pallas_call | solution.py:536
  16.4 2.1 %shard_map.106 = (f32[75,2,128]{2,1,0:T(2,128)}, f32[75,2,128]{2,1,0:T(2,128)}, f32[75,2,128]{2,1,0:T(2,128)}, f32[75,2,128]{2,1,0:T(2,128)}) custom-call(f32[2,4,80,128]{3,2,1,0:T(8,128)S(1)} %get-tuple-element.12.own, f32[2,4,80,128]{3,2,1,0:T(8,128)S(1)} %collective-permute-done.east, f32[2,4,80,128]{3,2,1,0:T(8,128)S(1)} %collective-permute-done.1.west, ...), custom_call_target="tpu_custom_call" | custom-call | tf_op jit(solution)/shard_map/pallas_call | solution.py:545
Async XLA Ops:
  1.9 3.5 %collective-permute-start.2 = (f32[24,128]{1,0:T(8,128)S(1)}, f32[24,128]{1,0:T(8,128)S(1)}, u32[]{:S(2)}, u32[]{:S(2)}) collective-permute-start(f32[24,128]{1,0:T(8,128)S(1)} %get-tuple-element.15.own), channel_id=1, source_target_pairs={{0,2},{2,4},{4,6},{6,8},{8,10},{10,12},{12,14},{14,16},{16,18},{18... | collective-permute-start | bytes 36872 | tf_op jit(solution)/shard_map/ppermute | solution.py:504
  4.6 7.8 %collective-permute-start.1 = (f32[2,4,80,128]{3,2,1,0:T(8,128)S(1)}, f32[2,4,80,128]{3,2,1,0:T(8,128)S(1)}, u32[]{:S(2)}, u32[]{:S(2)}) collective-permute-start(f32[2,4,80,128]{3,2,1,0:T(8,128)S(1)} %get-tuple-element.12.own), channel_id=1, source_target_pairs={{0,2},{2,4},{4,6},{6,8},{8,10},{10,12},{12,14},{14,16},{16,18},{18... | collective-permute-start | bytes 983048 | tf_op jit(solution)/shard_map/ppermute | solution.py:505
  4.6 10.1 %collective-permute-start = (f32[2,4,80,128]{3,2,1,0:T(8,128)S(1)}, f32[2,4,80,128]{3,2,1,0:T(8,128)S(1)}, u32[]{:S(2)}, u32[]{:S(2)}) collective-permute-start(f32[2,4,80,128]{3,2,1,0:T(8,128)S(1)} %get-tuple-element.12.own), channel_id=1, source_target_pairs={{2,0},{4,2},{6,4},{8,6},{10,8},{12,10},{14,12},{16,14},{18,16},{20... | collective-permute-start | bytes 983048 | tf_op jit(solution)/shard_map/ppermute | solution.py:506
  5.6 10.5 %collective-permute-start.3 = (f32[24,128]{1,0:T(8,128)S(1)}, f32[24,128]{1,0:T(8,128)S(1)}, u32[]{:S(2)}, u32[]{:S(2)}) collective-permute-start(f32[24,128]{1,0:T(8,128)S(1)} %get-tuple-element.16), channel_id=1, source_target_pairs={{2,1},{3,0},{4,3},{5,2},{6,5},{7,4},{8,7},{9,6},{10,9},{11,8},{12,... | collective-permute-start | bytes 36872 | tf_op jit(solution)/shard_map/ppermute | solution.py:510
  10.8 5.3 %collective-permute-start.4 = (f32[24,128]{1,0:T(8,128)S(1)}, f32[24,128]{1,0:T(8,128)S(1)}, u32[]{:S(2)}, u32[]{:S(2)}) collective-permute-start(f32[24,128]{1,0:T(8,128)S(1)} %get-tuple-element.17), channel_id=1, source_target_pairs={{1,31},{3,29},{5,27},{7,25},{9,23},{11,21},{13,19},{15,17},{17,15}... | collective-permute-start | bytes 36872 | tf_op jit(solution)/shard_map/ppermute | solution.py:515
  10.8 5.3 %collective-permute-start.5 = (f32[24,128]{1,0:T(8,128)S(1)}, f32[24,128]{1,0:T(8,128)S(1)}, u32[]{:S(2)}, u32[]{:S(2)}) collective-permute-start(f32[24,128]{1,0:T(8,128)S(1)} %get-tuple-element.18), channel_id=1, source_target_pairs={{0,1},{1,0},{2,3},{3,2},{4,5},{5,4},{6,7},{7,6},{8,9},{9,8},{10,11... | collective-permute-start | bytes 36872 | tf_op jit(solution)/shard_map/ppermute | solution.py:510

commit v8 on v7

--- a/solution.py
+++ b/solution.py
@@ -133,7 +133,7 @@
     )(edge, west)
 
 
-def edge_kernel(lat_count, south_east, north_east, fold, south, north, _, edges, lines):
+def edge_kernel(lat_count, south_east, north_east, south, north, fold, _, edges, lines):
     lat = lax.axis_index("lat")
     blocks = edges.shape[2] // ROWS
     lane = lax.broadcasted_iota(jnp.int32, (ROWS, LANES), 1)
@@ -540,7 +540,7 @@
         out_specs=vmem,
         scratch_shapes=[pltpu.VMEM((3, padded, LANES), jnp.float32)],
         compiler_params=pltpu.CompilerParams(vmem_limit_bytes=VMEM_LIMIT),
-    )(south[1], north[1], fold, south[0], north[0], own_pressure)
+    )(south[1], north[1], south[0], north[0], fold, own_pressure)
     result = jax.ShapeDtypeStruct(temp.shape, jnp.float32)
     return pl.pallas_call(
         functools.partial(step_kernel, levels, lat_count),

time: 18.7 us -> 18.7 us (level)
  the two profiles are of different devices: /device:TPU:1 before, /device:TPU:5 now
where the time goes in v8:
time: 18.7 us; the launch traced here: 18.5 us
  starting transfers between devices  8.63 us (46%)
  Pallas kernels  4.58 us (24%)
  waiting for transfers between devices  4.57 us (24%)
  between operations  0.68 us (4%)
    ppermute x1, starting transfers between devices, shards(): lax.ppermute(edge, axes, joint(westward, lats))  3.69 us
    ppermute x1, waiting for transfers between devices, shards(): east = lax.ppermute(tile, 'lon', westward)  2.71 us
    pallas_call x1, Pallas kernels, shards(): pl.pallas_call(functools.partial(step_kernel, levels, lat_count), out_sha...  2.11 us
    ppermute x1, starting transfers between devices, shards(): edge_west = lax.ppermute(edge, 'lon', eastward)  1.82 us
    ppermute x1, starting transfers between devices, shards(): lax.ppermute(band, axes, joint(same, lats))  1.71 us
    pallas_call x1, Pallas kernels, pack(): pl.pallas_call(functools.partial(pack_kernel, levels), out_shape=(jax.Sha...  1.28 us
    ppermute x1, waiting for transfers between devices, shards(): fold = lax.ppermute(top_edge, axes, pairs)  1.12 us
    ppermute x1, starting transfers between devices, shards(): fold = lax.ppermute(top_edge, axes, pairs)  0.91 us
  transfers between devices with their start and end apart: 6, of which 4 were waited for; matrix products, arithmetic and copies ran while one was open for 0% of the time, Pallas kernels for 5%

profile of v8, /device:TPU:5, one launch (start us, length us, event | category | flops | bytes accessed | tf_op | source)
XLA Modules:
  0.0 18.5 jit_solution(9567937886101759081)
XLA Ops:
  0.6 1.3 %shard_map.102 = (f32[2,4,80,128]{3,2,1,0:T(8,128)S(1)}, f32[24,128]{1,0:T(8,128)S(1)}, f32[2,128]{1,0:T(2,128)S(1)}) custom-call(f32[75,2,128]{2,1,0:T(2,128)} %temp.1, f32[75,2,128]{2,1,0:T(2,128)} %salt.1, f32[75,2,128]{2,1,0:T(2,128)} %zonal.1, f32[75,2,128]{2,1,0:T(2,128)} %merid.1, s32[2,128]{1,0:T(2,128)} %flood.1, f32[2,128]{1,0:T(2,128)} %mix.1, ...), custom_call_target="tpu_custom_call" | custom-call | tf_op jit(solution)/shard_map/pallas_call | solution.py:78
  1.9 1.8 %collective-permute-start.2 = (f32[24,128]{1,0:T(8,128)S(1)}, f32[24,128]{1,0:T(8,128)S(1)}, u32[]{:S(2)}, u32[]{:S(2)}) collective-permute-start(f32[24,128]{1,0:T(8,128)S(1)} %get-tuple-element.15.own), channel_id=1, source_target_pairs={{0,2},{2,4},{4,6},{6,8},{8,10},{10,12},{12,14},{14,16},{16,18},{18... | collective-permute-start | bytes 36872 | tf_op jit(solution)/shard_map/ppermute | solution.py:504
  3.7 0.1 collective-permute-start.1
  3.8 0.4 %collective-permute-start = (f32[2,4,80,128]{3,2,1,0:T(8,128)S(1)}, f32[2,4,80,128]{3,2,1,0:T(8,128)S(1)}, u32[]{:S(2)}, u32[]{:S(2)}) collective-permute-start(f32[2,4,80,128]{3,2,1,0:T(8,128)S(1)} %get-tuple-element.12.own), channel_id=1, source_target_pairs={{2,0},{4,2},{6,4},{8,6},{10,8},{12,10},{14,12},{16,14},{18,16},{20... | collective-permute-start | bytes 983048 | tf_op jit(solution)/shard_map/ppermute | solution.py:506
  4.3 0.3 %collective-permute-done.2.west = f32[24,128]{1,0:T(8,128)S(1)} collective-permute-done((f32[24,128]{1,0:T(8,128)S(1)}, f32[24,128]{1,0:T(8,128)S(1)}, u32[]{:S(2)}, u32[]{:S(2)}) %collective-permute-start.2) | collective-permute-done | bytes 12320 | tf_op jit(solution)/shard_map/ppermute | solution.py:504
  4.6 0.2 %shard_map.104 = (f32[24,128]{1,0:T(8,128)S(1)}, f32[24,128]{1,0:T(8,128)S(1)}, f32[24,128]{1,0:T(8,128)S(1)}) custom-call(f32[24,128]{1,0:T(8,128)S(1)} %get-tuple-element.15.own, f32[24,128]{1,0:T(8,128)S(1)} %collective-permute-done.2.west), custom_call_target="tpu_custom_call" | custom-call | flops 4294967296 | tf_op jit(solution)/shard_map/pallas_call | solution.py:126
  4.8 3.7 %collective-permute-start.3 = (f32[24,128]{1,0:T(8,128)S(1)}, f32[24,128]{1,0:T(8,128)S(1)}, u32[]{:S(2)}, u32[]{:S(2)}) collective-permute-start(f32[24,128]{1,0:T(8,128)S(1)} %get-tuple-element.16), channel_id=1, source_target_pairs={{2,1},{3,0},{4,3},{5,2},{6,5},{7,4},{8,7},{9,6},{10,9},{11,8},{12,... | collective-permute-start | bytes 36872 | tf_op jit(solution)/shard_map/ppermute | solution.py:510
  8.5 1.7 %collective-permute-start.4 = (f32[24,128]{1,0:T(8,128)S(1)}, f32[24,128]{1,0:T(8,128)S(1)}, u32[]{:S(2)}, u32[]{:S(2)}) collective-permute-start(f32[24,128]{1,0:T(8,128)S(1)} %get-tuple-element.17), channel_id=1, source_target_pairs={{0,1},{1,0},{2,3},{3,2},{4,5},{5,4},{6,7},{7,6},{8,9},{9,8},{10,11... | collective-permute-start | bytes 36872 | tf_op jit(solution)/shard_map/ppermute | solution.py:510
  10.2 0.9 %collective-permute-start.5 = (f32[24,128]{1,0:T(8,128)S(1)}, f32[24,128]{1,0:T(8,128)S(1)}, u32[]{:S(2)}, u32[]{:S(2)}) collective-permute-start(f32[24,128]{1,0:T(8,128)S(1)} %get-tuple-element.18), channel_id=1, source_target_pairs={{1,31},{3,29},{5,27},{7,25},{9,23},{11,21},{13,19},{15,17},{17,15}... | collective-permute-start | bytes 36872 | tf_op jit(solution)/shard_map/ppermute | solution.py:515
  11.1 0.4 %collective-permute-done.1.west = f32[2,4,80,128]{3,2,1,0:T(8,128)S(1)} collective-permute-done((f32[2,4,80,128]{3,2,1,0:T(8,128)S(1)}, f32[2,4,80,128]{3,2,1,0:T(8,128)S(1)}, u32[]{:S(2)}, u32[]{:S(2)}) %collective-permute-start.1) | collective-permute-done | bytes 327712 | tf_op jit(solution)/shard_map/ppermute | solution.py:505
  11.5 2.7 %collective-permute-done.east = f32[2,4,80,128]{3,2,1,0:T(8,128)S(1)} collective-permute-done((f32[2,4,80,128]{3,2,1,0:T(8,128)S(1)}, f32[2,4,80,128]{3,2,1,0:T(8,128)S(1)}, u32[]{:S(2)}, u32[]{:S(2)}) %collective-permute-start) | collective-permute-done | bytes 327712 | tf_op jit(solution)/shard_map/ppermute | solution.py:506
  14.2 0.6 %shard_map.103 = (f32[4,4,80,128]{3,2,1,0:T(8,128)S(1)}, f32[2,80,128]{2,1,0:T(8,128)S(1)}) custom-call(f32[2,4,80,128]{3,2,1,0:T(8,128)S(1)} %get-tuple-element.12.own, f32[2,4,80,128]{3,2,1,0:T(8,128)S(1)} %collective-permute-done.east, f32[2,4,80,128]{3,2,1,0:T(8,128)S(1)} %collective-permute-done.1.west), custom_call_target="tpu_custom_call" | custom-call | flops 1073741824 | tf_op jit(solution)/shard_map/pallas_call | solution.py:524
  14.9 0.0 collective-permute-done.3.south_east.north_east
  14.9 0.0 collective-permute-done.4.south.north
  14.9 1.1 %collective-permute-done.5.fold = f32[24,128]{1,0:T(8,128)S(1)} collective-permute-done((f32[24,128]{1,0:T(8,128)S(1)}, f32[24,128]{1,0:T(8,128)S(1)}, u32[]{:S(2)}, u32[]{:S(2)}) %collective-permute-start.5) | collective-permute-done | bytes 12320 | tf_op jit(solution)/shard_map/ppermute | solution.py:515
  16.0 0.3 %shard_map.105.edges = f32[3,4,80,128]{3,2,1,0:T(8,128)S(1)} custom-call(f32[24,128]{1,0:T(8,128)S(1)} %collective-permute-done.3.south_east.north_east, f32[24,128]{1,0:T(8,128)S(1)} %collective-permute-done.3.south_east.north_east, f32[24,128]{1,0:T(8,128)S(1)} %collective-permute-done.4.south.north, f32[24,128]{1,0:T(8,128)S(1)} %collective-permute-done.4.south.north, ...), custom_call_target="tpu_custom_call" | custom-call | tf_op jit(solution)/shard_map/pallas_call | solution.py:536
  16.4 2.1 %shard_map.106 = (f32[75,2,128]{2,1,0:T(2,128)}, f32[75,2,128]{2,1,0:T(2,128)}, f32[75,2,128]{2,1,0:T(2,128)}, f32[75,2,128]{2,1,0:T(2,128)}) custom-call(f32[2,4,80,128]{3,2,1,0:T(8,128)S(1)} %get-tuple-element.12.own, f32[2,4,80,128]{3,2,1,0:T(8,128)S(1)} %collective-permute-done.east, f32[2,4,80,128]{3,2,1,0:T(8,128)S(1)} %collective-permute-done.1.west, ...), custom_call_target="tpu_custom_call" | custom-call | tf_op jit(solution)/shard_map/pallas_call | solution.py:545
Async XLA Ops:
  1.9 2.7 %collective-permute-start.2 = (f32[24,128]{1,0:T(8,128)S(1)}, f32[24,128]{1,0:T(8,128)S(1)}, u32[]{:S(2)}, u32[]{:S(2)}) collective-permute-start(f32[24,128]{1,0:T(8,128)S(1)} %get-tuple-element.15.own), channel_id=1, source_target_pairs={{0,2},{2,4},{4,6},{6,8},{8,10},{10,12},{12,14},{14,16},{16,18},{18... | collective-permute-start | bytes 36872 | tf_op jit(solution)/shard_map/ppermute | solution.py:504
  3.7 7.8 %collective-permute-start.1 = (f32[2,4,80,128]{3,2,1,0:T(8,128)S(1)}, f32[2,4,80,128]{3,2,1,0:T(8,128)S(1)}, u32[]{:S(2)}, u32[]{:S(2)}) collective-permute-start(f32[2,4,80,128]{3,2,1,0:T(8,128)S(1)} %get-tuple-element.12.own), channel_id=1, source_target_pairs={{0,2},{2,4},{4,6},{6,8},{8,10},{10,12},{12,14},{14,16},{16,18},{18... | collective-permute-start | bytes 983048 | tf_op jit(solution)/shard_map/ppermute | solution.py:505
  3.8 10.4 %collective-permute-start = (f32[2,4,80,128]{3,2,1,0:T(8,128)S(1)}, f32[2,4,80,128]{3,2,1,0:T(8,128)S(1)}, u32[]{:S(2)}, u32[]{:S(2)}) collective-permute-start(f32[2,4,80,128]{3,2,1,0:T(8,128)S(1)} %get-tuple-element.12.own), channel_id=1, source_target_pairs={{2,0},{4,2},{6,4},{8,6},{10,8},{12,10},{14,12},{16,14},{18,16},{20... | collective-permute-start | bytes 983048 | tf_op jit(solution)/shard_map/ppermute | solution.py:506
  4.8 10.1 %collective-permute-start.3 = (f32[24,128]{1,0:T(8,128)S(1)}, f32[24,128]{1,0:T(8,128)S(1)}, u32[]{:S(2)}, u32[]{:S(2)}) collective-permute-start(f32[24,128]{1,0:T(8,128)S(1)} %get-tuple-element.16), channel_id=1, source_target_pairs={{2,1},{3,0},{4,3},{5,2},{6,5},{7,4},{8,7},{9,6},{10,9},{11,8},{12,... | collective-permute-start | bytes 36872 | tf_op jit(solution)/shard_map/ppermute | solution.py:510
  8.5 6.4 %collective-permute-start.4 = (f32[24,128]{1,0:T(8,128)S(1)}, f32[24,128]{1,0:T(8,128)S(1)}, u32[]{:S(2)}, u32[]{:S(2)}) collective-permute-start(f32[24,128]{1,0:T(8,128)S(1)} %get-tuple-element.17), channel_id=1, source_target_pairs={{0,1},{1,0},{2,3},{3,2},{4,5},{5,4},{6,7},{7,6},{8,9},{9,8},{10,11... | collective-permute-start | bytes 36872 | tf_op jit(solution)/shard_map/ppermute | solution.py:510
  10.2 5.8 %collective-permute-start.5 = (f32[24,128]{1,0:T(8,128)S(1)}, f32[24,128]{1,0:T(8,128)S(1)}, u32[]{:S(2)}, u32[]{:S(2)}) collective-permute-start(f32[24,128]{1,0:T(8,128)S(1)} %get-tuple-element.18), channel_id=1, source_target_pairs={{1,31},{3,29},{5,27},{7,25},{9,23},{11,21},{13,19},{15,17},{17,15}... | collective-permute-start | bytes 36872 | tf_op jit(solution)/shard_map/ppermute | solution.py:515
